TPU v7x, 32 devices: a whole 2x2x4 slice. The times are simulated.
32 devices in a mesh: group: 2 (over y), tenant: 4 (over x, core), mp: 4 (over z).
Axes of the slice: x: 2, y: 2, z: 4, core: 2. Of those that a mesh axis runs over, the one named last changes fastest.
Arguments:
- tokens: bfloat16 [8192, 8192], P(('group', 'tenant'), 'mp'), parts along dimension 0, may hold values from -6 to 6
- kv_weight: bfloat16 [8192, 2, 1024], P(None, None, 'mp'), may hold values from -0.0625 to 0.0625
- delta_in: bfloat16 [48, 64, 8192], P(('group', 'tenant'), None, 'mp'), parts along dimension 0, may hold values from -0.0625 to 0.0625
- delta_out: bfloat16 [48, 64, 2, 1024], P(('group', 'tenant'), None, None, 'mp'), parts along dimension 0, may hold values from -0.75 to 0.75
- delta_scale: bfloat16 [48, 64], P(('group', 'tenant')), parts along dimension 0, may hold values from 0.29882812 to 3
- owner_map: int32 [48], P('group'), parts along dimension 0, may hold values from 0 to 23, as said below
- resp_tenant: int32 [16], P(('group', 'tenant')), parts along dimension 0, may hold values from 0 to 23, as said below
Outputs:
- keys_values: bfloat16 [8192, 2, 1024], P(('group', 'tenant'), None, 'mp'), parts along dimension 0
There are 2 independent parts, one for each index of `group`. A program takes and returns all parts, laid end to end along the dimension named above; an argument that names none is the same for every part. Nothing has to cross between parts.
Inputs may be any that keep to these rules, and one draw needn't show every extreme that they name: A permutation: tenant t's factors are in store row owner_map[t], which lies with owner owner_map[t] // 6. `resp_tenant`: exactly 4 distinct tenants are named over all responses; their store rows fall on at most 2 distinct rows of any one owner: a quarter of the owners hold 2 named tenants, a quarter none, the others one.
All inputs are finite; a program needn't handle non-finite values.
Results may differ from a plain program's by a relative error of at most 0.0044.
Values may be sent and summed in bfloat16 or wider, within the bound.
No kernel may reach another device: no remote copies, remote signals or barrier semaphores. Data moves between devices by JAX's collectives and lax.ppermute only.
A program may use at most 128 MiB of HBM per device.

v0:
```python
import jax
import jax.numpy as jnp
from jax import lax
from jax.sharding import PartitionSpec as P

CAPO = 2


def take_rows(chooser, pieces):
    first = jnp.einsum("rn,nkd->rkd", chooser, pieces[0], preferred_element_type=jnp.float32)
    second = jnp.einsum("rn,nkme->rkme", chooser, pieces[1], preferred_element_type=jnp.float32)
    third = jnp.dot(chooser, pieces[2], preferred_element_type=jnp.float32)
    return (first, second, third)


def shards(tokens, kv_weight, delta_in, delta_out, delta_scale, owner_map, resp_tenant):
    tok_dev = tokens.shape[0]
    d_shard = tokens.shape[1]
    resp_dev = resp_tenant.shape[0]
    resp_len = tok_dev // resp_dev
    ten_dev = delta_in.shape[0]
    head_cols = kv_weight.shape[2]
    n_owner = lax.axis_size("tenant")
    tenants = owner_map.shape[0]
    tenant_ids = jnp.arange(tenants, dtype=jnp.int32)
    my_slot = jnp.sum(
        jnp.where(resp_tenant[:, None] == tenant_ids[None, :], owner_map[None, :], 0), axis=1
    )
    requests = lax.all_gather(my_slot, "tenant", axis=0, tiled=True)
    layout = tenant_ids.reshape(n_owner, ten_dev)
    wanted = jnp.any(requests[None, None, :] == layout[:, :, None], axis=2)
    ranking = jnp.cumsum(wanted.astype(jnp.int32), axis=1) - 1
    positions = jnp.arange(CAPO, dtype=jnp.int32)
    packing = wanted[:, :, None] & (ranking[:, :, None] == positions[None, None, :])
    filled = jnp.any(packing, axis=1)
    packed_slot = jnp.sum(jnp.where(packing, layout[:, :, None], 0), axis=1)
    own_rows = lax.dynamic_index_in_dim(
        packing, lax.axis_index("tenant"), 0, keepdims=False
    ).astype(jnp.bfloat16)
    packed_in = jnp.einsum(
        "jc,jkd->ckd", own_rows, delta_in, preferred_element_type=jnp.float32
    ).astype(jnp.bfloat16)
    packed_out = jnp.einsum(
        "jc,jkme->ckme", own_rows, delta_out, preferred_element_type=jnp.float32
    ).astype(jnp.bfloat16)
    packed_scale = jnp.einsum(
        "jc,jk->ck", own_rows, delta_scale, preferred_element_type=jnp.float32
    ).astype(jnp.bfloat16)
    chooser = (
        (my_slot[:, None] == packed_slot.reshape(-1)[None, :]) & filled.reshape(-1)[None, :]
    ).astype(jnp.bfloat16)
    picked = take_rows(
        chooser,
        (
            lax.all_gather(packed_in, "tenant", axis=0, tiled=True),
            lax.all_gather(packed_out, "tenant", axis=0, tiled=True),
            lax.all_gather(packed_scale, "tenant", axis=0, tiled=True),
        ),
    )
    picked_in = picked[0].astype(jnp.bfloat16)
    picked_out = picked[1].astype(jnp.bfloat16)
    picked_scale = picked[2]
    blocks = tokens.reshape(resp_dev, resp_len, d_shard)
    partial_coeff = jnp.einsum(
        "rld,rkd->rlk", blocks, picked_in, preferred_element_type=jnp.float32
    )
    coeff = lax.psum(partial_coeff, "mp")
    lowrank = (coeff * picked_scale[:, None, :]).astype(jnp.bfloat16)
    delta = jnp.einsum(
        "rlk,rkme->rlme", lowrank, picked_out, preferred_element_type=jnp.float32
    ).reshape(tok_dev, 2, head_cols)
    flat_weight = kv_weight.reshape(kv_weight.shape[0], 2 * head_cols)
    base = jnp.dot(
        lax.all_gather(tokens, "mp", axis=1, tiled=True),
        flat_weight,
        preferred_element_type=jnp.float32,
    )
    return (base.reshape(tok_dev, 2, head_cols) + delta).astype(jnp.bfloat16)


def solution(mesh):
    return jax.shard_map(
        shards,
        mesh=mesh,
        in_specs=(
            P(("group", "tenant"), "mp"),
            P(None, None, "mp"),
            P(("group", "tenant"), None, "mp"),
            P(("group", "tenant"), None, None, "mp"),
            P(("group", "tenant"), None),
            P("group"),
            P(("group", "tenant")),
        ),
        out_specs=P(("group", "tenant"), None, "mp"),
        check_vma=False,
    )
```

profile of v0, /device:TPU:0, one launch (start us, length us, event | category | flops | bytes accessed | tf_op | source)
XLA Modules:
  0.0 397.4 jit_solution(3713200214790920392)
XLA Ops:
  6.5 0.0 copy-start
  6.5 0.0 all-gather.6.cloned.1.call-start
  6.5 1.4 dynamic-slice
  8.5 0.9 fusion.21
  9.4 0.2 dynamic-update-slice
  9.7 6.4 %all-reduce = s32[8]{0:T(128)S(1)} all-reduce(s32[8]{0:T(128)S(1)} %dynamic-update-slice), channel_id=1, replica_groups=mesh['group'=2,'tenant'=4,'mp'=4] {'tenant'}, use_global_device_ids=true, to_apply=%add | all-reduce | flops 8 | bytes 64
  16.0 0.1 copy.26
  16.1 0.3 compare_reduce_fusion
  16.4 0.1 copy.27
  16.5 0.1 copy.28
  16.6 0.2 select_reduce_fusion
  16.8 0.0 copy-done
  16.8 1.2 convolution_convert_fusion.1
  18.0 1.0 copy.30
  19.0 0.0 all-gather.6.cloned.1.call-update
  19.0 0.0 all-reduce.3.cloned.1.call-start
  19.0 0.1 reduce_or.19
  19.2 0.1 and.21
  19.3 0.1 eq.64
  19.4 0.1 compare_and_fusion.1
  19.4 22.9 %all-gather.6.cloned.1.call-done = bf16[8,64,2048]{2,1,0:T(8,128)(2,1)} async-done(((bf16[2,64,2048]{2,1,0:T(8,128)(2,1)}), bf16[8,64,2048]{2,1,0:T(8,128)(2,1)}) %all-gather.6.cloned.1.call-update) | async-done | bytes 2097168 | tf_op jit(solution)/shard_map/all_gather | solution.py:55
  42.3 3.2 convolution_convert_fusion
  45.5 4.3 %convolution_bitcast_fusion = f32[2,512,64]{1,2,0:T(8,128)} fusion(bf16[2,512,2048]{2,1,0:T(8,128)(2,1)} %bitcast.50, bf16[2,64,2048]{2,0,1:T(2,128)(2,1)S(1)} %convolution_convert_fusion), kind=kOutput, calls=%fused_computation.8 | convolution fusion | flops 268435456 | bytes 4980736 | tf_op jit(solution)/shard_map/rld,rkd->rlk/dot_general | solution.py:64
  49.9 0.0 all-reduce.3.cloned.1.call-update
  49.9 0.0 copy-start.1
  49.9 0.0 all-gather.4.cloned.1.call-start
  50.0 0.7 all-gather.4.cloned.1.call-update
  50.7 0.2 copy-done.1
  50.9 0.3 convolution_convert_fusion.3
  51.3 8.0 %copy.44 = bf16[1024,8,2,256]{3,1,2,0:T(8,128)(2,1)} copy(bf16[1024,8,2,256]{3,2,1,0:T(2,128)(2,1)} %bitcast.51) | data formatting | bytes 16777216
  59.3 0.0 copy-start.2
  59.3 11.3 %copy.25 = bf16[512,8192]{1,0:T(8,128)(2,1)} copy(bf16[512,8192]{0,1:T(8,128)(2,1)} %bitcast.49) | data formatting | bytes 16777216 | tf_op jit(solution)/shard_map/dot_general | solution.py:73
  70.6 0.0 copy-done.2
  70.6 0.1 fusion.7
  70.7 5.0 %all-gather = bf16[4,2,64]{2,1,0:T(2,128)(2,1)S(1)} all-gather(bf16[1,2,64]{2,1,0:T(2,128)(2,1)S(1)} %fusion.7), channel_id=1, replica_groups=mesh['group'=2,'tenant'=4,'mp'=4] {'tenant'}, dimensions={0}, use_global_device_ids=true | all-gather | bytes 1280 | tf_op jit(solution)/shard_map/all_gather | solution.py:57
  75.8 7.4 %all_gather.19 = bf16[8,64,2,256]{3,1,2,0:T(8,128)(2,1)S(1)} all-gather(bf16[2,64,2,256]{3,1,2,0:T(8,128)(2,1)S(1)} %copy.34), channel_id=1, replica_groups=mesh['group'=2,'tenant'=4,'mp'=4] {'tenant'}, dimensions={0}, use_global_device_ids=true | all-gather | bytes 655360 | tf_op jit(solution)/shard_map/all_gather | solution.py:56
  83.2 0.1 fusion.22
  83.3 0.4 convolution_convert_fusion.2
  83.7 1.7 all-reduce.3.cloned.1.call-done
  85.4 2.9 fusion.12
  88.3 285.3 %all-gather.4.cloned.1.call-done = bf16[1024,8192]{1,0:T(8,128)(2,1)} async-done(((bf16[1024,2048]{1,0:T(8,128)(2,1)}), bf16[1024,8192]{1,0:T(8,128)(2,1)}) %all-gather.4.cloned.1.call-update) | async-done | bytes 16777232 | tf_op jit(solution)/shard_map/all_gather | solution.py:74
  373.6 15.2 %fusion.2 = bf16[1024,2,256]{2,0,1:T(8,128)(2,1)S(1)} fusion(f32[2,512,2,256]{3,1,0,2:T(8,128)} %fusion.12, bf16[2,256,8192]{2,1,0:T(8,128)(2,1)} %bitcast.52, bf16[1024,8192]{1,0:T(8,128)(2,1)} %all-gather.4.cloned.1.call-done), kind=kOutput, calls=%fused_computation.5 | convolution fusion | flops 8590983168 | bytes 28311552 | tf_op jit(solution)/shard_map/dot_general | solution.py:73
  388.8 2.0 copy.38
  (6 shorter events, 0.1 us)
Async XLA Ops:
  6.5 10.2 %copy-start = (bf16[6,64,2048]{2,1,0:T(8,128)(2,1)S(1)}, bf16[6,64,2048]{2,1,0:T(8,128)(2,1)}, u32[]{:S(2)}) copy-start(bf16[6,64,2048]{2,1,0:T(8,128)(2,1)} %param.9) | copy-start | bytes 4718596
  6.5 35.8 %all-gather.6.cloned.1.call-start = ((), (), s32[]{:S(2)}) async-start(), calls=%async_computation.1 | async-start | bytes 2621440 | tf_op jit(solution)/shard_map/all_gather | solution.py:55
  19.0 66.4 %all-reduce.3.cloned.1.call-start = ((), (), s32[]{:S(2)}) async-start(), calls=%async_computation.2 | async-start | bytes 524288 | tf_op jit(solution)/shard_map/psum | solution.py:67
  49.9 1.0 copy-start.1
  49.9 323.7 %all-gather.4.cloned.1.call-start = ((), (), s32[]{:S(2)}) async-start(), calls=%async_computation | async-start | bytes 20971520 | tf_op jit(solution)/shard_map/all_gather | solution.py:74
  59.3 11.3 %copy-start.2 = (bf16[6,64]{1,0:T(8,128)(2,1)S(1)}, bf16[6,64]{1,0:T(8,128)(2,1)}, u32[]{:S(2)}) copy-start(bf16[6,64]{1,0:T(8,128)(2,1)} %param.11) | copy-start | bytes 2308
Sparse Core Ops, SparseCore 0:
  19.1 23.1 all-gather.5
  50.0 35.3 all-reduce.2
  87.1 286.5 all-gather.3
where the time goes:
time: 398 us; the launch traced here: 397 us
  waiting for transfers between devices  311 us (78%)
  matrix products  27.8 us (7%)
  local copies, waits for them, and re-layouts  24.7 us (6%)
  blocking collectives  18.8 us (5%)
  between operations  13.8 us (3%)
    all_gather x1, waiting for transfers between devices, shards(): lax.all_gather(tokens, 'mp', axis=1, tiled=True)  285 us
    all_gather x1, waiting for transfers between devices, shards(): lax.all_gather(packed_in, 'tenant', axis=0, tiled=True)  22.9 us
    dot_general x1, matrix products, shards(): jnp.dot(lax.all_gather(tokens, 'mp', axis=1, tiled=True), flat_weight, pr...  15.2 us
    dot_general x1, local copies, waits for them, and re-layouts, shards(): jnp.dot(lax.all_gather(tokens, 'mp', axis=1, tiled=True), flat_weight, pr...  11.3 us
    unnamed x10, local copies, waits for them, and re-layouts  9.86 us
  transfers between devices with their start and end apart: 3, of which 3 were waited for; matrix products, arithmetic and copies ran while one was open for 6% of the time, Pallas kernels for 0%

commit v1 on v0

v1 whole, which is shorter than its diff:
```python
import jax
import jax.numpy as jnp
from jax import lax
from jax.sharding import PartitionSpec as P

CAPO = 2
F32 = jnp.float32
BF16 = jnp.bfloat16


def swap(value, axis, size, mask):
    return lax.ppermute(value, axis, [(i, i ^ mask) for i in range(size)])


def hop(value, n, at):
    return lax.ppermute(value, "mp", [(at, at + 1), (n - 1 - at, n - 2 - at)])


def shards(tokens, kv_weight, delta_in, delta_out, delta_scale, owner_map, resp_tenant):
    tok_dev, d_shard = tokens.shape
    resp_dev = resp_tenant.shape[0]
    resp_len = tok_dev // resp_dev
    ten_dev, rank = delta_in.shape[0], delta_in.shape[1]
    head_cols = kv_weight.shape[2]
    cols = 2 * head_cols
    n_group = lax.axis_size("group")
    n_owner = lax.axis_size("tenant")
    n = lax.axis_size("mp")
    plane = n_group * n_owner
    share_rows = d_shard // plane
    tenants = owner_map.shape[0]
    me_mp = lax.axis_index("mp")
    me_owner = lax.axis_index("tenant")
    me_share = lax.axis_index("group") * n_owner + me_owner
    hop_type = BF16 if n <= 4 else F32

    def weight_pieces(k):
        row = (me_mp ^ k) * d_shard + me_share * share_rows
        part = lax.dynamic_slice_in_dim(kv_weight, row, share_rows, 0).reshape(share_rows, cols)
        arrived = swap(part, "mp", n, k)
        pieces = [arrived] + [
            swap(arrived, ("group", "tenant"), plane, mask) for mask in range(2, plane, 2)
        ]
        mine = jnp.concatenate(pieces, axis=0)
        other = swap(mine, "tenant", n_owner, 1)
        return mine, other

    blocks_of = tokens.reshape(tok_dev, plane, share_rows)
    order = [m for m in range(0, plane, 2)] + [m ^ 1 for m in range(0, plane, 2)]
    ordered = jnp.concatenate(
        [lax.dynamic_index_in_dim(blocks_of, me_share ^ m, 1, keepdims=False) for m in order], axis=1
    )

    def partial_of(k):
        mine, other = weight_pieces(k)
        return jnp.dot(ordered, jnp.concatenate([mine, other], axis=0), preferred_element_type=F32)

    tenant_ids = jnp.arange(tenants, dtype=jnp.int32)
    my_slot = jnp.sum(
        jnp.where(resp_tenant[:, None] == tenant_ids[None, :], owner_map[None, :], 0), axis=1
    )
    requests = jnp.concatenate(
        [my_slot] + [swap(my_slot, "tenant", n_owner, m) for m in range(1, n_owner)]
    )
    stored = me_owner * ten_dev + jnp.arange(ten_dev, dtype=jnp.int32)
    wanted = jnp.any(requests[None, :] == stored[:, None], axis=1)
    ranking = jnp.cumsum(wanted.astype(jnp.int32)) - 1
    rows, names = [], []
    for c in range(CAPO):
        hit = wanted & (ranking == c)
        at = jnp.sum(jnp.where(hit, jnp.arange(ten_dev, dtype=jnp.int32), 0))
        rows.append(at)
        names.append(jnp.where(jnp.any(hit), me_owner * ten_dev + at, -1))
    name = jnp.stack(names)

    def pack(store):
        return jnp.stack([lax.dynamic_index_in_dim(store, at, 0, keepdims=False) for at in rows])

    def spread(packed):
        mine = jnp.concatenate(
            [packed] + [swap(packed, "tenant", n_owner, m) for m in range(2, n_owner, 2)], axis=0
        )
        return jnp.concatenate([mine, swap(mine, "tenant", n_owner, 1)], axis=0)

    all_names = spread(name)
    all_in = spread(pack(delta_in))
    all_out = spread(pack(delta_out).reshape(CAPO, rank, cols))
    all_scale = spread(pack(delta_scale))
    picked = [jnp.argmax(all_names == my_slot[r]).astype(jnp.int32) for r in range(resp_dev)]

    def choose(store):
        return jnp.stack([lax.dynamic_index_in_dim(store, at, 0, keepdims=False) for at in picked])

    part_coeff = jnp.einsum(
        "rld,rkd->rlk",
        tokens.reshape(resp_dev, resp_len, d_shard),
        choose(all_in),
        preferred_element_type=F32,
    )
    coeff, came = part_coeff, None
    for h in range(n - 1):
        came = hop(part_coeff if came is None else part_coeff + came, n, h)
        coeff = coeff + came
    lowrank = (coeff * choose(all_scale).astype(F32)[:, None, :]).astype(BF16)
    delta = jnp.einsum(
        "rlk,rkc->rlc", lowrank, choose(all_out), preferred_element_type=F32
    ).reshape(tok_dev, cols)

    own = lax.dynamic_slice_in_dim(kv_weight, me_mp * d_shard, d_shard, 0).reshape(d_shard, cols)
    parts = {k: partial_of(k) for k in range(n - 1, 0, -1)}
    came = []
    for s in range(1, n):
        now = []
        for h in range(s):
            load = parts[h ^ (h + n - s)]
            if h:
                load = load + came[h - 1].astype(F32)
            now.append(hop(load.astype(hop_type), n, h))
        came = now
    total = jnp.dot(tokens, own, preferred_element_type=F32) + delta
    for value in came:
        total = total + value.astype(F32)
    return total.astype(BF16).reshape(tok_dev, 2, head_cols)


def solution(mesh):
    return jax.shard_map(
        shards,
        mesh=mesh,
        in_specs=(
            P(("group", "tenant"), "mp"),
            P(None, None, "mp"),
            P(("group", "tenant"), None, "mp"),
            P(("group", "tenant"), None, None, "mp"),
            P(("group", "tenant"), None),
            P("group"),
            P(("group", "tenant")),
        ),
        out_specs=P(("group", "tenant"), None, "mp"),
        check_vma=False,
    )
```

time: 398 us -> 227 us (0.57)
  waiting for transfers between devices: 311 us -> 63.1 us
  starting transfers between devices: 0.09 us -> 66.8 us
  local copies, waits for them, and re-layouts: 24.7 us -> 48.5 us
  blocking collectives: 18.8 us -> 0 us
  other arithmetic: 1.52 us -> 17.8 us
  matrix products: 27.8 us -> 19.1 us
    all_gather x2 -> x0, waiting for transfers between devices: 308 us -> none  [the longest x1 285 us: shards(): lax.all_gather(tokens, 'mp', axis=1, tiled=True)]
    ppermute x0 -> x35, starting transfers between devices: none -> 66.8 us  [the longest x9 42 us: hop(): return lax.ppermute(value, 'mp', [(at, at + 1), (n - 1 - at, n - 2 - at)])]
    ppermute x0 -> x35, waiting for transfers between devices: none -> 63.1 us  [the longest x9 44.1 us: hop(): return lax.ppermute(value, 'mp', [(at, at + 1), (n - 1 - at, n - 2 - at)])]
    dynamic_slice x0 -> x17, local copies, waits for them, and re-layouts: none -> 16.2 us  [the longest x9 9.17 us: shards(): lax.dynamic_index_in_dim(blocks_of, me_share ^ m, 1, keepdims=False)]
    unnamed x10 -> x58, local copies, waits for them, and re-layouts: 9.86 us -> 25.3 us
    all_gather x2 -> x0, blocking collectives: 12.4 us -> none  [the longest x1 7.41 us: shards(): lax.all_gather(packed_out, 'tenant', axis=0, tiled=True)]
    dot_general x1 -> x0, local copies, waits for them, and re-layouts: 11.3 us -> none  [shards(): jnp.dot(lax.all_gather(tokens, 'mp', axis=1, tiled=True), flat_weight, pr...]
    dot_general x9 -> x6, matrix products: 27.8 us -> 19.1 us  [the longest x3 13.4 us: partial_of(): jnp.dot(ordered, jnp.concatenate([mine, other], axis=0), preferred_elemen...]
  transfers between devices with their start and end apart: 3 -> 35, of which waited for: 3 -> 10; matrix products, arithmetic and copies ran while one was open for 6% -> 32% of each run, Pallas kernels for 0% -> 0%
where the time goes in v1:
time: 227 us; the launch traced here: 226 us
  starting transfers between devices  66.8 us (29%)
  waiting for transfers between devices  63.1 us (28%)
  local copies, waits for them, and re-layouts  48.5 us (21%)
  matrix products  19.1 us (8%)
  other arithmetic  17.8 us (8%)
  between operations  10.6 us (5%)
    ppermute x9, waiting for transfers between devices, hop(): return lax.ppermute(value, 'mp', [(at, at + 1), (n - 1 - at, n - 2 - at)])  44.1 us
    ppermute x9, starting transfers between devices, hop(): return lax.ppermute(value, 'mp', [(at, at + 1), (n - 1 - at, n - 2 - at)])  42 us
    unnamed x58, local copies, waits for them, and re-layouts  25.3 us
    ppermute x26, starting transfers between devices, swap(): return lax.ppermute(value, axis, [(i, i ^ mask) for i in range(size)])  24.8 us
    ppermute x26, waiting for transfers between devices, swap(): return lax.ppermute(value, axis, [(i, i ^ mask) for i in range(size)])  19 us
    dot_general x3, matrix products, partial_of(): jnp.dot(ordered, jnp.concatenate([mine, other], axis=0), preferred_elemen...  13.4 us
    dynamic_slice x9, local copies, waits for them, and re-layouts, shards(): lax.dynamic_index_in_dim(blocks_of, me_share ^ m, 1, keepdims=False)  9.17 us
    concatenate x3, other arithmetic, weight_pieces(): mine = jnp.concatenate(pieces, axis=0)  4.66 us
  transfers between devices with their start and end apart: 35, of which 10 were waited for; matrix products, arithmetic and copies ran while one was open for 32% of the time, Pallas kernels for 0%

profile of v1, /device:TPU:0, one launch (start us, length us, event | category | flops | bytes accessed | tf_op | source)
XLA Modules:
  0.0 225.9 jit_solution(9680104908267320044)
XLA Ops:
  1.4 2.6 %collective-permute-start.1 = (s32[2]{0:T(128)S(1)}, s32[2]{0:T(128)S(1)}, u32[]{:S(2)}, u32[]{:S(2)}) collective-permute-start(s32[2]{0:T(128)S(1)} %fusion.12), channel_id=1, source_target_pairs={{0,8},{4,12},{8,0},{12,4},{1,9},{5,13},{9,1},{13,5},{2,10},{6,14},... | collective-permute-start | bytes 32 | tf_op jit(solution)/shard_map/ppermute | solution.py:12
  4.0 1.6 constant_dynamic-slice_fusion.1
  6.4 2.8 %collective-permute-start.25 = (bf16[256,512]{1,0:T(8,128)(2,1)}, bf16[256,512]{1,0:T(8,128)(2,1)}, u32[]{:S(2)}, u32[]{:S(2)}) collective-permute-start(bf16[256,512]{1,0:T(8,128)(2,1)} %bitcast.28), channel_id=1, source_target_pairs={{0,2},{1,3},{2,0},{3,1},{4,6},{5,7},{6,4},{7,5},{8,10},{9,11},{10,... | collective-permute-start | bytes 786440 | tf_op jit(solution)/shard_map/ppermute | solution.py:12
  9.9 1.3 collective-permute-start.20
  11.8 6.4 %copy.42 = bf16[1024,2048]{0,1:T(8,128)(2,1)} copy(bf16[1024,2048]{1,0:T(8,128)(2,1)} %param.7) | data formatting | bytes 8388608 | tf_op args[0]
  18.2 3.6 %constant_dynamic-slice_fusion.3 = (bf16[1024,1,256]{0,2,1:T(8,128)(2,1)}, bf16[1024,1,256]{0,2,1:T(8,128)(2,1)S(1)}, bf16[1024,1,256]{0,2,1:T(8,128)(2,1)S(1)},...) fusion(bf16[1024,8,256]{0,2,1:T(8,128)(2,1)} %bitcast.68, ...), kind=kLoop, calls=%fused_computation.55 | loop fusion | bytes 8388640 | tf_op jit(solution)/shard_map/jit(dynamic_index_in_dim)/dynamic_slice | solution.py:51
  21.9 1.2 copy.43
  24.0 1.2 copy.44
  25.2 1.0 copy.45
  27.0 1.2 copy.50
  29.0 3.2 %constant_dynamic-slice_fusion.23 = bf16[2048,2,256]{2,1,0:T(2,128)(2,1)S(1)} fusion(bf16[8192,2,256]{2,1,0:T(2,128)(2,1)} %param.8, s32[]{:T(128)S(6)} %select_n.87), kind=kLoop, calls=%fused_computation.75 | loop fusion | bytes 4194308 | tf_op jit(solution)/shard_map/dynamic_slice | solution.py:109
  32.8 1.6 copy-done
  34.5 3.7 %fusion.20 = f32[512,1024]{1,0:T(8,128)} fusion(bf16[2048,512]{1,0:T(8,128)(2,1)S(1)} %bitcast.72, bf16[1024,2048]{1,0:T(8,128)(2,1)S(1)} %copy-done), kind=kOutput, calls=%fused_computation.102 | convolution fusion | flops 2147483648 | bytes 8388608 | tf_op jit(solution)/shard_map/dot_general | solution.py:120
  38.8 1.9 copy-done.12
  49.3 1.0 constant_dynamic-slice_fusion.14
  51.2 1.4 collective-permute-start.26
  52.6 1.5 collective-permute-start.27
  54.7 1.1 constant_dynamic-slice_fusion.22
  55.8 4.8 %collective-permute-done.26 = bf16[256,512]{1,0:T(8,128)(2,1)S(1)} collective-permute-done((bf16[256,512]{1,0:T(8,128)(2,1)}, bf16[256,512]{1,0:T(8,128)(2,1)S(1)}, u32[]{:S(2)}, u32[]{:S(2)}) %collective-permute-start.26) | collective-permute-done | bytes 262176 | tf_op jit(solution)/shard_map/ppermute | solution.py:12
  60.6 5.6 %collective-permute-done.27 = bf16[256,512]{1,0:T(8,128)(2,1)S(1)} collective-permute-done((bf16[256,512]{1,0:T(8,128)(2,1)}, bf16[256,512]{1,0:T(8,128)(2,1)S(1)}, u32[]{:S(2)}, u32[]{:S(2)}) %collective-permute-start.27) | collective-permute-done | bytes 262176 | tf_op jit(solution)/shard_map/ppermute | solution.py:12
  66.9 1.0 pad_maximum_fusion.4
  68.9 1.2 collective-permute-start.21
  70.9 1.4 collective-permute-start.23
  72.4 1.0 reshape.84
  74.1 1.0 constant_dynamic-update-slice_fusion.17
  75.1 3.1 %collective-permute-done.21 = bf16[256,512]{1,0:T(8,128)(2,1)S(1)} collective-permute-done((bf16[256,512]{1,0:T(8,128)(2,1)}, bf16[256,512]{1,0:T(8,128)(2,1)S(1)}, u32[]{:S(2)}, u32[]{:S(2)}) %collective-permute-start.21) | collective-permute-done | bytes 262176 | tf_op jit(solution)/shard_map/ppermute | solution.py:12
  78.2 1.2 collective-permute-start.5
  79.4 3.2 %collective-permute-done.22 = bf16[256,512]{1,0:T(8,128)(2,1)} collective-permute-done((bf16[256,512]{1,0:T(8,128)(2,1)}, bf16[256,512]{1,0:T(8,128)(2,1)}, u32[]{:S(2)}, u32[]{:S(2)}) %collective-permute-start.22) | collective-permute-done | bytes 262176 | tf_op jit(solution)/shard_map/ppermute | solution.py:12
  82.5 2.5 %collective-permute-start.3 = (bf16[2,64,2048]{2,1,0:T(8,128)(2,1)}, bf16[2,64,2048]{2,1,0:T(8,128)(2,1)S(1)}, u32[]{:S(2)}, u32[]{:S(2)}) collective-permute-start(bf16[2,64,2048]{2,1,0:T(8,128)(2,1)} %pad_maximum_fusion.5), channel_id=1, source_target_pairs={{0,8},{4,12},{8,0},{12,4},{1,9},{5,13},{9,1},{13,5},{2,10},{6,14},... | collective-permute-start | bytes 1572872 | tf_op jit(solution)/shard_map/ppermute | solution.py:12
  85.1 2.5 %pad_maximum_fusion.3 = bf16[1024,512]{1,0:T(8,128)(2,1)} fusion(bf16[256,512]{1,0:T(8,128)(2,1)} %collective-permute-done.23, bf16[256,512]{1,0:T(8,128)(2,1)} %collective-permute-done.22, bf16[256,512]{1,0:T(8,128)(2,1)} %copy-done.3, bf16[256,512]{1,0:T(8,128)(2,1)} %collective-permute-done.20), kind=kLoop, calls=%fused_computation.12 | loop fusion | flops 4194304 | bytes 2097152 | tf_op jit(solution)/shard_map/concatenate | solution.py:44
  88.0 3.4 %fusion.19 = (bf16[1024,512]{0,1:T(8,128)(2,1)}, f32[1024,512]{0,1:T(8,128)S(1)}) fusion(bf16[1024,2048]{1,0:T(8,128)(2,1)S(1)} %copy-done.13, bf16[2048,512]{1,0:T(8,128)(2,1)S(1)} %constant_dynamic-update-slice_fusion.13), kind=kOutput, calls=%fused_computation.101 | convolution fusion | flops 2148007936 | bytes 9437184 | tf_op jit(solution)/shard_map/dot_general | solution.py:56
  91.4 4.5 %collective-permute-start.30 = (bf16[1024,512]{0,1:T(8,128)(2,1)}, bf16[1024,512]{0,1:T(8,128)(2,1)}, u32[]{:S(2)}, u32[]{:S(2)}) collective-permute-start(bf16[1024,512]{0,1:T(8,128)(2,1)} %get-tuple-element.42), channel_id=1, source_target_pairs={{0,1},{3,2},{4,5},{7,6},{8,9},{11,10},{12,13},{15,14},{16,17},{19,... | collective-permute-start | bytes 3145736 | tf_op jit(solution)/shard_map/ppermute | solution.py:16
  95.9 1.1 collective-permute-done.6
  97.1 1.2 compare_reduce_fusion.2
  99.9 1.7 collective-permute-start.16
  102.6 1.0 constant_dynamic-update-slice_fusion.11
  103.6 1.0 constant_dynamic-update-slice_fusion.10
  104.6 1.0 constant_dynamic-update-slice_fusion.9
  105.5 1.4 collective-permute-start.17
  107.0 1.3 constant_dynamic-update-slice_fusion.8
  108.3 9.7 %collective-permute-done.30 = bf16[1024,512]{0,1:T(8,128)(2,1)} collective-permute-done((bf16[1024,512]{0,1:T(8,128)(2,1)}, bf16[1024,512]{0,1:T(8,128)(2,1)}, u32[]{:S(2)}, u32[]{:S(2)}) %collective-permute-start.30) | collective-permute-done | bytes 1048608 | tf_op jit(solution)/shard_map/ppermute | solution.py:16
  118.0 6.2 %add_convert_fusion.2 = (bf16[1024,512]{0,1:T(8,128)(2,1)}, bf16[1024,512]{0,1:T(8,128)(2,1)}) fusion(bf16[1024,512]{0,1:T(8,128)(2,1)} %collective-permute-done.30, bf16[1024,2048]{1,0:T(8,128)(2,1)} %copy-done.12, bf16[2048,512]{1,0:T(8,128)(2,1)S(1)} %constant_dynamic-update-slice_fusion.8), kind=kOutput, calls=%fused_computation.8 | convolution fusion | flops 2149580800 | bytes 9437184 | tf_op jit(solution)/shard_map/dot_general | solution.py:56
  124.2 5.4 %collective-permute-start.32 = (bf16[1024,512]{0,1:T(8,128)(2,1)}, bf16[1024,512]{0,1:T(8,128)(2,1)}, u32[]{:S(2)}, u32[]{:S(2)}) collective-permute-start(bf16[1024,512]{0,1:T(8,128)(2,1)} %get-tuple-element.27), channel_id=1, source_target_pairs={{0,1},{3,2},{4,5},{7,6},{8,9},{11,10},{12,13},{15,14},{16,17},{19,... | collective-permute-start | bytes 3145736 | tf_op jit(solution)/shard_map/ppermute | solution.py:16
  129.6 1.3 compare_reduce_fusion.1
  133.7 1.7 collective-permute-start.10
  135.4 1.2 pad_maximum_fusion.2
  137.3 1.1 collective-permute-done.10
  138.5 1.0 constant_dynamic-update-slice_fusion.6
  139.5 1.0 constant_dynamic-update-slice_fusion.5
  140.4 10.5 %collective-permute-done.32 = bf16[1024,512]{0,1:T(8,128)(2,1)} collective-permute-done((bf16[1024,512]{0,1:T(8,128)(2,1)}, bf16[1024,512]{0,1:T(8,128)(2,1)}, u32[]{:S(2)}, u32[]{:S(2)}) %collective-permute-start.32) | collective-permute-done | bytes 1048608 | tf_op jit(solution)/shard_map/ppermute | solution.py:16
  150.9 1.6 add_convert_fusion.1
  153.2 1.0 constant_dynamic-update-slice_fusion.4
  154.6 1.9 copy-done.1
  156.5 1.4 convolution_bitcast_fusion
  157.9 7.2 %collective-permute-start.7 = (f32[2,512,64]{1,2,0:T(8,128)S(1)}, f32[2,512,64]{1,2,0:T(8,128)S(1)}, u32[]{:S(2)}, u32[]{:S(2)}) collective-permute-start(f32[2,512,64]{1,2,0:T(8,128)S(1)} %convolution_bitcast_fusion), channel_id=1, source_target_pairs={{0,1},{3,2},{4,5},{7,6},{8,9},{11,10},{12,13},{15,14},{16,17},{19,... | collective-permute-start | bytes 786440 | tf_op jit(solution)/shard_map/ppermute | solution.py:16
  165.0 1.6 collective-permute-start.31
  166.7 3.8 %fusion.17 = (bf16[1024,512]{0,1:T(8,128)(2,1)}, bf16[1024,512]{0,1:T(8,128)(2,1)}) fusion(bf16[1024,512]{0,1:T(8,128)(2,1)S(1)} %collective-permute-done.33, bf16[1024,2048]{1,0:T(8,128)(2,1)S(1)} %copy-done.14, bf16[2048,512]{1,0:T(8,128)(2,1)S(1)} %constant_dynamic-update-slice_fusion.3), kind=kOutput, calls=%fused_computation.99 | convolution fusion | flops 2149580800 | bytes 9437184 | tf_op jit(solution)/shard_map/dot_general | solution.py:56
  170.5 19.3 %collective-permute-start.19 = (bf16[1024,512]{0,1:T(8,128)(2,1)}, bf16[1024,512]{0,1:T(8,128)(2,1)}, u32[]{:S(2)}, u32[]{:S(2)}) collective-permute-start(bf16[1024,512]{0,1:T(8,128)(2,1)} %get-tuple-element.24), channel_id=1, source_target_pairs={{0,1},{3,2},{4,5},{7,6},{8,9},{11,10},{12,13},{15,14},{16,17},{19,... | collective-permute-start | bytes 3145736 | tf_op jit(solution)/shard_map/ppermute | solution.py:16
  189.8 1.3 collective-permute-start.34
  192.1 1.3 collective-permute-start.9
  193.5 23.9 %collective-permute-done.9 = f32[2,512,64]{1,2,0:T(8,128)S(1)} collective-permute-done((f32[2,512,64]{1,2,0:T(8,128)S(1)}, f32[2,512,64]{1,2,0:T(8,128)S(1)}, u32[]{:S(2)}, u32[]{:S(2)}) %collective-permute-start.9) | collective-permute-done | bytes 262176 | tf_op jit(solution)/shard_map/ppermute | solution.py:16
  218.1 1.8 copy.61
  219.9 4.0 %fusion.3 = bf16[1024,512]{0,1:T(8,128)(2,1)S(1)} fusion(f32[1024,512]{0,1:T(8,128)} %copy.61, f32[512,1024]{1,0:T(8,128)} %fusion.20, bf16[1024,512]{0,1:T(8,128)(2,1)} %collective-permute-done.34, bf16[1024,512]{0,1:T(8,128)(2,1)} %collective-permute-done.31, bf16[1024,512]{0,1:T(8,128)(2,1)} %collective-permute-done.19), kind=kLoop, calls=%fused_computation.5 | loop fusion | flops 4194304 | bytes 8388608 | tf_op jit(solution)/shard_map/convert_element_type | solution.py:123
  223.9 2.0 copy.57
  (125 shorter events, 19.6 us)
Async XLA Ops:
  0.9 37.9 %collective-permute-start = (s32[2]{0:T(128)S(1)}, s32[2]{0:T(128)S(1)}, u32[]{:S(2)}, u32[]{:S(2)}) collective-permute-start(s32[2]{0:T(128)S(1)} %fusion.12), channel_id=1, source_target_pairs={{0,4},{4,0},{8,12},{12,8},{1,5},{5,1},{9,13},{13,9},{2,6},{6,2},{1... | collective-permute-start | bytes 32 | tf_op jit(solution)/shard_map/ppermute | solution.py:12
  1.4 39.6 %collective-permute-start.1 = (s32[2]{0:T(128)S(1)}, s32[2]{0:T(128)S(1)}, u32[]{:S(2)}, u32[]{:S(2)}) collective-permute-start(s32[2]{0:T(128)S(1)} %fusion.12), channel_id=1, source_target_pairs={{0,8},{4,12},{8,0},{12,4},{1,9},{5,13},{9,1},{13,5},{2,10},{6,14},... | collective-permute-start | bytes 32 | tf_op jit(solution)/shard_map/ppermute | solution.py:12
  3.9 37.0 %collective-permute-start.2 = (s32[2]{0:T(128)S(1)}, s32[2]{0:T(128)S(1)}, u32[]{:S(2)}, u32[]{:S(2)}) collective-permute-start(s32[2]{0:T(128)S(1)} %fusion.12), channel_id=1, source_target_pairs={{0,12},{4,8},{8,4},{12,0},{1,13},{5,9},{9,5},{13,1},{2,14},{6,10},... | collective-permute-start | bytes 32 | tf_op jit(solution)/shard_map/ppermute | solution.py:12
  6.4 44.8 %collective-permute-start.25 = (bf16[256,512]{1,0:T(8,128)(2,1)}, bf16[256,512]{1,0:T(8,128)(2,1)}, u32[]{:S(2)}, u32[]{:S(2)}) collective-permute-start(bf16[256,512]{1,0:T(8,128)(2,1)} %bitcast.28), channel_id=1, source_target_pairs={{0,2},{1,3},{2,0},{3,1},{4,6},{5,7},{6,4},{7,5},{8,10},{9,11},{10,... | collective-permute-start | bytes 786440 | tf_op jit(solution)/shard_map/ppermute | solution.py:12
  9.9 58.9 %collective-permute-start.20 = (bf16[256,512]{1,0:T(8,128)(2,1)}, bf16[256,512]{1,0:T(8,128)(2,1)}, u32[]{:S(2)}, u32[]{:S(2)}) collective-permute-start(bf16[256,512]{1,0:T(8,128)(2,1)} %bitcast.26), channel_id=1, source_target_pairs={{0,3},{1,2},{2,1},{3,0},{4,7},{5,6},{6,5},{7,4},{8,11},{9,10},{10,... | collective-permute-start | bytes 786440 | tf_op jit(solution)/shard_map/ppermute | solution.py:12
  32.3 2.2 copy-start
  34.5 3.7 %copy-start.11 = (bf16[1024,2048]{1,0:T(8,128)(2,1)S(1)}, bf16[1024,2048]{1,0:T(8,128)(2,1)}, u32[]{:S(2)}) copy-start(bf16[1024,2048]{1,0:T(8,128)(2,1)} %bitcast_dynamic-update-slice_fusion.7) | copy-start | bytes 12582916
  34.5 3.8 %copy-start.2 = (bf16[1024,1,256]{2,0,1:T(8,128)(2,1)S(1)}, bf16[1024,1,256]{2,0,1:T(8,128)(2,1)}, u32[]{:S(2)}) copy-start(bf16[1024,1,256]{2,0,1:T(8,128)(2,1)} %copy.45) | copy-start | bytes 1572868
  38.4 8.2 %copy-start.15 = (bf16[6,64]{1,0:T(8,128)(2,1)S(1)}, bf16[6,64]{1,0:T(8,128)(2,1)}, u32[]{:S(2)}) copy-start(bf16[6,64]{1,0:T(8,128)(2,1)} %param.11) | copy-start | bytes 2308
  38.7 1.9 copy-start.12
  40.7 58.8 %collective-permute-start.14 = (bf16[256,512]{1,0:T(8,128)(2,1)}, bf16[256,512]{1,0:T(8,128)(2,1)S(1)}, u32[]{:S(2)}, u32[]{:S(2)}) collective-permute-start(bf16[256,512]{1,0:T(8,128)(2,1)} %bitcast.24), channel_id=1, source_target_pairs={{0,1},{1,0},{2,3},{3,2},{4,5},{5,4},{6,7},{7,6},{8,9},{9,8},{10,11... | collective-permute-start | bytes 786440 | tf_op jit(solution)/shard_map/ppermute | solution.py:12
  51.2 9.4 %collective-permute-start.26 = (bf16[256,512]{1,0:T(8,128)(2,1)}, bf16[256,512]{1,0:T(8,128)(2,1)S(1)}, u32[]{:S(2)}, u32[]{:S(2)}) collective-permute-start(bf16[256,512]{1,0:T(8,128)(2,1)} %collective-permute-done.25), channel_id=1, source_target_pairs={{0,8},{4,12},{8,0},{12,4},{16,24},{20,28},{24,16},{28,20},{1,9},{5... | collective-permute-start | bytes 786440 | tf_op jit(solution)/shard_map/ppermute | solution.py:12
  52.6 13.5 %collective-permute-start.27 = (bf16[256,512]{1,0:T(8,128)(2,1)}, bf16[256,512]{1,0:T(8,128)(2,1)S(1)}, u32[]{:S(2)}, u32[]{:S(2)}) collective-permute-start(bf16[256,512]{1,0:T(8,128)(2,1)} %collective-permute-done.25), channel_id=1, source_target_pairs={{0,16},{4,20},{8,24},{12,28},{16,0},{20,4},{24,8},{28,12},{1,17},{... | collective-permute-start | bytes 786440 | tf_op jit(solution)/shard_map/ppermute | solution.py:12
  54.1 12.0 %collective-permute-start.28 = (bf16[256,512]{1,0:T(8,128)(2,1)}, bf16[256,512]{1,0:T(8,128)(2,1)S(1)}, u32[]{:S(2)}, u32[]{:S(2)}) collective-permute-start(bf16[256,512]{1,0:T(8,128)(2,1)} %collective-permute-done.25), channel_id=1, source_target_pairs={{0,24},{4,28},{8,16},{12,20},{16,8},{20,12},{24,0},{28,4},{1,25},{... | collective-permute-start | bytes 786440 | tf_op jit(solution)/shard_map/ppermute | solution.py:12
  60.6 8.3 %copy-start.4 = (bf16[256,512]{1,0:T(8,128)(2,1)}, bf16[256,512]{1,0:T(8,128)(2,1)S(1)}, u32[]{:S(2)}) copy-start(bf16[256,512]{1,0:T(8,128)(2,1)S(1)} %collective-permute-done.26) | copy-start | bytes 786436
  66.1 8.9 %copy-start.6 = (bf16[256,512]{1,0:T(8,128)(2,1)}, bf16[256,512]{1,0:T(8,128)(2,1)S(1)}, u32[]{:S(2)}) copy-start(bf16[256,512]{1,0:T(8,128)(2,1)S(1)} %collective-permute-done.27) | copy-start | bytes 786436
  66.1 0.7 copy-start.8
  67.9 19.7 %collective-permute-start.29 = (bf16[1024,512]{1,0:T(8,128)(2,1)S(1)}, bf16[1024,512]{1,0:T(8,128)(2,1)S(1)}, u32[]{:S(2)}, u32[]{:S(2)}) collective-permute-start(bf16[1024,512]{1,0:T(8,128)(2,1)S(1)} %pad_maximum_fusion.4), channel_id=1, source_target_pairs={{0,4},{4,0},{8,12},{12,8},{1,5},{5,1},{9,13},{13,9},{2,6},{6,2},{1... | collective-permute-start | bytes 3145736 | tf_op jit(solution)/shard_map/ppermute | solution.py:12
  68.9 9.3 %collective-permute-start.21 = (bf16[256,512]{1,0:T(8,128)(2,1)}, bf16[256,512]{1,0:T(8,128)(2,1)S(1)}, u32[]{:S(2)}, u32[]{:S(2)}) collective-permute-start(bf16[256,512]{1,0:T(8,128)(2,1)} %collective-permute-done.20), channel_id=1, source_target_pairs={{0,8},{4,12},{8,0},{12,4},{16,24},{20,28},{24,16},{28,20},{1,9},{5... | collective-permute-start | bytes 786440 | tf_op jit(solution)/shard_map/ppermute | solution.py:12
  70.1 12.5 %collective-permute-start.22 = (bf16[256,512]{1,0:T(8,128)(2,1)}, bf16[256,512]{1,0:T(8,128)(2,1)}, u32[]{:S(2)}, u32[]{:S(2)}) collective-permute-start(bf16[256,512]{1,0:T(8,128)(2,1)} %collective-permute-done.20), channel_id=1, source_target_pairs={{0,16},{4,20},{8,24},{12,28},{16,0},{20,4},{24,8},{28,12},{1,17},{... | collective-permute-start | bytes 786440 | tf_op jit(solution)/shard_map/ppermute | solution.py:12
  70.9 14.1 %collective-permute-start.23 = (bf16[256,512]{1,0:T(8,128)(2,1)}, bf16[256,512]{1,0:T(8,128)(2,1)}, u32[]{:S(2)}, u32[]{:S(2)}) collective-permute-start(bf16[256,512]{1,0:T(8,128)(2,1)} %collective-permute-done.20), channel_id=1, source_target_pairs={{0,24},{4,28},{8,16},{12,20},{16,8},{20,12},{24,0},{28,4},{1,25},{... | collective-permute-start | bytes 786440 | tf_op jit(solution)/shard_map/ppermute | solution.py:12
  73.4 14.2 %copy-start.5 = (bf16[256,512]{1,0:T(8,128)(2,1)S(1)}, bf16[256,512]{1,0:T(8,128)(2,1)}, u32[]{:S(2)}) copy-start(bf16[256,512]{1,0:T(8,128)(2,1)} %copy-done.4) | copy-start | bytes 786436
  73.4 14.2 %copy-start.9 = (bf16[256,512]{1,0:T(8,128)(2,1)S(1)}, bf16[256,512]{1,0:T(8,128)(2,1)}, u32[]{:S(2)}) copy-start(bf16[256,512]{1,0:T(8,128)(2,1)} %copy-done.8) | copy-start | bytes 786436
  78.2 1.2 copy-start.3
  78.2 9.4 %copy-start.7 = (bf16[256,512]{1,0:T(8,128)(2,1)S(1)}, bf16[256,512]{1,0:T(8,128)(2,1)}, u32[]{:S(2)}) copy-start(bf16[256,512]{1,0:T(8,128)(2,1)} %copy-done.6) | copy-start | bytes 786436
  78.2 17.6 %collective-permute-start.5 = (s32[2]{0:T(128)S(1)}, s32[2]{0:T(128)S(1)}, u32[]{:S(2)}, u32[]{:S(2)}) collective-permute-start(s32[2]{0:T(128)S(1)} %pad_add_fusion.1), channel_id=1, source_target_pairs={{0,8},{4,12},{8,0},{12,4},{1,9},{5,13},{9,1},{13,5},{2,10},{6,14},... | collective-permute-start | bytes 32 | tf_op jit(solution)/shard_map/ppermute | solution.py:12
  82.5 54.1 %collective-permute-start.3 = (bf16[2,64,2048]{2,1,0:T(8,128)(2,1)}, bf16[2,64,2048]{2,1,0:T(8,128)(2,1)S(1)}, u32[]{:S(2)}, u32[]{:S(2)}) collective-permute-start(bf16[2,64,2048]{2,1,0:T(8,128)(2,1)} %pad_maximum_fusion.5), channel_id=1, source_target_pairs={{0,8},{4,12},{8,0},{12,4},{1,9},{5,13},{9,1},{13,5},{2,10},{6,14},... | collective-permute-start | bytes 1572872 | tf_op jit(solution)/shard_map/ppermute | solution.py:12
  85.1 2.9 %copy-start.13 = (bf16[1024,2048]{1,0:T(8,128)(2,1)S(1)}, bf16[1024,2048]{1,0:T(8,128)(2,1)}, u32[]{:S(2)}) copy-start(bf16[1024,2048]{1,0:T(8,128)(2,1)} %copy-done.12) | copy-start | bytes 12582916
  87.5 18.0 %collective-permute-start.24 = (bf16[1024,512]{1,0:T(8,128)(2,1)}, bf16[1024,512]{1,0:T(8,128)(2,1)}, u32[]{:S(2)}, u32[]{:S(2)}) collective-permute-start(bf16[1024,512]{1,0:T(8,128)(2,1)} %pad_maximum_fusion.3), channel_id=1, source_target_pairs={{0,4},{4,0},{8,12},{12,8},{1,5},{5,1},{9,13},{13,9},{2,6},{6,2},{1... | collective-permute-start | bytes 3145736 | tf_op jit(solution)/shard_map/ppermute | solution.py:12
  91.4 26.6 %collective-permute-start.30 = (bf16[1024,512]{0,1:T(8,128)(2,1)}, bf16[1024,512]{0,1:T(8,128)(2,1)}, u32[]{:S(2)}, u32[]{:S(2)}) collective-permute-start(bf16[1024,512]{0,1:T(8,128)(2,1)} %get-tuple-element.42), channel_id=1, source_target_pairs={{0,1},{3,2},{4,5},{7,6},{8,9},{11,10},{12,13},{15,14},{16,17},{19,... | collective-permute-start | bytes 3145736 | tf_op jit(solution)/shard_map/ppermute | solution.py:16
  95.9 1.1 collective-permute-start.6
  99.5 33.8 %collective-permute-start.15 = (bf16[256,512]{1,0:T(8,128)(2,1)S(1)}, bf16[256,512]{1,0:T(8,128)(2,1)}, u32[]{:S(2)}, u32[]{:S(2)}) collective-permute-start(bf16[256,512]{1,0:T(8,128)(2,1)S(1)} %collective-permute-done.14), channel_id=1, source_target_pairs={{0,8},{4,12},{8,0},{12,4},{16,24},{20,28},{24,16},{28,20},{1,9},{5... | collective-permute-start | bytes 786440 | tf_op jit(solution)/shard_map/ppermute | solution.py:12
  99.9 33.8 %collective-permute-start.16 = (bf16[256,512]{1,0:T(8,128)(2,1)S(1)}, bf16[256,512]{1,0:T(8,128)(2,1)}, u32[]{:S(2)}, u32[]{:S(2)}) collective-permute-start(bf16[256,512]{1,0:T(8,128)(2,1)S(1)} %collective-permute-done.14), channel_id=1, source_target_pairs={{0,16},{4,20},{8,24},{12,28},{16,0},{20,4},{24,8},{28,12},{1,17},{... | collective-permute-start | bytes 786440 | tf_op jit(solution)/shard_map/ppermute | solution.py:12
  105.5 29.8 %collective-permute-start.17 = (bf16[256,512]{1,0:T(8,128)(2,1)S(1)}, bf16[256,512]{1,0:T(8,128)(2,1)}, u32[]{:S(2)}, u32[]{:S(2)}) collective-permute-start(bf16[256,512]{1,0:T(8,128)(2,1)S(1)} %collective-permute-done.14), channel_id=1, source_target_pairs={{0,24},{4,28},{8,16},{12,20},{16,8},{20,12},{24,0},{28,4},{1,25},{... | collective-permute-start | bytes 786440 | tf_op jit(solution)/shard_map/ppermute | solution.py:12
  124.2 26.8 %collective-permute-start.32 = (bf16[1024,512]{0,1:T(8,128)(2,1)}, bf16[1024,512]{0,1:T(8,128)(2,1)}, u32[]{:S(2)}, u32[]{:S(2)}) collective-permute-start(bf16[1024,512]{0,1:T(8,128)(2,1)} %get-tuple-element.27), channel_id=1, source_target_pairs={{0,1},{3,2},{4,5},{7,6},{8,9},{11,10},{12,13},{15,14},{16,17},{19,... | collective-permute-start | bytes 3145736 | tf_op jit(solution)/shard_map/ppermute | solution.py:16
  133.3 58.6 %collective-permute-start.12 = (bf16[2,64,512]{2,1,0:T(8,128)(2,1)S(1)}, bf16[2,64,512]{2,1,0:T(8,128)(2,1)S(1)}, u32[]{:S(2)}, u32[]{:S(2)}) collective-permute-start(bf16[2,64,512]{2,1,0:T(8,128)(2,1)S(1)} %reshape.84), channel_id=1, source_target_pairs={{0,8},{4,12},{8,0},{12,4},{1,9},{5,13},{9,1},{13,5},{2,10},{6,14},... | collective-permute-start | bytes 393224 | tf_op jit(solution)/shard_map/ppermute | solution.py:12
  133.7 4.7 %collective-permute-start.10 = (bf16[2,64]{1,0:T(2,128)(2,1)S(1)}, bf16[2,64]{1,0:T(2,128)(2,1)S(1)}, u32[]{:S(2)}, u32[]{:S(2)}) collective-permute-start(bf16[2,64]{1,0:T(2,128)(2,1)S(1)} %pad_maximum_fusion.10), channel_id=1, source_target_pairs={{0,8},{4,12},{8,0},{12,4},{1,9},{5,13},{9,1},{13,5},{2,10},{6,14},... | collective-permute-start | bytes 776 | tf_op jit(solution)/shard_map/ppermute | solution.py:12
  136.6 17.6 %collective-permute-start.18 = (bf16[1024,512]{1,0:T(8,128)(2,1)S(1)}, bf16[1024,512]{1,0:T(8,128)(2,1)S(1)}, u32[]{:S(2)}, u32[]{:S(2)}) collective-permute-start(bf16[1024,512]{1,0:T(8,128)(2,1)S(1)} %pad_maximum_fusion.2), channel_id=1, source_target_pairs={{0,4},{4,0},{8,12},{12,8},{1,5},{5,1},{9,13},{13,9},{2,6},{6,2},{1... | collective-permute-start | bytes 3145736 | tf_op jit(solution)/shard_map/ppermute | solution.py:12
  136.8 17.5 %collective-permute-start.4 = (bf16[4,64,2048]{2,1,0:T(8,128)(2,1)S(1)}, bf16[4,64,2048]{2,1,0:T(8,128)(2,1)S(1)}, u32[]{:S(2)}, u32[]{:S(2)}) collective-permute-start(bf16[4,64,2048]{2,1,0:T(8,128)(2,1)S(1)} %pad_maximum_fusion.1), channel_id=1, source_target_pairs={{0,4},{4,0},{8,12},{12,8},{1,5},{5,1},{9,13},{13,9},{2,6},{6,2},{1... | collective-permute-start | bytes 3145736 | tf_op jit(solution)/shard_map/ppermute | solution.py:12
  138.4 51.4 %collective-permute-start.11 = (bf16[4,64]{1,0:T(4,128)(2,1)S(1)}, bf16[4,64]{1,0:T(4,128)(2,1)S(1)}, u32[]{:S(2)}, u32[]{:S(2)}) collective-permute-start(bf16[4,64]{1,0:T(4,128)(2,1)S(1)} %pad_maximum_fusion.9), channel_id=1, source_target_pairs={{0,4},{4,0},{8,12},{12,8},{1,5},{5,1},{9,13},{13,9},{2,6},{6,2},{1... | collective-permute-start | bytes 1544 | tf_op jit(solution)/shard_map/ppermute | solution.py:12
  152.5 14.2 %collective-permute-start.33 = (bf16[1024,512]{0,1:T(8,128)(2,1)S(1)}, bf16[1024,512]{0,1:T(8,128)(2,1)S(1)}, u32[]{:S(2)}, u32[]{:S(2)}) collective-permute-start(bf16[1024,512]{0,1:T(8,128)(2,1)S(1)} %add_convert_fusion.1), channel_id=1, source_target_pairs={{1,2},{2,1},{5,6},{6,5},{9,10},{10,9},{13,14},{14,13},{17,18},{18,... | collective-permute-start | bytes 3145736 | tf_op jit(solution)/shard_map/ppermute | solution.py:16
  154.3 2.2 copy-start.1
  156.5 10.2 %copy-start.14 = (bf16[1024,2048]{1,0:T(8,128)(2,1)S(1)}, bf16[1024,2048]{1,0:T(8,128)(2,1)}, u32[]{:S(2)}) copy-start(bf16[1024,2048]{1,0:T(8,128)(2,1)} %copy-done.12) | copy-start | bytes 12582916
  157.9 33.2 %collective-permute-start.7 = (f32[2,512,64]{1,2,0:T(8,128)S(1)}, f32[2,512,64]{1,2,0:T(8,128)S(1)}, u32[]{:S(2)}, u32[]{:S(2)}) collective-permute-start(f32[2,512,64]{1,2,0:T(8,128)S(1)} %convolution_bitcast_fusion), channel_id=1, source_target_pairs={{0,1},{3,2},{4,5},{7,6},{8,9},{11,10},{12,13},{15,14},{16,17},{19,... | collective-permute-start | bytes 786440 | tf_op jit(solution)/shard_map/ppermute | solution.py:16
  165.0 54.9 %collective-permute-start.31 = (bf16[1024,512]{0,1:T(8,128)(2,1)}, bf16[1024,512]{0,1:T(8,128)(2,1)}, u32[]{:S(2)}, u32[]{:S(2)}) collective-permute-start(bf16[1024,512]{0,1:T(8,128)(2,1)} %get-tuple-element.26), channel_id=1, source_target_pairs={{1,2},{2,1},{5,6},{6,5},{9,10},{10,9},{13,14},{14,13},{17,18},{18,... | collective-permute-start | bytes 3145736 | tf_op jit(solution)/shard_map/ppermute | solution.py:16
  170.5 22.9 %copy-start.10 = (bf16[8,64,512]{2,1,0:T(8,128)(2,1)S(1)}, bf16[8,64,512]{2,1,0:T(8,128)(2,1)}, u32[]{:S(2)}) copy-start(bf16[8,64,512]{2,1,0:T(8,128)(2,1)} %constant_dynamic-update-slice_fusion.2) | copy-start | bytes 1572868
  170.5 49.4 %collective-permute-start.19 = (bf16[1024,512]{0,1:T(8,128)(2,1)}, bf16[1024,512]{0,1:T(8,128)(2,1)}, u32[]{:S(2)}, u32[]{:S(2)}) collective-permute-start(bf16[1024,512]{0,1:T(8,128)(2,1)} %get-tuple-element.24), channel_id=1, source_target_pairs={{0,1},{3,2},{4,5},{7,6},{8,9},{11,10},{12,13},{15,14},{16,17},{19,... | collective-permute-start | bytes 3145736 | tf_op jit(solution)/shard_map/ppermute | solution.py:16
  189.8 30.1 %collective-permute-start.34 = (bf16[1024,512]{0,1:T(8,128)(2,1)}, bf16[1024,512]{0,1:T(8,128)(2,1)}, u32[]{:S(2)}, u32[]{:S(2)}) collective-permute-start(bf16[1024,512]{0,1:T(8,128)(2,1)} %get-tuple-element.25), channel_id=1, source_target_pairs={{2,3},{1,0},{6,7},{5,4},{10,11},{9,8},{14,15},{13,12},{18,19},{17,... | collective-permute-start | bytes 3145736 | tf_op jit(solution)/shard_map/ppermute | solution.py:16
  191.2 0.8 collective-permute-start.8
  191.9 1.6 collective-permute-start.13
  192.1 25.4 %collective-permute-start.9 = (f32[2,512,64]{1,2,0:T(8,128)S(1)}, f32[2,512,64]{1,2,0:T(8,128)S(1)}, u32[]{:S(2)}, u32[]{:S(2)}) collective-permute-start(f32[2,512,64]{1,2,0:T(8,128)S(1)} %add.138), channel_id=1, source_target_pairs={{2,3},{1,0},{6,7},{5,4},{10,11},{9,8},{14,15},{13,12},{18,19},{17,... | collective-permute-start | bytes 786440 | tf_op jit(solution)/shard_map/ppermute | solution.py:16

commit v2 on v1

v2 whole, which is shorter than its diff:
```python
import functools

import jax
import jax.numpy as jnp
from jax import lax
from jax.experimental import pallas as pl
from jax.experimental.pallas import tpu as pltpu
from jax.sharding import PartitionSpec as P

CAPO = 2
F32 = jnp.float32
BF16 = jnp.bfloat16
I32 = jnp.int32
VMEM_LIMIT = 60 * 1024 * 1024
SMALL = pl.CostEstimate(flops=1, bytes_accessed=1, transcendentals=0)


def swap(value, axis, size, mask):
    return lax.ppermute(value, axis, [(i, i ^ mask) for i in range(size)])


def hop(value, n, at):
    return lax.ppermute(value, "mp", [(at, at + 1), (n - 1 - at, n - 2 - at)])


def tied(value, *others):
    return lax.optimization_barrier((value, *others))[0]


def partial_kernel(masks, share_ref, tok_ref, *refs):
    pieces = refs[: len(masks)]
    low_ref, full_ref, weight = refs[len(masks) :]
    rows = weight.shape[0] // len(masks)

    @pl.when(pl.program_id(0) == 0)
    def _():
        for mask, piece in zip(masks, pieces):
            to = pl.multiple_of((share_ref[0] ^ mask) * rows, rows)
            weight[pl.ds(to, rows), :] = piece[...]

    product = jnp.dot(tok_ref[...], weight[...], preferred_element_type=F32)
    full_ref[...] = product
    low_ref[...] = product.astype(low_ref.dtype)


def partial_product(share, tokens, pieces, low_type):
    tok_dev, depth = tokens.shape
    masks, pieces = tuple(pieces), tuple(pieces.values())
    cols = pieces[0].shape[1]
    tile = min(256, tok_dev)
    whole = lambda i, s: (0, 0)
    row = lambda i, s: (i, 0)
    return pl.pallas_call(
        functools.partial(partial_kernel, masks),
        out_shape=(
            jax.ShapeDtypeStruct((tok_dev, cols), low_type),
            jax.ShapeDtypeStruct((tok_dev, cols), F32),
        ),
        grid_spec=pltpu.PrefetchScalarGridSpec(
            num_scalar_prefetch=1,
            grid=(tok_dev // tile,),
            in_specs=[pl.BlockSpec((tile, depth), row)]
            + [pl.BlockSpec(piece.shape, whole) for piece in pieces],
            out_specs=(pl.BlockSpec((tile, cols), row), pl.BlockSpec((tile, cols), row)),
            scratch_shapes=[pltpu.VMEM((depth, cols), BF16)],
        ),
        compiler_params=pltpu.CompilerParams(vmem_limit_bytes=VMEM_LIMIT),
        cost_estimate=SMALL,
        name="partial_product",
    )(share, tokens, *pieces)


def pack_kernel(n_owner, ten_dev, resp_dev, owner_ref, map_ref, *refs):
    asked_refs = refs[:n_owner]
    in_ref, out_ref, in_to, out_to, pick_ref, sems = refs[n_owner:]
    me = owner_ref[0]
    asked = [map_ref[ref[r]] for ref in asked_refs for r in range(resp_dev)]

    def is_asked(slot):
        hits = [slot == other for other in asked]
        return functools.reduce(jnp.logical_or, hits).astype(I32)

    found = I32(0)
    first, second = I32(0), I32(0)
    for j in range(ten_dev):
        hit = is_asked(me * ten_dev + j)
        first = jnp.where((hit == 1) & (found == 0), j, first)
        second = jnp.where((hit == 1) & (found == 1), j, second)
        found = found + hit
    copies = []
    for c, at in enumerate((first, second)):
        copies.append(pltpu.make_async_copy(in_ref.at[at], in_to.at[c], sems.at[2 * c]))
        copies.append(pltpu.make_async_copy(out_ref.at[at], out_to.at[c], sems.at[2 * c + 1]))
    for copy in copies:
        copy.start()
    for r in range(resp_dev):
        slot = asked[r]
        owner = lax.div(slot, I32(ten_dev))
        before = I32(0)
        for j in range(ten_dev):
            other = owner * ten_dev + j
            before = before + jnp.where(other < slot, is_asked(other), 0)
        mask = owner ^ me
        pick_ref[r] = ((mask >> 1) + (mask & 1) * (n_owner // 2)) * CAPO + before
    for copy in copies:
        copy.wait()


def pack(owner, owner_map, asked, delta_in, out_rows):
    ten_dev = delta_in.shape[0]
    smem = pl.BlockSpec(memory_space=pltpu.SMEM)
    hbm = pl.BlockSpec(memory_space=pl.ANY)
    vmem = pl.BlockSpec(memory_space=pltpu.VMEM)
    return pl.pallas_call(
        functools.partial(pack_kernel, len(asked), ten_dev, asked[0].shape[0]),
        out_shape=(
            jax.ShapeDtypeStruct((CAPO,) + delta_in.shape[1:], BF16),
            jax.ShapeDtypeStruct((CAPO,) + out_rows.shape[1:], BF16),
            jax.ShapeDtypeStruct(asked[0].shape, I32),
        ),
        in_specs=[smem] * (2 + len(asked)) + [hbm, hbm],
        out_specs=(vmem, vmem, smem),
        scratch_shapes=[pltpu.SemaphoreType.DMA((2 * CAPO,))],
        compiler_params=pltpu.CompilerParams(vmem_limit_bytes=VMEM_LIMIT),
        cost_estimate=SMALL,
        name="pack_named",
    )(owner, owner_map, *asked, delta_in, out_rows)


def coeff_kernel(pick_ref, tok_ref, mine_ref, other_ref, coeff_ref, *, half):
    here = pick_ref[pl.program_id(0)] < half
    factor = jnp.where(here, mine_ref[...].astype(F32), other_ref[...].astype(F32)).astype(BF16)
    coeff_ref[...] = lax.dot_general(
        factor, tok_ref[...], (((1,), (1,)), ((), ())), preferred_element_type=F32
    )


def coefficients(pick, tokens, mine, other, resp_len):
    depth = tokens.shape[1]
    half, rank = mine.shape[0], mine.shape[1]
    resp_dev = pick.shape[0]
    return pl.pallas_call(
        functools.partial(coeff_kernel, half=half),
        out_shape=jax.ShapeDtypeStruct((resp_dev, rank, resp_len), F32),
        grid_spec=pltpu.PrefetchScalarGridSpec(
            num_scalar_prefetch=1,
            grid=(resp_dev,),
            in_specs=[
                pl.BlockSpec((resp_len, depth), lambda r, p: (r, 0)),
                pl.BlockSpec((None, rank, depth), lambda r, p: (jnp.minimum(p[r], half - 1), 0, 0)),
                pl.BlockSpec((None, rank, depth), lambda r, p: (jnp.maximum(p[r] - half, 0), 0, 0)),
            ],
            out_specs=pl.BlockSpec((None, rank, resp_len), lambda r, p: (r, 0, 0)),
        ),
        compiler_params=pltpu.CompilerParams(vmem_limit_bytes=VMEM_LIMIT),
        cost_estimate=SMALL,
        name="coefficients",
    )(pick, tokens, mine, other)


def shards(tokens, kv_weight, delta_in, delta_out, delta_scale, owner_map, resp_tenant):
    tok_dev, d_shard = tokens.shape
    resp_dev = resp_tenant.shape[0]
    resp_len = tok_dev // resp_dev
    rank = delta_in.shape[1]
    head_cols = kv_weight.shape[2]
    cols = 2 * head_cols
    n_owner = lax.axis_size("tenant")
    n = lax.axis_size("mp")
    plane = lax.axis_size("group") * n_owner
    share_rows = d_shard // plane
    me_mp = lax.axis_index("mp")
    me_owner = lax.axis_index("tenant")
    me_share = lax.axis_index("group") * n_owner + me_owner
    share = me_share.astype(I32).reshape(1)
    hop_type = BF16 if n <= 4 else F32

    def sent(k):
        row = (me_mp ^ k) * d_shard + me_share * share_rows
        return lax.dynamic_slice_in_dim(kv_weight, row, share_rows, 0).reshape(share_rows, cols)

    def shared(arrived):
        pieces = {0: arrived}
        for mask in range(2, plane, 2):
            pieces[mask] = swap(arrived, ("group", "tenant"), plane, mask)
        for mask in range(0, plane, 2):
            pieces[mask | 1] = swap(pieces[mask], "tenant", n_owner, 1)
        return pieces

    order = list(range(n - 1, 0, -1))
    low, full, before = {}, {}, []
    last = None
    for k in order:
        block = sent(k) if last is None else tied(sent(k), last)
        last = swap(block, "mp", n, k)
        here = tied(last, low[k + 1]) if k + 1 in low else last
        pieces = shared(here)
        before.append(pieces[plane - 2])
        low[k], full[k] = partial_product(share, tokens, pieces, hop_type)

    asked = [resp_tenant] + [swap(resp_tenant, "tenant", n_owner, m) for m in range(1, n_owner)]
    pad = ((0, 0), (0, 0), (0, 1), (0, head_cols - rank))
    out_rows = jnp.concatenate([delta_out, jnp.pad(delta_scale[:, None, None, :], pad)], axis=1)
    packed_in, packed_out, pick = pack(
        me_owner.astype(I32).reshape(1), owner_map, asked, delta_in, out_rows
    )

    def spread(packed):
        mine = jnp.concatenate(
            [packed] + [swap(packed, "tenant", n_owner, m) for m in range(2, n_owner, 2)], axis=0
        )
        return mine, swap(mine, "tenant", n_owner, 1)

    packed_in = tied(packed_in, before[0])
    part_coeff = coefficients(pick, tokens, *spread(packed_in), resp_len)
    coeff, came = part_coeff, None
    for h in range(n - 1):
        came = hop(part_coeff if came is None else part_coeff + came, n, h)
        coeff = coeff + came
    all_out = jnp.concatenate(spread(packed_out), axis=0)
    chosen = jnp.stack(
        [lax.dynamic_index_in_dim(all_out, pick[r], 0, keepdims=False) for r in range(resp_dev)]
    )
    scale = chosen[:, rank, 0, :rank].astype(F32)
    lowrank = (coeff * scale[:, :, None]).astype(BF16)
    delta = jnp.einsum(
        "rkl,rkc->rlc",
        lowrank,
        chosen[:, :rank].reshape(resp_dev, rank, cols),
        preferred_element_type=F32,
    ).reshape(tok_dev, cols)
    own = lax.dynamic_slice_in_dim(kv_weight, me_mp * d_shard, d_shard, 0).reshape(d_shard, cols)
    base = jnp.dot(tokens, own, preferred_element_type=F32) + delta

    came = []
    for s in range(1, n):
        now = []
        for h in range(s):
            k = h ^ (h + n - s)
            load = low[k] if h == 0 else (full[k] + came[h - 1].astype(F32)).astype(hop_type)
            now.append(hop(load, n, h))
        came = now
    total = lax.optimization_barrier(base)
    for value in came:
        total = total + value.astype(F32)
    return total.astype(BF16).reshape(tok_dev, 2, head_cols)


def solution(mesh):
    return jax.shard_map(
        shards,
        mesh=mesh,
        in_specs=(
            P(("group", "tenant"), "mp"),
            P(None, None, "mp"),
            P(("group", "tenant"), None, "mp"),
            P(("group", "tenant"), None, None, "mp"),
            P(("group", "tenant"), None),
            P("group"),
            P(("group", "tenant")),
        ),
        out_specs=P(("group", "tenant"), None, "mp"),
        check_vma=False,
    )
```

time: 227 us -> 170 us (0.75)
  local copies, waits for them, and re-layouts: 48.5 us -> 15.1 us
  Pallas kernels: 0 us -> 27.3 us
  starting transfers between devices: 66.8 us -> 46.3 us
  matrix products: 19.1 us -> 6.12 us
  waiting for transfers between devices: 63.1 us -> 56.8 us
  between operations: 10.6 us -> 4.32 us
  other arithmetic: 17.8 us -> 13.6 us
    pallas_call x0 -> x5, Pallas kernels: none -> 27.3 us  [the longest x3 20 us: partial_product(): pl.pallas_call(functools.partial(partial_kernel, masks), out_shape=(jax.S...]
    ppermute x9, starting transfers between devices: 42 us -> 17.2 us  [hop(): return lax.ppermute(value, 'mp', [(at, at + 1), (n - 1 - at, n - 2 - at)])]
    ppermute x9, waiting for transfers between devices: 44.1 us -> 22.3 us  [hop(): return lax.ppermute(value, 'mp', [(at, at + 1), (n - 1 - at, n - 2 - at)])]
    unnamed x58 -> x77, local copies, waits for them, and re-layouts: 25.3 us -> 7.07 us
    ppermute x26 -> x31, waiting for transfers between devices: 19 us -> 34.5 us  [swap(): return lax.ppermute(value, axis, [(i, i ^ mask) for i in range(size)])]
    dot_general x6 -> x2, matrix products: 19.1 us -> 6.12 us  [the longest x1 4.52 us: shards(): base = jnp.dot(tokens, own, preferred_element_type=F32) + delta]
    dynamic_slice x16 -> x2, local copies, waits for them, and re-layouts: 13 us -> 1.8 us  [the longest x1 1.7 us: sent(): lax.dynamic_slice_in_dim(kv_weight, row, share_rows, 0)]
    convert_element_type x3 -> x4, other arithmetic: 1.58 us -> 7.28 us  [the longest x3 7.28 us: shards(): (full[k] + came[h - 1].astype(F32)).astype(hop_type)]
  transfers between devices with their start and end apart: 35 -> 40, of which waited for: 10 -> 12; matrix products, arithmetic and copies ran while one was open for 32% -> 15% of each run, Pallas kernels for 0% -> 16%
where the time goes in v2:
time: 170 us
  waiting for transfers between devices  56.8 us (33%)
  starting transfers between devices  46.3 us (27%)
  Pallas kernels  27.3 us (16%)
  local copies, waits for them, and re-layouts  15.1 us (9%)
  other arithmetic  13.6 us (8%)
  matrix products  6.12 us (4%)
  between operations  4.32 us (3%)
    ppermute x31, waiting for transfers between devices, swap(): return lax.ppermute(value, axis, [(i, i ^ mask) for i in range(size)])  34.5 us
    ppermute x31, starting transfers between devices, swap(): return lax.ppermute(value, axis, [(i, i ^ mask) for i in range(size)])  29.1 us
    ppermute x9, waiting for transfers between devices, hop(): return lax.ppermute(value, 'mp', [(at, at + 1), (n - 1 - at, n - 2 - at)])  22.3 us
    pallas_call x3, Pallas kernels, partial_product(): pl.pallas_call(functools.partial(partial_kernel, masks), out_shape=(jax.S...  20 us
    ppermute x9, starting transfers between devices, hop(): return lax.ppermute(value, 'mp', [(at, at + 1), (n - 1 - at, n - 2 - at)])  17.2 us
    convert_element_type x3, other arithmetic, shards(): (full[k] + came[h - 1].astype(F32)).astype(hop_type)  7.28 us
    unnamed x77, local copies, waits for them, and re-layouts  7.07 us
    pallas_call x1, Pallas kernels, coefficients(): pl.pallas_call(functools.partial(coeff_kernel, half=half), out_shape=jax....  4.58 us
  transfers between devices with their start and end apart: 40, of which 12 were waited for; matrix products, arithmetic and copies ran while one was open for 15% of the time, Pallas kernels for 16%

profile of v2, /device:TPU:0, one launch (start us, length us, event | category | flops | bytes accessed | tf_op | source)
XLA Modules:
  0.0 169.6 jit_solution(4218630722153219889)
XLA Ops:
  0.0 1.7 %constant_dynamic-slice_fusion.4 = (bf16[256,2,256]{2,1,0:T(2,128)(2,1)S(1)}, bf16[256,2,256]{2,1,0:T(2,128)(2,1)S(1)}, bf16[256,2,256]{2,1,0:T(2,128)(2,1)S(1)}) fusion(bf16[8192,2,256]{2,1,0:T(2,128)(2,1)} %param.8, s32[]{:T(128)S(6)} %select_n.20, s32[]{:T(128)S(6)} %select_n.24, s32[]{:T(128)S(6)} %select_n.23), kind=kLoop, calls=%fused_computation.21 | loop fusion | bytes 1572876 | tf_op jit(solution)/shard_map/dynamic_slice | solution.py:180
  1.7 5.1 %collective-permute-start.3 = (bf16[256,512]{1,0:T(8,128)(2,1)S(1)}, bf16[256,512]{1,0:T(8,128)(2,1)S(1)}, u32[]{:S(2)}, u32[]{:S(2)}) collective-permute-start(bf16[256,512]{1,0:T(8,128)(2,1)S(1)} %bitcast.27), channel_id=1, source_target_pairs={{0,3},{1,2},{2,1},{3,0},{4,7},{5,6},{6,5},{7,4},{8,11},{9,10},{10,... | collective-permute-start | bytes 786440 | tf_op jit(solution)/shard_map/ppermute | solution.py:19
  6.9 6.4 %collective-permute-done.3.refs_0_ = bf16[256,512]{1,0:T(8,128)(2,1)S(1)} collective-permute-done((bf16[256,512]{1,0:T(8,128)(2,1)S(1)}, bf16[256,512]{1,0:T(8,128)(2,1)S(1)}, u32[]{:S(2)}, u32[]{:S(2)}) %collective-permute-start.3) | collective-permute-done | bytes 262176 | tf_op jit(solution)/shard_map/ppermute | solution.py:19
  13.3 2.4 %collective-permute-start.4 = (bf16[256,512]{1,0:T(8,128)(2,1)S(1)}, bf16[256,512]{1,0:T(8,128)(2,1)S(1)}, u32[]{:S(2)}, u32[]{:S(2)}) collective-permute-start(bf16[256,512]{1,0:T(8,128)(2,1)S(1)} %collective-permute-done.3.refs_0_), channel_id=1, source_target_pairs={{0,24},{4,28},{8,16},{12,20},{16,8},{20,12},{24,0},{28,4},{1,25},{... | collective-permute-start | bytes 786440 | tf_op jit(solution)/shard_map/ppermute | solution.py:19
  15.8 0.5 collective-permute-start.14
  16.3 0.5 collective-permute-start.15
  16.8 6.7 %collective-permute-done.4.refs_3_ = bf16[256,512]{1,0:T(8,128)(2,1)S(1)} collective-permute-done((bf16[256,512]{1,0:T(8,128)(2,1)S(1)}, bf16[256,512]{1,0:T(8,128)(2,1)S(1)}, u32[]{:S(2)}, u32[]{:S(2)}) %collective-permute-start.4) | collective-permute-done | bytes 262176 | tf_op jit(solution)/shard_map/ppermute | solution.py:19
  23.5 3.7 %collective-permute-done.14.refs_1_ = bf16[256,512]{1,0:T(8,128)(2,1)S(1)} collective-permute-done((bf16[256,512]{1,0:T(8,128)(2,1)S(1)}, bf16[256,512]{1,0:T(8,128)(2,1)S(1)}, u32[]{:S(2)}, u32[]{:S(2)}) %collective-permute-start.14) | collective-permute-done | bytes 262176 | tf_op jit(solution)/shard_map/ppermute | solution.py:19
  27.8 1.1 fusion.refs_5_
  29.1 1.5 collective-permute-start.1
  30.6 2.0 %collective-permute-done.1.refs_2_ = s32[2]{0:T(128)S(1)} collective-permute-done((s32[2]{0:T(128)S(1)}, s32[2]{0:T(128)S(1)}, u32[]{:S(2)}, u32[]{:S(2)}) %collective-permute-start.1) | collective-permute-done | bytes 40 | tf_op jit(solution)/shard_map/ppermute | solution.py:19
  32.8 2.8 %collective-permute-done.2.refs_3_ = s32[2]{0:T(128)S(1)} collective-permute-done((s32[2]{0:T(128)S(1)}, s32[2]{0:T(128)S(1)}, u32[]{:S(2)}, u32[]{:S(2)}) %collective-permute-start.2) | collective-permute-done | bytes 40 | tf_op jit(solution)/shard_map/ppermute | solution.py:19
  35.6 0.6 copy-done.34
  36.2 2.7 %pack_named.1 = (bf16[2,64,2048]{2,1,0:T(8,128)(2,1)}, bf16[2,65,2,256]{3,2,1,0:T(2,128)(2,1)}, s32[2]{0:T(128)}) custom-call(s32[1]{0:T(128)} %bitcast.1.owner_ref, s32[24]{0:T(128)} %map_ref.1, s32[2]{0:T(128)} %refs_0_.1, s32[2]{0:T(128)} %copy-done.32, s32[2]{0:T(128)} %copy-done.33, s32[2]{0:T(128)} %copy-done.34, bf16[6,64,2048]{2,1,0:T(8,128)(2,1)} %refs_4_.1, ...), custom_call_target="tpu_custom_call" | custom-call | flops 1 | bytes 1 | tf_op jit(solution)/shard_map/pack_named/pallas_call | solution.py:114
  38.9 6.3 %collective-permute-start.12 = (bf16[256,512]{1,0:T(8,128)(2,1)S(1)}, bf16[256,512]{1,0:T(8,128)(2,1)S(1)}, u32[]{:S(2)}, u32[]{:S(2)}) collective-permute-start(bf16[256,512]{1,0:T(8,128)(2,1)S(1)} %bitcast.26), channel_id=1, source_target_pairs={{0,2},{1,3},{2,0},{3,1},{4,6},{5,7},{6,4},{7,5},{8,10},{9,11},{10,... | collective-permute-start | bytes 786440 | tf_op jit(solution)/shard_map/ppermute | solution.py:19
  45.2 1.5 collective-permute-start.5
  46.8 0.6 copy-done.20
  47.6 6.7 %partial_product.3 = (bf16[1024,512]{1,0:T(8,128)(2,1)}, f32[1024,512]{1,0:T(8,128)}) custom-call(s32[1]{0:T(128)} %bitcast.7.share_ref, bf16[1024,2048]{1,0:T(8,128)(2,1)} %tok_ref.7, bf16[256,512]{1,0:T(8,128)(2,1)} %copy-done.12, bf16[256,512]{1,0:T(8,128)(2,1)} %copy-done.15, bf16[256,512]{1,0:T(8,128)(2,1)} %copy-done.16, bf16[256,512]{1,0:T(8,128)(2,1)} %copy-done.13, ...), custom_call_target="tpu_custom_call" | custom-call | flops 1 | bytes 1 | tf_op jit(solution)/shard_map/partial_product/pallas_call | solution.py:53
  54.3 2.3 %collective-permute-start.37 = (bf16[1024,512]{1,0:T(8,128)(2,1)}, bf16[1024,512]{1,0:T(8,128)(2,1)}, u32[]{:S(2)}, u32[]{:S(2)}) collective-permute-start(bf16[1024,512]{1,0:T(8,128)(2,1)} %get-tuple-element.25), channel_id=1, source_target_pairs={{0,1},{3,2},{4,5},{7,6},{8,9},{11,10},{12,13},{15,14},{16,17},{19,... | collective-permute-start | bytes 3145736 | tf_op jit(solution)/shard_map/ppermute | solution.py:23
  56.5 0.6 collective-permute-done.12.refs_0_
  57.1 0.7 collective-permute-start.20
  57.9 1.3 collective-permute-start.10
  59.2 1.2 collective-permute-start.21
  60.4 7.1 %collective-permute-done.10 = bf16[2,65,2,256]{3,2,1,0:T(2,128)(2,1)S(1)} collective-permute-done((bf16[2,65,2,256]{3,2,1,0:T(2,128)(2,1)S(1)}, bf16[2,65,2,256]{3,2,1,0:T(2,128)(2,1)S(1)}, u32[]{:S(2)}, u32[]{:S(2)}) %collective-permute-start.10) | collective-permute-done | bytes 133152 | tf_op jit(solution)/shard_map/ppermute | solution.py:19
  67.5 0.9 collective-permute-start.22
  68.5 0.5 collective-permute-start.24
  69.2 1.0 copy.14
  70.2 5.0 %collective-permute-done.22.refs_3_ = bf16[256,512]{1,0:T(8,128)(2,1)} collective-permute-done((bf16[256,512]{1,0:T(8,128)(2,1)S(1)}, bf16[256,512]{1,0:T(8,128)(2,1)}, u32[]{:S(2)}, u32[]{:S(2)}) %collective-permute-start.22) | collective-permute-done | bytes 262176 | tf_op jit(solution)/shard_map/ppermute | solution.py:19
  75.1 0.5 collective-permute-start.26
  75.9 0.7 copy-done.25
  76.9 0.6 collective-permute-start.11
  77.6 0.7 copy-done.28
  78.3 6.7 %partial_product.4 = (bf16[1024,512]{1,0:T(8,128)(2,1)}, f32[1024,512]{1,0:T(8,128)}) custom-call(s32[1]{0:T(128)} %bitcast.7.share_ref, bf16[1024,2048]{1,0:T(8,128)(2,1)} %tok_ref.7, bf16[256,512]{1,0:T(8,128)(2,1)} %copy-done.10, bf16[256,512]{1,0:T(8,128)(2,1)} %copy-done.14, bf16[256,512]{1,0:T(8,128)(2,1)} %copy-done.18, ...), custom_call_target="tpu_custom_call" | custom-call | flops 1 | bytes 1 | tf_op jit(solution)/shard_map/partial_product/pallas_call | solution.py:53
  85.0 4.0 %collective-permute-start.35 = (bf16[1024,512]{1,0:T(8,128)(2,1)}, bf16[1024,512]{1,0:T(8,128)(2,1)S(1)}, u32[]{:S(2)}, u32[]{:S(2)}) collective-permute-start(bf16[1024,512]{1,0:T(8,128)(2,1)} %get-tuple-element.27), channel_id=1, source_target_pairs={{0,1},{3,2},{4,5},{7,6},{8,9},{11,10},{12,13},{15,14},{16,17},{19,... | collective-permute-start | bytes 3145736 | tf_op jit(solution)/shard_map/ppermute | solution.py:23
  89.3 1.0 collective-permute-start.28
  90.3 3.3 %add_convert_fusion.2 = bf16[1024,512]{1,0:T(8,128)(2,1)} fusion(f32[1024,512]{1,0:T(8,128)} %get-tuple-element.32, bf16[1024,512]{1,0:T(8,128)(2,1)} %collective-permute-done.37), kind=kLoop, calls=%fused_computation.3 | loop fusion | flops 1572864 | bytes 4194304 | tf_op jit(solution)/shard_map/convert_element_type | solution.py:240
  93.6 1.6 collective-permute-start.38
  95.2 3.2 %constant_dynamic-slice_fusion.5 = bf16[2048,2,256]{2,1,0:T(2,128)(2,1)S(1)} fusion(bf16[8192,2,256]{2,1,0:T(2,128)(2,1)} %param.8, s32[]{:T(128)S(6)} %select_n.19), kind=kLoop, calls=%fused_computation.22 | loop fusion | bytes 4194308 | tf_op jit(solution)/shard_map/dynamic_slice | solution.py:232
  98.5 1.9 %copy.12 = bf16[256,8,2,256]{3,1,2,0:T(8,128)(2,1)} copy(bf16[256,8,2,256]{3,2,1,0:T(2,128)(2,1)S(1)} %bitcast.21) | data formatting | bytes 4194304
  100.4 2.2 %collective-permute-start.29 = (bf16[256,512]{1,0:T(8,128)(2,1)S(1)}, bf16[256,512]{1,0:T(8,128)(2,1)}, u32[]{:S(2)}, u32[]{:S(2)}) collective-permute-start(bf16[256,512]{1,0:T(8,128)(2,1)S(1)} %collective-permute-done.13.refs_0_), channel_id=1, source_target_pairs={{0,24},{4,28},{8,16},{12,20},{16,8},{20,12},{24,0},{28,4},{1,25},{... | collective-permute-start | bytes 786440 | tf_op jit(solution)/shard_map/ppermute | solution.py:19
  102.6 0.5 collective-permute-start.31
  103.1 0.6 fusion.3
  107.8 4.6 %coefficients.1 = f32[2,64,512]{2,1,0:T(8,128)} custom-call(s32[2]{0:T(128)} %get-tuple-element.19.pick_ref, bf16[1024,2048]{1,0:T(8,128)(2,1)} %tok_ref.7, bf16[4,64,2048]{2,1,0:T(8,128)(2,1)} %copy-done, bf16[4,64,2048]{2,1,0:T(8,128)(2,1)} %collective-permute-done.6.other_ref), custom_call_target="tpu_custom_call" | custom-call | flops 1 | bytes 1 | tf_op jit(solution)/shard_map/coefficients/pallas_call | solution.py:142
  112.5 0.4 collective-permute-start.33
  113.0 2.8 %collective-permute-start.7 = (f32[2,64,512]{2,1,0:T(8,128)}, f32[2,64,512]{2,1,0:T(8,128)}, u32[]{:S(2)}, u32[]{:S(2)}) collective-permute-start(f32[2,64,512]{2,1,0:T(8,128)} %coefficients.1), channel_id=1, source_target_pairs={{0,1},{3,2},{4,5},{7,6},{8,9},{11,10},{12,13},{15,14},{16,17},{19,... | collective-permute-start | bytes 786440 | tf_op jit(solution)/shard_map/ppermute | solution.py:23
  116.1 0.8 pad_maximum_fusion.1
  117.0 0.7 copy-done.27
  117.7 6.7 %partial_product.5 = (bf16[1024,512]{1,0:T(8,128)(2,1)}, f32[1024,512]{1,0:T(8,128)}) custom-call(s32[1]{0:T(128)} %bitcast.7.share_ref, bf16[1024,2048]{1,0:T(8,128)(2,1)} %tok_ref.7, bf16[256,512]{1,0:T(8,128)(2,1)} %copy-done.9, bf16[256,512]{1,0:T(8,128)(2,1)} %copy-done.11, bf16[256,512]{1,0:T(8,128)(2,1)} %collective-permute-done.28.refs_2_, ...), custom_call_target="tpu_custom_call" | custom-call | flops 1 | bytes 1 | tf_op jit(solution)/shard_map/partial_product/pallas_call | solution.py:53
  124.3 2.3 %collective-permute-start.34 = (bf16[1024,512]{1,0:T(8,128)(2,1)}, bf16[1024,512]{1,0:T(8,128)(2,1)}, u32[]{:S(2)}, u32[]{:S(2)}) collective-permute-start(bf16[1024,512]{1,0:T(8,128)(2,1)} %get-tuple-element.29), channel_id=1, source_target_pairs={{0,1},{3,2},{4,5},{7,6},{8,9},{11,10},{12,13},{15,14},{16,17},{19,... | collective-permute-start | bytes 3145736 | tf_op jit(solution)/shard_map/ppermute | solution.py:23
  126.6 1.0 add.71
  127.6 0.7 collective-permute-start.8
  128.3 1.4 add_convert_fusion.3
  129.7 0.7 collective-permute-start.36
  130.4 0.8 add.73
  131.3 1.3 collective-permute-start.9
  132.6 2.6 %add_convert_fusion.1 = bf16[1024,512]{1,0:T(8,128)(2,1)} fusion(f32[1024,512]{1,0:T(8,128)S(1)} %copy-done.4, bf16[1024,512]{1,0:T(8,128)(2,1)} %collective-permute-done.38), kind=kLoop, calls=%fused_computation.2 | loop fusion | flops 1572864 | bytes 4194304 | tf_op jit(solution)/shard_map/convert_element_type | solution.py:240
  135.2 1.6 collective-permute-start.39
  136.8 1.0 reshape.37
  137.8 6.7 %collective-permute-done.9 = f32[2,64,512]{2,1,0:T(8,128)} collective-permute-done((f32[2,64,512]{2,1,0:T(8,128)}, f32[2,64,512]{2,1,0:T(8,128)}, u32[]{:S(2)}, u32[]{:S(2)}) %collective-permute-start.9) | collective-permute-done | bytes 262176 | tf_op jit(solution)/shard_map/ppermute | solution.py:23
  144.6 1.6 fusion.1
  146.2 4.5 %bitcast_add_fusion = f32[1024,512]{1,0:T(8,128)S(1)} fusion(f32[2,512,512]{2,1,0:T(8,128)S(1)} %fusion.1, bf16[1024,2048]{1,0:T(8,128)(2,1)} %tok_ref.7, bf16[2048,512]{1,0:T(8,128)(2,1)S(1)} %bitcast.22), kind=kOutput, calls=%fused_computation | convolution fusion | flops 2148007936 | bytes 10485760 | tf_op jit(solution)/shard_map/dot_general | solution.py:233
  150.7 15.5 %collective-permute-done.39 = bf16[1024,512]{1,0:T(8,128)(2,1)} collective-permute-done((bf16[1024,512]{1,0:T(8,128)(2,1)}, bf16[1024,512]{1,0:T(8,128)(2,1)}, u32[]{:S(2)}, u32[]{:S(2)}) %collective-permute-start.39) | collective-permute-done | bytes 1048608 | tf_op jit(solution)/shard_map/ppermute | solution.py:23
  166.2 2.2 %add_convert_fusion = bf16[1024,512]{1,0:T(8,128)(2,1)S(1)} fusion(bf16[1024,512]{1,0:T(8,128)(2,1)} %collective-permute-done.39, bf16[1024,512]{1,0:T(8,128)(2,1)S(1)} %collective-permute-done.36, f32[1024,512]{1,0:T(8,128)S(1)} %bitcast_add_fusion, bf16[1024,512]{1,0:T(8,128)(2,1)} %collective-permute-done.34), kind=kLoop, calls=%fused_computation.1 | loop fusion | flops 3670016 | bytes 6291456 | tf_op jit(solution)/shard_map/convert_element_type | solution.py:246
  168.5 1.1 reshape.42
  (119 shorter events, 3.3 us)
Async XLA Ops:
  0.0 27.7 %copy-start.31 = (s32[2]{0:T(128)S(1)}, s32[2]{0:T(128)}, u32[]{:S(2)}) copy-start(s32[2]{0:T(128)} %refs_0_.1) | copy-start | bytes 28
  0.0 27.8 %copy-start.30 = (bf16[6,64]{1,0:T(8,128)(2,1)S(1)}, bf16[6,64]{1,0:T(8,128)(2,1)}, u32[]{:S(2)}) copy-start(bf16[6,64]{1,0:T(8,128)(2,1)} %param.11) | copy-start | bytes 2308
  0.0 27.8 %copy-start.8 = (bf16[6,64,2,256]{3,2,1,0:T(2,128)(2,1)S(1)}, bf16[6,64,2,256]{3,2,1,0:T(2,128)(2,1)}, u32[]{:S(2)}) copy-start(bf16[6,64,2,256]{3,2,1,0:T(2,128)(2,1)} %param.10) | copy-start | bytes 1179652
  1.7 11.6 %collective-permute-start.3 = (bf16[256,512]{1,0:T(8,128)(2,1)S(1)}, bf16[256,512]{1,0:T(8,128)(2,1)S(1)}, u32[]{:S(2)}, u32[]{:S(2)}) collective-permute-start(bf16[256,512]{1,0:T(8,128)(2,1)S(1)} %bitcast.27), channel_id=1, source_target_pairs={{0,3},{1,2},{2,1},{3,0},{4,7},{5,6},{6,5},{7,4},{8,11},{9,10},{10,... | collective-permute-start | bytes 786440 | tf_op jit(solution)/shard_map/ppermute | solution.py:19
  13.3 33.4 %copy-start.12 = (bf16[256,512]{1,0:T(8,128)(2,1)}, bf16[256,512]{1,0:T(8,128)(2,1)S(1)}, u32[]{:S(2)}) copy-start(bf16[256,512]{1,0:T(8,128)(2,1)S(1)} %collective-permute-done.3.refs_0_) | copy-start | bytes 786436
  13.3 10.2 %collective-permute-start.4 = (bf16[256,512]{1,0:T(8,128)(2,1)S(1)}, bf16[256,512]{1,0:T(8,128)(2,1)S(1)}, u32[]{:S(2)}, u32[]{:S(2)}) collective-permute-start(bf16[256,512]{1,0:T(8,128)(2,1)S(1)} %collective-permute-done.3.refs_0_), channel_id=1, source_target_pairs={{0,24},{4,28},{8,16},{12,20},{16,8},{20,12},{24,0},{28,4},{1,25},{... | collective-permute-start | bytes 786440 | tf_op jit(solution)/shard_map/ppermute | solution.py:19
  15.8 11.4 %collective-permute-start.14 = (bf16[256,512]{1,0:T(8,128)(2,1)S(1)}, bf16[256,512]{1,0:T(8,128)(2,1)S(1)}, u32[]{:S(2)}, u32[]{:S(2)}) collective-permute-start(bf16[256,512]{1,0:T(8,128)(2,1)S(1)} %collective-permute-done.3.refs_0_), channel_id=1, source_target_pairs={{0,8},{4,12},{8,0},{12,4},{16,24},{20,28},{24,16},{28,20},{1,9},{5... | collective-permute-start | bytes 786440 | tf_op jit(solution)/shard_map/ppermute | solution.py:19
  16.3 11.0 %collective-permute-start.15 = (bf16[256,512]{1,0:T(8,128)(2,1)S(1)}, bf16[256,512]{1,0:T(8,128)(2,1)S(1)}, u32[]{:S(2)}, u32[]{:S(2)}) collective-permute-start(bf16[256,512]{1,0:T(8,128)(2,1)S(1)} %collective-permute-done.3.refs_0_), channel_id=1, source_target_pairs={{0,16},{4,20},{8,24},{12,28},{16,0},{20,4},{24,8},{28,12},{1,17},{... | collective-permute-start | bytes 786440 | tf_op jit(solution)/shard_map/ppermute | solution.py:19
  16.8 28.4 %collective-permute-start.16 = (bf16[256,512]{1,0:T(8,128)(2,1)S(1)}, bf16[256,512]{1,0:T(8,128)(2,1)S(1)}, u32[]{:S(2)}, u32[]{:S(2)}) collective-permute-start(bf16[256,512]{1,0:T(8,128)(2,1)S(1)} %collective-permute-done.3.refs_0_), channel_id=1, source_target_pairs={{0,4},{4,0},{8,12},{12,8},{1,5},{5,1},{9,13},{13,9},{2,6},{6,2},{1... | collective-permute-start | bytes 786440 | tf_op jit(solution)/shard_map/ppermute | solution.py:19
  23.5 23.2 %copy-start.13 = (bf16[256,512]{1,0:T(8,128)(2,1)}, bf16[256,512]{1,0:T(8,128)(2,1)S(1)}, u32[]{:S(2)}) copy-start(bf16[256,512]{1,0:T(8,128)(2,1)S(1)} %collective-permute-done.4.refs_3_) | copy-start | bytes 786436
  23.5 23.2 %collective-permute-start.19 = (bf16[256,512]{1,0:T(8,128)(2,1)S(1)}, bf16[256,512]{1,0:T(8,128)(2,1)S(1)}, u32[]{:S(2)}, u32[]{:S(2)}) collective-permute-start(bf16[256,512]{1,0:T(8,128)(2,1)S(1)} %collective-permute-done.4.refs_3_), channel_id=1, source_target_pairs={{0,4},{4,0},{8,12},{12,8},{1,5},{5,1},{9,13},{13,9},{2,6},{6,2},{1... | collective-permute-start | bytes 786440 | tf_op jit(solution)/shard_map/ppermute | solution.py:19
  27.2 19.6 %copy-start.15 = (bf16[256,512]{1,0:T(8,128)(2,1)}, bf16[256,512]{1,0:T(8,128)(2,1)S(1)}, u32[]{:S(2)}) copy-start(bf16[256,512]{1,0:T(8,128)(2,1)S(1)} %collective-permute-done.14.refs_1_) | copy-start | bytes 786436
  27.2 19.5 %collective-permute-start.17 = (bf16[256,512]{1,0:T(8,128)(2,1)S(1)}, bf16[256,512]{1,0:T(8,128)(2,1)S(1)}, u32[]{:S(2)}, u32[]{:S(2)}) collective-permute-start(bf16[256,512]{1,0:T(8,128)(2,1)S(1)} %collective-permute-done.14.refs_1_), channel_id=1, source_target_pairs={{0,4},{4,0},{8,12},{12,8},{1,5},{5,1},{9,13},{13,9},{2,6},{6,2},{1... | collective-permute-start | bytes 786440 | tf_op jit(solution)/shard_map/ppermute | solution.py:19
  27.3 19.5 %copy-start.16 = (bf16[256,512]{1,0:T(8,128)(2,1)}, bf16[256,512]{1,0:T(8,128)(2,1)S(1)}, u32[]{:S(2)}) copy-start(bf16[256,512]{1,0:T(8,128)(2,1)S(1)} %collective-permute-done.15.refs_2_) | copy-start | bytes 786436
  27.3 19.4 %collective-permute-start.18 = (bf16[256,512]{1,0:T(8,128)(2,1)S(1)}, bf16[256,512]{1,0:T(8,128)(2,1)S(1)}, u32[]{:S(2)}, u32[]{:S(2)}) collective-permute-start(bf16[256,512]{1,0:T(8,128)(2,1)S(1)} %collective-permute-done.15.refs_2_), channel_id=1, source_target_pairs={{0,4},{4,0},{8,12},{12,8},{1,5},{5,1},{9,13},{13,9},{2,6},{6,2},{1... | collective-permute-start | bytes 786440 | tf_op jit(solution)/shard_map/ppermute | solution.py:19
  27.7 1.4 collective-permute-start
  29.1 6.5 %copy-start.32 = (s32[2]{0:T(128)}, s32[2]{0:T(128)S(1)}, u32[]{:S(2)}) copy-start(s32[2]{0:T(128)S(1)} %collective-permute-done.refs_1_) | copy-start | bytes 28
  29.1 3.5 %collective-permute-start.1 = (s32[2]{0:T(128)S(1)}, s32[2]{0:T(128)S(1)}, u32[]{:S(2)}, u32[]{:S(2)}) collective-permute-start(s32[2]{0:T(128)S(1)} %copy-done.31), channel_id=1, source_target_pairs={{0,8},{4,12},{8,0},{12,4},{1,9},{5,13},{9,1},{13,5},{2,10},{6,14},... | collective-permute-start | bytes 32 | tf_op jit(solution)/shard_map/ppermute | solution.py:19
  32.6 3.0 %collective-permute-start.2 = (s32[2]{0:T(128)S(1)}, s32[2]{0:T(128)S(1)}, u32[]{:S(2)}, u32[]{:S(2)}) collective-permute-start(s32[2]{0:T(128)S(1)} %copy-done.31), channel_id=1, source_target_pairs={{0,12},{4,8},{8,4},{12,0},{1,13},{5,9},{9,5},{13,1},{2,14},{6,10},... | collective-permute-start | bytes 32 | tf_op jit(solution)/shard_map/ppermute | solution.py:19
  38.9 18.2 %collective-permute-start.12 = (bf16[256,512]{1,0:T(8,128)(2,1)S(1)}, bf16[256,512]{1,0:T(8,128)(2,1)S(1)}, u32[]{:S(2)}, u32[]{:S(2)}) collective-permute-start(bf16[256,512]{1,0:T(8,128)(2,1)S(1)} %bitcast.26), channel_id=1, source_target_pairs={{0,2},{1,3},{2,0},{3,1},{4,6},{5,7},{6,4},{7,5},{8,10},{9,11},{10,... | collective-permute-start | bytes 786440 | tf_op jit(solution)/shard_map/ppermute | solution.py:19
  45.2 23.3 %collective-permute-start.5 = (bf16[2,64,2048]{2,1,0:T(8,128)(2,1)}, bf16[2,64,2048]{2,1,0:T(8,128)(2,1)S(1)}, u32[]{:S(2)}, u32[]{:S(2)}) collective-permute-start(bf16[2,64,2048]{2,1,0:T(8,128)(2,1)} %get-tuple-element.21), channel_id=1, source_target_pairs={{0,8},{4,12},{8,0},{12,4},{1,9},{5,13},{9,1},{13,5},{2,10},{6,14},... | collective-permute-start | bytes 1572872 | tf_op jit(solution)/shard_map/ppermute | solution.py:19
  47.6 10.3 %copy-start.6 = (bf16[2,65,2,256]{3,2,1,0:T(2,128)(2,1)S(1)}, bf16[2,65,2,256]{3,2,1,0:T(2,128)(2,1)}, u32[]{:S(2)}) copy-start(bf16[2,65,2,256]{3,2,1,0:T(2,128)(2,1)} %get-tuple-element.22) | copy-start | bytes 399364
  47.6 12.8 %copy-start.7 = (bf16[2,64,2048]{2,1,0:T(8,128)(2,1)S(1)}, bf16[2,64,2048]{2,1,0:T(8,128)(2,1)}, u32[]{:S(2)}) copy-start(bf16[2,64,2048]{2,1,0:T(8,128)(2,1)} %get-tuple-element.21) | copy-start | bytes 1572868
  54.3 35.1 %collective-permute-start.37 = (bf16[1024,512]{1,0:T(8,128)(2,1)}, bf16[1024,512]{1,0:T(8,128)(2,1)}, u32[]{:S(2)}, u32[]{:S(2)}) collective-permute-start(bf16[1024,512]{1,0:T(8,128)(2,1)} %get-tuple-element.25), channel_id=1, source_target_pairs={{0,1},{3,2},{4,5},{7,6},{8,9},{11,10},{12,13},{15,14},{16,17},{19,... | collective-permute-start | bytes 3145736 | tf_op jit(solution)/shard_map/ppermute | solution.py:23
  57.1 20.4 %copy-start.10 = (bf16[256,512]{1,0:T(8,128)(2,1)}, bf16[256,512]{1,0:T(8,128)(2,1)S(1)}, u32[]{:S(2)}) copy-start(bf16[256,512]{1,0:T(8,128)(2,1)S(1)} %collective-permute-done.12.refs_0_) | copy-start | bytes 786436
  57.1 11.3 %collective-permute-start.20 = (bf16[256,512]{1,0:T(8,128)(2,1)S(1)}, bf16[256,512]{1,0:T(8,128)(2,1)S(1)}, u32[]{:S(2)}, u32[]{:S(2)}) collective-permute-start(bf16[256,512]{1,0:T(8,128)(2,1)S(1)} %collective-permute-done.12.refs_0_), channel_id=1, source_target_pairs={{0,8},{4,12},{8,0},{12,4},{16,24},{20,28},{24,16},{28,20},{1,9},{5... | collective-permute-start | bytes 786440 | tf_op jit(solution)/shard_map/ppermute | solution.py:19
  57.9 9.6 %collective-permute-start.10 = (bf16[2,65,2,256]{3,2,1,0:T(2,128)(2,1)S(1)}, bf16[2,65,2,256]{3,2,1,0:T(2,128)(2,1)S(1)}, u32[]{:S(2)}, u32[]{:S(2)}) collective-permute-start(bf16[2,65,2,256]{3,2,1,0:T(2,128)(2,1)S(1)} %copy-done.6), channel_id=1, source_target_pairs={{0,8},{4,12},{8,0},{12,4},{1,9},{5,13},{9,1},{13,5},{2,10},{6,14},... | collective-permute-start | bytes 399368 | tf_op jit(solution)/shard_map/ppermute | solution.py:19
  59.2 9.8 %collective-permute-start.21 = (bf16[256,512]{1,0:T(8,128)(2,1)S(1)}, bf16[256,512]{1,0:T(8,128)(2,1)S(1)}, u32[]{:S(2)}, u32[]{:S(2)}) collective-permute-start(bf16[256,512]{1,0:T(8,128)(2,1)S(1)} %collective-permute-done.12.refs_0_), channel_id=1, source_target_pairs={{0,16},{4,20},{8,24},{12,28},{16,0},{20,4},{24,8},{28,12},{1,17},{... | collective-permute-start | bytes 786440 | tf_op jit(solution)/shard_map/ppermute | solution.py:19
  67.5 7.6 %collective-permute-start.22 = (bf16[256,512]{1,0:T(8,128)(2,1)S(1)}, bf16[256,512]{1,0:T(8,128)(2,1)}, u32[]{:S(2)}, u32[]{:S(2)}) collective-permute-start(bf16[256,512]{1,0:T(8,128)(2,1)S(1)} %collective-permute-done.12.refs_0_), channel_id=1, source_target_pairs={{0,24},{4,28},{8,16},{12,20},{16,8},{20,12},{24,0},{28,4},{1,25},{... | collective-permute-start | bytes 786440 | tf_op jit(solution)/shard_map/ppermute | solution.py:19
  68.4 6.7 %collective-permute-start.23 = (bf16[256,512]{1,0:T(8,128)(2,1)S(1)}, bf16[256,512]{1,0:T(8,128)(2,1)S(1)}, u32[]{:S(2)}, u32[]{:S(2)}) collective-permute-start(bf16[256,512]{1,0:T(8,128)(2,1)S(1)} %collective-permute-done.12.refs_0_), channel_id=1, source_target_pairs={{0,4},{4,0},{8,12},{12,8},{1,5},{5,1},{9,13},{13,9},{2,6},{6,2},{1... | collective-permute-start | bytes 786440 | tf_op jit(solution)/shard_map/ppermute | solution.py:19
  68.5 9.0 %copy-start.14 = (bf16[256,512]{1,0:T(8,128)(2,1)}, bf16[256,512]{1,0:T(8,128)(2,1)S(1)}, u32[]{:S(2)}) copy-start(bf16[256,512]{1,0:T(8,128)(2,1)S(1)} %collective-permute-done.20.refs_1_) | copy-start | bytes 786436
  68.5 7.2 %collective-permute-start.24 = (bf16[256,512]{1,0:T(8,128)(2,1)S(1)}, bf16[256,512]{1,0:T(8,128)(2,1)S(1)}, u32[]{:S(2)}, u32[]{:S(2)}) collective-permute-start(bf16[256,512]{1,0:T(8,128)(2,1)S(1)} %collective-permute-done.20.refs_1_), channel_id=1, source_target_pairs={{0,4},{4,0},{8,12},{12,8},{1,5},{5,1},{9,13},{13,9},{2,6},{6,2},{1... | collective-permute-start | bytes 786440 | tf_op jit(solution)/shard_map/ppermute | solution.py:19
  69.0 16.0 %copy-start = (bf16[4,64,2048]{2,1,0:T(8,128)(2,1)}, bf16[4,64,2048]{2,1,0:T(8,128)(2,1)S(1)}, u32[]{:S(2)}) copy-start(bf16[4,64,2048]{2,1,0:T(8,128)(2,1)S(1)} %constant_dynamic-update-slice_fusion.mine_ref) | copy-start | bytes 3145732
  69.0 8.5 %copy-start.18 = (bf16[256,512]{1,0:T(8,128)(2,1)}, bf16[256,512]{1,0:T(8,128)(2,1)S(1)}, u32[]{:S(2)}) copy-start(bf16[256,512]{1,0:T(8,128)(2,1)S(1)} %collective-permute-done.21.refs_2_) | copy-start | bytes 786436
  69.0 33.6 %collective-permute-start.6 = (bf16[4,64,2048]{2,1,0:T(8,128)(2,1)S(1)}, bf16[4,64,2048]{2,1,0:T(8,128)(2,1)}, u32[]{:S(2)}, u32[]{:S(2)}) collective-permute-start(bf16[4,64,2048]{2,1,0:T(8,128)(2,1)S(1)} %constant_dynamic-update-slice_fusion.mine_ref), channel_id=1, source_target_pairs={{0,4},{4,0},{8,12},{12,8},{1,5},{5,1},{9,13},{13,9},{2,6},{6,2},{1... | collective-permute-start | bytes 3145736 | tf_op jit(solution)/shard_map/ppermute | solution.py:19
  75.1 1.8 %collective-permute-start.25 = (bf16[256,512]{1,0:T(8,128)(2,1)S(1)}, bf16[256,512]{1,0:T(8,128)(2,1)S(1)}, u32[]{:S(2)}, u32[]{:S(2)}) collective-permute-start(bf16[256,512]{1,0:T(8,128)(2,1)S(1)} %collective-permute-done.21.refs_2_), channel_id=1, source_target_pairs={{0,4},{4,0},{8,12},{12,8},{1,5},{5,1},{9,13},{13,9},{2,6},{6,2},{1... | collective-permute-start | bytes 786440 | tf_op jit(solution)/shard_map/ppermute | solution.py:19
  75.1 2.4 %collective-permute-start.26 = (bf16[256,512]{1,0:T(8,128)(2,1)}, bf16[256,512]{1,0:T(8,128)(2,1)S(1)}, u32[]{:S(2)}, u32[]{:S(2)}) collective-permute-start(bf16[256,512]{1,0:T(8,128)(2,1)} %collective-permute-done.22.refs_3_), channel_id=1, source_target_pairs={{0,4},{4,0},{8,12},{12,8},{1,5},{5,1},{9,13},{13,9},{2,6},{6,2},{1... | collective-permute-start | bytes 786440 | tf_op jit(solution)/shard_map/ppermute | solution.py:19
  76.5 12.4 %collective-permute-start.13 = (bf16[256,512]{1,0:T(8,128)(2,1)}, bf16[256,512]{1,0:T(8,128)(2,1)S(1)}, u32[]{:S(2)}, u32[]{:S(2)}) collective-permute-start(bf16[256,512]{1,0:T(8,128)(2,1)} %bitcast.13), channel_id=1, source_target_pairs={{0,1},{1,0},{2,3},{3,2},{4,5},{5,4},{6,7},{7,6},{8,9},{9,8},{10,11... | collective-permute-start | bytes 786440 | tf_op jit(solution)/shard_map/ppermute | solution.py:19
  76.9 16.7 %collective-permute-start.11 = (bf16[4,65,2,256]{3,2,1,0:T(2,128)(2,1)S(1)}, bf16[4,65,2,256]{3,2,1,0:T(2,128)(2,1)S(1)}, u32[]{:S(2)}, u32[]{:S(2)}) collective-permute-start(bf16[4,65,2,256]{3,2,1,0:T(2,128)(2,1)S(1)} %pad_maximum_fusion), channel_id=1, source_target_pairs={{0,4},{4,0},{8,12},{12,8},{1,5},{5,1},{9,13},{13,9},{2,6},{6,2},{1... | collective-permute-start | bytes 798728 | tf_op jit(solution)/shard_map/ppermute | solution.py:19
  85.0 43.3 %collective-permute-start.35 = (bf16[1024,512]{1,0:T(8,128)(2,1)}, bf16[1024,512]{1,0:T(8,128)(2,1)S(1)}, u32[]{:S(2)}, u32[]{:S(2)}) collective-permute-start(bf16[1024,512]{1,0:T(8,128)(2,1)} %get-tuple-element.27), channel_id=1, source_target_pairs={{0,1},{3,2},{4,5},{7,6},{8,9},{11,10},{12,13},{15,14},{16,17},{19,... | collective-permute-start | bytes 3145736 | tf_op jit(solution)/shard_map/ppermute | solution.py:23
  89.0 13.6 %copy-start.9 = (bf16[256,512]{1,0:T(8,128)(2,1)}, bf16[256,512]{1,0:T(8,128)(2,1)S(1)}, u32[]{:S(2)}) copy-start(bf16[256,512]{1,0:T(8,128)(2,1)S(1)} %collective-permute-done.13.refs_0_) | copy-start | bytes 786436
  89.0 11.4 %collective-permute-start.27 = (bf16[256,512]{1,0:T(8,128)(2,1)S(1)}, bf16[256,512]{1,0:T(8,128)(2,1)S(1)}, u32[]{:S(2)}, u32[]{:S(2)}) collective-permute-start(bf16[256,512]{1,0:T(8,128)(2,1)S(1)} %collective-permute-done.13.refs_0_), channel_id=1, source_target_pairs={{0,8},{4,12},{8,0},{12,4},{16,24},{20,28},{24,16},{28,20},{1,9},{5... | collective-permute-start | bytes 786440 | tf_op jit(solution)/shard_map/ppermute | solution.py:19
  89.3 13.2 %collective-permute-start.28 = (bf16[256,512]{1,0:T(8,128)(2,1)S(1)}, bf16[256,512]{1,0:T(8,128)(2,1)}, u32[]{:S(2)}, u32[]{:S(2)}) collective-permute-start(bf16[256,512]{1,0:T(8,128)(2,1)S(1)} %collective-permute-done.13.refs_0_), channel_id=1, source_target_pairs={{0,16},{4,20},{8,24},{12,28},{16,0},{20,4},{24,8},{28,12},{1,17},{... | collective-permute-start | bytes 786440 | tf_op jit(solution)/shard_map/ppermute | solution.py:19
  93.6 39.0 %collective-permute-start.38 = (bf16[1024,512]{1,0:T(8,128)(2,1)}, bf16[1024,512]{1,0:T(8,128)(2,1)}, u32[]{:S(2)}, u32[]{:S(2)}) collective-permute-start(bf16[1024,512]{1,0:T(8,128)(2,1)} %add_convert_fusion.2), channel_id=1, source_target_pairs={{1,2},{2,1},{5,6},{6,5},{9,10},{10,9},{13,14},{14,13},{17,18},{18,... | collective-permute-start | bytes 3145736 | tf_op jit(solution)/shard_map/ppermute | solution.py:23
  98.5 4.6 %copy-start.29 = (s32[2]{0:T(128)S(1)}, s32[2]{0:T(128)}, u32[]{:S(2)}) copy-start(s32[2]{0:T(128)} %get-tuple-element.19.pick_ref) | copy-start | bytes 28
  100.3 12.0 %copy-start.11 = (bf16[256,512]{1,0:T(8,128)(2,1)}, bf16[256,512]{1,0:T(8,128)(2,1)S(1)}, u32[]{:S(2)}) copy-start(bf16[256,512]{1,0:T(8,128)(2,1)S(1)} %collective-permute-done.27.refs_1_) | copy-start | bytes 786436
  100.4 12.0 %collective-permute-start.29 = (bf16[256,512]{1,0:T(8,128)(2,1)S(1)}, bf16[256,512]{1,0:T(8,128)(2,1)}, u32[]{:S(2)}, u32[]{:S(2)}) collective-permute-start(bf16[256,512]{1,0:T(8,128)(2,1)S(1)} %collective-permute-done.13.refs_0_), channel_id=1, source_target_pairs={{0,24},{4,28},{8,16},{12,20},{16,8},{20,12},{24,0},{28,4},{1,25},{... | collective-permute-start | bytes 786440 | tf_op jit(solution)/shard_map/ppermute | solution.py:19
  102.6 9.9 %collective-permute-start.30 = (bf16[256,512]{1,0:T(8,128)(2,1)S(1)}, bf16[256,512]{1,0:T(8,128)(2,1)S(1)}, u32[]{:S(2)}, u32[]{:S(2)}) collective-permute-start(bf16[256,512]{1,0:T(8,128)(2,1)S(1)} %collective-permute-done.13.refs_0_), channel_id=1, source_target_pairs={{0,4},{4,0},{8,12},{12,8},{1,5},{5,1},{9,13},{13,9},{2,6},{6,2},{1... | collective-permute-start | bytes 786440 | tf_op jit(solution)/shard_map/ppermute | solution.py:19
  102.6 10.4 %collective-permute-start.31 = (bf16[256,512]{1,0:T(8,128)(2,1)S(1)}, bf16[256,512]{1,0:T(8,128)(2,1)S(1)}, u32[]{:S(2)}, u32[]{:S(2)}) collective-permute-start(bf16[256,512]{1,0:T(8,128)(2,1)S(1)} %collective-permute-done.27.refs_1_), channel_id=1, source_target_pairs={{0,4},{4,0},{8,12},{12,8},{1,5},{5,1},{9,13},{13,9},{2,6},{6,2},{1... | collective-permute-start | bytes 786440 | tf_op jit(solution)/shard_map/ppermute | solution.py:19
  112.4 4.6 %collective-permute-start.32 = (bf16[256,512]{1,0:T(8,128)(2,1)}, bf16[256,512]{1,0:T(8,128)(2,1)S(1)}, u32[]{:S(2)}, u32[]{:S(2)}) collective-permute-start(bf16[256,512]{1,0:T(8,128)(2,1)} %collective-permute-done.28.refs_2_), channel_id=1, source_target_pairs={{0,4},{4,0},{8,12},{12,8},{1,5},{5,1},{9,13},{13,9},{2,6},{6,2},{1... | collective-permute-start | bytes 786440 | tf_op jit(solution)/shard_map/ppermute | solution.py:19
  112.5 3.2 %copy-start.19 = (bf16[256,512]{1,0:T(8,128)(2,1)}, bf16[256,512]{1,0:T(8,128)(2,1)S(1)}, u32[]{:S(2)}) copy-start(bf16[256,512]{1,0:T(8,128)(2,1)S(1)} %collective-permute-done.30.refs_4_) | copy-start | bytes 786436
  112.5 4.4 %collective-permute-start.33 = (bf16[256,512]{1,0:T(8,128)(2,1)}, bf16[256,512]{1,0:T(8,128)(2,1)}, u32[]{:S(2)}, u32[]{:S(2)}) collective-permute-start(bf16[256,512]{1,0:T(8,128)(2,1)} %collective-permute-done.29.refs_3_), channel_id=1, source_target_pairs={{0,4},{4,0},{8,12},{12,8},{1,5},{5,1},{9,13},{13,9},{2,6},{6,2},{1... | collective-permute-start | bytes 786440 | tf_op jit(solution)/shard_map/ppermute | solution.py:19
  113.0 4.0 %copy-start.21 = (bf16[256,512]{1,0:T(8,128)(2,1)}, bf16[256,512]{1,0:T(8,128)(2,1)S(1)}, u32[]{:S(2)}) copy-start(bf16[256,512]{1,0:T(8,128)(2,1)S(1)} %collective-permute-done.31.refs_5_) | copy-start | bytes 786436
  113.0 13.6 %collective-permute-start.7 = (f32[2,64,512]{2,1,0:T(8,128)}, f32[2,64,512]{2,1,0:T(8,128)}, u32[]{:S(2)}, u32[]{:S(2)}) collective-permute-start(f32[2,64,512]{2,1,0:T(8,128)} %coefficients.1), channel_id=1, source_target_pairs={{0,1},{3,2},{4,5},{7,6},{8,9},{11,10},{12,13},{15,14},{16,17},{19,... | collective-permute-start | bytes 786440 | tf_op jit(solution)/shard_map/ppermute | solution.py:23
  116.9 9.7 %copy-start.1 = (f32[2,64,512]{2,1,0:T(8,128)S(1)}, f32[2,64,512]{2,1,0:T(8,128)}, u32[]{:S(2)}) copy-start(f32[2,64,512]{2,1,0:T(8,128)} %coefficients.1) | copy-start | bytes 786436
  116.9 11.4 %copy-start.2 = (f32[1024,512]{1,0:T(8,128)S(1)}, f32[1024,512]{1,0:T(8,128)}, u32[]{:S(2)}) copy-start(f32[1024,512]{1,0:T(8,128)} %get-tuple-element.30) | copy-start | bytes 6291460
  124.3 26.4 %collective-permute-start.34 = (bf16[1024,512]{1,0:T(8,128)(2,1)}, bf16[1024,512]{1,0:T(8,128)(2,1)}, u32[]{:S(2)}, u32[]{:S(2)}) collective-permute-start(bf16[1024,512]{1,0:T(8,128)(2,1)} %get-tuple-element.29), channel_id=1, source_target_pairs={{0,1},{3,2},{4,5},{7,6},{8,9},{11,10},{12,13},{15,14},{16,17},{19,... | collective-permute-start | bytes 3145736 | tf_op jit(solution)/shard_map/ppermute | solution.py:23
  127.6 2.8 %collective-permute-start.8 = (f32[2,64,512]{2,1,0:T(8,128)S(1)}, f32[2,64,512]{2,1,0:T(8,128)S(1)}, u32[]{:S(2)}, u32[]{:S(2)}) collective-permute-start(f32[2,64,512]{2,1,0:T(8,128)S(1)} %add.71), channel_id=1, source_target_pairs={{1,2},{2,1},{5,6},{6,5},{9,10},{10,9},{13,14},{14,13},{17,18},{18,... | collective-permute-start | bytes 786440 | tf_op jit(solution)/shard_map/ppermute | solution.py:23
  128.3 4.2 %copy-start.4 = (f32[1024,512]{1,0:T(8,128)S(1)}, f32[1024,512]{1,0:T(8,128)}, u32[]{:S(2)}) copy-start(f32[1024,512]{1,0:T(8,128)} %get-tuple-element.31) | copy-start | bytes 6291460
  129.7 21.0 %collective-permute-start.36 = (bf16[1024,512]{1,0:T(8,128)(2,1)}, bf16[1024,512]{1,0:T(8,128)(2,1)S(1)}, u32[]{:S(2)}, u32[]{:S(2)}) collective-permute-start(bf16[1024,512]{1,0:T(8,128)(2,1)} %add_convert_fusion.3), channel_id=1, source_target_pairs={{1,2},{2,1},{5,6},{6,5},{9,10},{10,9},{13,14},{14,13},{17,18},{18,... | collective-permute-start | bytes 3145736 | tf_op jit(solution)/shard_map/ppermute | solution.py:23
  130.4 4.8 %copy-start.5 = (f32[2,64,512]{2,1,0:T(8,128)}, f32[2,64,512]{2,1,0:T(8,128)S(1)}, u32[]{:S(2)}) copy-start(f32[2,64,512]{2,1,0:T(8,128)S(1)} %collective-permute-done.8) | copy-start | bytes 786436
  131.3 13.3 %collective-permute-start.9 = (f32[2,64,512]{2,1,0:T(8,128)}, f32[2,64,512]{2,1,0:T(8,128)}, u32[]{:S(2)}, u32[]{:S(2)}) collective-permute-start(f32[2,64,512]{2,1,0:T(8,128)} %add.73), channel_id=1, source_target_pairs={{2,3},{1,0},{6,7},{5,4},{10,11},{9,8},{14,15},{13,12},{18,19},{17,... | collective-permute-start | bytes 786440 | tf_op jit(solution)/shard_map/ppermute | solution.py:23
  135.2 11.0 %copy-start.3 = (bf16[256,8,2,256]{3,1,2,0:T(8,128)(2,1)S(1)}, bf16[256,8,2,256]{3,1,2,0:T(8,128)(2,1)}, u32[]{:S(2)}) copy-start(bf16[256,8,2,256]{3,1,2,0:T(8,128)(2,1)} %copy.12) | copy-start | bytes 6291460
  135.2 31.0 %collective-permute-start.39 = (bf16[1024,512]{1,0:T(8,128)(2,1)}, bf16[1024,512]{1,0:T(8,128)(2,1)}, u32[]{:S(2)}, u32[]{:S(2)}) collective-permute-start(bf16[1024,512]{1,0:T(8,128)(2,1)} %add_convert_fusion.1), channel_id=1, source_target_pairs={{2,3},{1,0},{6,7},{5,4},{10,11},{9,8},{14,15},{13,12},{18,19},{17,... | collective-permute-start | bytes 3145736 | tf_op jit(solution)/shard_map/ppermute | solution.py:23
  (11 other events, 11.1 us)

commit v3 on v2

--- a/solution.py
+++ b/solution.py
@@ -13,6 +13,7 @@
 I32 = jnp.int32
 VMEM_LIMIT = 60 * 1024 * 1024
 SMALL = pl.CostEstimate(flops=1, bytes_accessed=1, transcendentals=0)
+LARGE = pl.CostEstimate(flops=20_000_000_000, bytes_accessed=1, transcendentals=0)
 
 
 def swap(value, axis, size, mask):
@@ -23,51 +24,140 @@
     return lax.ppermute(value, "mp", [(at, at + 1), (n - 1 - at, n - 2 - at)])
 
 
+def stages(n):
+    if n == 4:
+        return [(3, 0, 3, 0), (2, 3, 0, 1), (1, 2, 1, 2)]
+    return [tuple(m ^ k for m in range(n)) for k in range(n - 1, 0, -1)]
+
+
+def rounds(targets):
+    left, out = [(source, m) for m, source in enumerate(targets)], []
+    while left:
+        now, rest = {}, []
+        for source, m in left:
+            if source in now or (len(targets) == 4 and (source ^ m) != (left[0][0] ^ left[0][1])):
+                rest.append((source, m))
+            else:
+                now[source] = m
+        out.append(list(now.items()))
+        left = rest
+    return out
+
+
 def tied(value, *others):
     return lax.optimization_barrier((value, *others))[0]
 
 
-def partial_kernel(masks, share_ref, tok_ref, *refs):
-    pieces = refs[: len(masks)]
-    low_ref, full_ref, weight = refs[len(masks) :]
-    rows = weight.shape[0] // len(masks)
-
-    @pl.when(pl.program_id(0) == 0)
-    def _():
-        for mask, piece in zip(masks, pieces):
-            to = pl.multiple_of((share_ref[0] ^ mask) * rows, rows)
-            weight[pl.ds(to, rows), :] = piece[...]
-
-    product = jnp.dot(tok_ref[...], weight[...], preferred_element_type=F32)
-    full_ref[...] = product
-    low_ref[...] = product.astype(low_ref.dtype)
-
-
-def partial_product(share, tokens, pieces, low_type):
+def gate(values, *others):
+    kept = lax.optimization_barrier((*values.values(), *others))
+    return dict(zip(values, kept))
+
+
+def step_kernel(masks, arrivals, earlier, place_ref, tok_ref, *refs):
+    count = len(masks)
+    pieces, refs = refs[:count], refs[count:]
+    extra, refs = refs[: arrivals + earlier], refs[arrivals + earlier :]
+    *out_refs, weight, token, total, held, sems, held_sems = refs
+    rows = weight.shape[1]
+    copies = []
+    for at, mask in enumerate(masks):
+        here = pl.ds(pl.multiple_of((place_ref[0] ^ mask) * rows, rows), rows)
+        copies.append(
+            (
+                pltpu.make_async_copy(pieces[at], weight.at[at], sems.at[0, at]),
+                pltpu.make_async_copy(tok_ref.at[:, here], token.at[at], sems.at[1, at]),
+            )
+        )
+    late = [
+        pltpu.make_async_copy(ref, held.at[at], held_sems.at[at]) for at, ref in enumerate(extra)
+    ]
+    for pair in copies:
+        for copy in pair:
+            copy.start()
+    for copy in late:
+        copy.start()
+    for at, pair in enumerate(copies):
+        for copy in pair:
+            copy.wait()
+        product = jnp.dot(token[at], weight[at], preferred_element_type=F32)
+        if at:
+            product = total[...] + product
+        if at < count - 1 or late:
+            total[...] = product
+        else:
+            out_refs[0][...] = product.astype(out_refs[0].dtype)
+    for copy in late:
+        copy.wait()
+    if late:
+        finish(arrivals, earlier, place_ref, total, held, out_refs)
+
+
+def finish(arrivals, earlier, place_ref, total, held, out_refs):
+    for at, ref in enumerate(out_refs):
+
+        def put(mine, ref=ref, at=at):
+            ref[...] = (mine[...].astype(F32) + held[at].astype(F32)).astype(ref.dtype)
+
+        if earlier:
+            pl.when(place_ref[1 + at] == 1)(lambda put=put: put(held.at[arrivals]))
+            pl.when(place_ref[1 + at] != 1)(lambda put=put: put(total))
+        else:
+            put(total)
+
+
+def thin_kernel(masks, arrivals, earlier, place_ref, tok_ref, *refs):
+    pieces, refs = refs[: len(masks)], refs[len(masks) :]
+    extra, refs = refs[: arrivals + earlier], refs[arrivals + earlier :]
+    *out_refs, weight, total, held, held_sems = refs
+    rows = pieces[0].shape[0]
+    late = [
+        pltpu.make_async_copy(ref, held.at[at], held_sems.at[at]) for at, ref in enumerate(extra)
+    ]
+    for copy in late:
+        copy.start()
+    for mask, piece in zip(masks, pieces):
+        to = pl.multiple_of((place_ref[0] ^ mask) * rows, rows)
+        weight[pl.ds(to, rows), :] = piece[...]
+    total[...] = jnp.dot(tok_ref[...], weight[...], preferred_element_type=F32)
+    for copy in late:
+        copy.wait()
+    if late:
+        finish(arrivals, earlier, place_ref, total, held, out_refs)
+    else:
+        out_refs[0][...] = total[...].astype(out_refs[0].dtype)
+
+
+def step(place, tokens, pieces, arrivals, earlier, outs, out_type, cost):
     tok_dev, depth = tokens.shape
     masks, pieces = tuple(pieces), tuple(pieces.values())
-    cols = pieces[0].shape[1]
-    tile = min(256, tok_dev)
-    whole = lambda i, s: (0, 0)
-    row = lambda i, s: (i, 0)
+    rows, cols = pieces[0].shape
+    count = len(pieces)
+    extra = len(arrivals) + len(earlier)
+    vmem = pl.BlockSpec(memory_space=pltpu.VMEM)
+    far = pl.BlockSpec(memory_space=pl.ANY)
+    held = [pltpu.VMEM((max(extra, 1), tok_dev, cols), out_type)]
+    total = [pltpu.VMEM((tok_dev, cols), F32)]
+    held_sems = [pltpu.SemaphoreType.DMA((max(extra, 1),))]
+    if rows % 128:
+        kernel, where = thin_kernel, vmem
+        scratch = [pltpu.VMEM((depth, cols), BF16)] + total + held + held_sems
+    else:
+        kernel, where = step_kernel, far
+        scratch = [
+            pltpu.VMEM((count, rows, cols), BF16),
+            pltpu.VMEM((count, tok_dev, rows), BF16),
+        ]
+        scratch += total + held + [pltpu.SemaphoreType.DMA((2, count))] + held_sems
     return pl.pallas_call(
-        functools.partial(partial_kernel, masks),
-        out_shape=(
-            jax.ShapeDtypeStruct((tok_dev, cols), low_type),
-            jax.ShapeDtypeStruct((tok_dev, cols), F32),
-        ),
-        grid_spec=pltpu.PrefetchScalarGridSpec(
-            num_scalar_prefetch=1,
-            grid=(tok_dev // tile,),
-            in_specs=[pl.BlockSpec((tile, depth), row)]
-            + [pl.BlockSpec(piece.shape, whole) for piece in pieces],
-            out_specs=(pl.BlockSpec((tile, cols), row), pl.BlockSpec((tile, cols), row)),
-            scratch_shapes=[pltpu.VMEM((depth, cols), BF16)],
-        ),
+        functools.partial(kernel, masks, len(arrivals), len(earlier)),
+        out_shape=[jax.ShapeDtypeStruct((tok_dev, cols), out_type)] * outs,
+        in_specs=[pl.BlockSpec(memory_space=pltpu.SMEM)] + [where] * (1 + count) + [far] * extra,
+        out_specs=[vmem] * outs,
+        scratch_shapes=scratch,
         compiler_params=pltpu.CompilerParams(vmem_limit_bytes=VMEM_LIMIT),
-        cost_estimate=SMALL,
-        name="partial_product",
-    )(share, tokens, *pieces)
+        cost_estimate=cost,
+        name="walk_step",
+    )(place, tokens, *pieces, *arrivals, *earlier)
 
 
 def pack_kernel(n_owner, ten_dev, resp_dev, owner_ref, map_ref, *refs):
@@ -122,7 +212,7 @@
         out_specs=(vmem, vmem, smem),
         scratch_shapes=[pltpu.SemaphoreType.DMA((2 * CAPO,))],
         compiler_params=pltpu.CompilerParams(vmem_limit_bytes=VMEM_LIMIT),
-        cost_estimate=SMALL,
+        cost_estimate=LARGE,
         name="pack_named",
     )(owner, owner_map, *asked, delta_in, out_rows)
 
@@ -175,51 +265,123 @@
     share = me_share.astype(I32).reshape(1)
     hop_type = BF16 if n <= 4 else F32
 
-    def sent(k):
-        row = (me_mp ^ k) * d_shard + me_share * share_rows
+    def part_for(pairs):
+        to = sum(jnp.where(me_mp == source, target, 0) for source, target in pairs)
+        row = to * d_shard + me_share * share_rows
         return lax.dynamic_slice_in_dim(kv_weight, row, share_rows, 0).reshape(share_rows, cols)
 
-    def shared(arrived):
+    def arrival(targets, *waits):
+        return sum(
+            lax.ppermute(tied(part_for(pairs), *waits), "mp", pairs) for pairs in rounds(targets)
+        )
+
+    def crossed(arrived):
         pieces = {0: arrived}
         for mask in range(2, plane, 2):
             pieces[mask] = swap(arrived, ("group", "tenant"), plane, mask)
+        return pieces
+
+    def paired(pieces):
+        pieces = dict(pieces)
         for mask in range(0, plane, 2):
             pieces[mask | 1] = swap(pieces[mask], "tenant", n_owner, 1)
         return pieces
 
-    order = list(range(n - 1, 0, -1))
-    low, full, before = {}, {}, []
-    last = None
-    for k in order:
-        block = sent(k) if last is None else tied(sent(k), last)
-        last = swap(block, "mp", n, k)
-        here = tied(last, low[k + 1]) if k + 1 in low else last
-        pieces = shared(here)
-        before.append(pieces[plane - 2])
-        low[k], full[k] = partial_product(share, tokens, pieces, hop_type)
-
+    plan = stages(n)
+    firsts = [part_for(pairs) for pairs in rounds(plan[0])]
     asked = [resp_tenant] + [swap(resp_tenant, "tenant", n_owner, m) for m in range(1, n_owner)]
     pad = ((0, 0), (0, 0), (0, 1), (0, head_cols - rank))
     out_rows = jnp.concatenate([delta_out, jnp.pad(delta_scale[:, None, None, :], pad)], axis=1)
+    arrived = {
+        0: sum(lax.ppermute(part, "mp", pairs) for part, pairs in zip(firsts, rounds(plan[0])))
+    }
+    arrived[0], *asked = lax.optimization_barrier((arrived[0], *asked))
     packed_in, packed_out, pick = pack(
         me_owner.astype(I32).reshape(1), owner_map, asked, delta_in, out_rows
     )
-
-    def spread(packed):
-        mine = jnp.concatenate(
+    even = {0: crossed(arrived[0])}
+    arrived[1] = arrival(plan[1], arrived[0])
+    own = lax.dynamic_slice_in_dim(kv_weight, me_mp * d_shard, d_shard, 0).reshape(d_shard, cols)
+    base = jnp.dot(tokens, own, preferred_element_type=F32)
+    kept = lax.optimization_barrier((*even[0].values(), arrived[1], packed_in, base))
+    even[0], (arrived[1], packed_in, base) = dict(zip(even[0], kept)), kept[-3:]
+
+    def gathered(packed):
+        return jnp.concatenate(
             [packed] + [swap(packed, "tenant", n_owner, m) for m in range(2, n_owner, 2)], axis=0
         )
-        return mine, swap(mine, "tenant", n_owner, 1)
-
-    packed_in = tied(packed_in, before[0])
-    part_coeff = coefficients(pick, tokens, *spread(packed_in), resp_len)
-    coeff, came = part_coeff, None
-    for h in range(n - 1):
-        came = hop(part_coeff if came is None else part_coeff + came, n, h)
-        coeff = coeff + came
-    all_out = jnp.concatenate(spread(packed_out), axis=0)
+
+    def needed(m, t):
+        return next(at for at, to in enumerate(plan) if to[m] == m + n - t)
+
+    low, moved, ready, sent_on = {}, [], [], []
+    for t in range(1, n):
+        new = t - 1
+        if t == 1:
+            pieces = gate(paired(even[0]))
+        else:
+            even[new] = crossed(tied(arrived[new], *ready))
+            if t == 2:
+                packed_in = tied(packed_in, *even[new].values())
+                packed_out = tied(packed_out, *even[new].values())
+            pieces = gate(paired(gate(even[new], *sent_on)))
+        ready = [*pieces.values()]
+        if t + 1 < len(plan):
+            arrived[t + 1] = arrival(plan[t + 1], arrived[t])
+        right = {m: needed(m, t) for m in range(t)}
+        left = {n - 1 - m: at for m, at in right.items()}
+        uses = [{**right, **left}] if 2 * t <= n else [right, left]
+        others = {at for use in uses for at in use.values()} - {new}
+        again = any(needed(m, later) == new for later in range(t + 1, n) for m in range(later))
+        fused = t == 1 or (len(others) <= 1 and not again)
+
+        def holds(use, at):
+            hits = [me_mp == m for m, value in use.items() if value == at]
+            return functools.reduce(jnp.logical_or, hits, jnp.zeros((), bool))
+
+        earlier = [low[at] for at in others] if fused else []
+        flags = [holds(use, *others) if earlier else jnp.zeros((), bool) for use in uses]
+        spot = jnp.stack([me_share.astype(I32)] + [flag.astype(I32) for flag in flags])
+        if fused:
+            sent_on = step(
+                tied(spot, *moved), tokens, pieces, moved, earlier, len(uses), hop_type,
+                SMALL if new else LARGE,
+            )
+            low[new] = sent_on[0]
+        else:
+            low[new] = step(spot, tokens, pieces, [], [], 1, hop_type, SMALL)[0]
+            sent_on = []
+            for use, other in zip(uses, moved):
+                value = low[new]
+                for at in set(use.values()) - {new}:
+                    value = jnp.where(holds(use, at), low[at], value)
+                sent_on.append(value + other)
+        rights = [(m, m + 1) for m in range(t)]
+        lefts = [(n - 1 - m, n - 2 - m) for m in range(t)]
+        if 2 * t < n:
+            moved = [lax.ppermute(sent_on[0], "mp", rights + lefts)]
+        else:
+            moved = [lax.ppermute(sent_on[0], "mp", rights), lax.ppermute(sent_on[-1], "mp", lefts)]
+    came = moved
+    factors, outs = gathered(packed_in), gathered(packed_out)
+    part_coeff = coefficients(
+        pick, tokens, factors, swap(factors, "tenant", n_owner, 1), resp_len
+    )
+    part_coeff = tied(part_coeff, low[min(1, n - 2)])
+    if n <= 4:
+        sent_coeff = part_coeff.astype(hop_type)
+        coeff = part_coeff
+        for k in range(n - 1, 0, -1):
+            coeff = coeff + swap(sent_coeff, "mp", n, k).astype(F32)
+    else:
+        coeff, mask = part_coeff, 1
+        while mask < n:
+            coeff = coeff + swap(coeff, "mp", n, mask)
+            mask *= 2
+    outs, later_pick = lax.optimization_barrier((outs, pick, part_coeff))[:2]
+    all_out = jnp.concatenate((outs, swap(outs, "tenant", n_owner, 1)), axis=0)
     chosen = jnp.stack(
-        [lax.dynamic_index_in_dim(all_out, pick[r], 0, keepdims=False) for r in range(resp_dev)]
+        [lax.dynamic_index_in_dim(all_out, later_pick[r], 0, keepdims=False) for r in range(resp_dev)]
     )
     scale = chosen[:, rank, 0, :rank].astype(F32)
     lowrank = (coeff * scale[:, :, None]).astype(BF16)
@@ -229,18 +391,8 @@
         chosen[:, :rank].reshape(resp_dev, rank, cols),
         preferred_element_type=F32,
     ).reshape(tok_dev, cols)
-    own = lax.dynamic_slice_in_dim(kv_weight, me_mp * d_shard, d_shard, 0).reshape(d_shard, cols)
-    base = jnp.dot(tokens, own, preferred_element_type=F32) + delta
-
-    came = []
-    for s in range(1, n):
-        now = []
-        for h in range(s):
-            k = h ^ (h + n - s)
-            load = low[k] if h == 0 else (full[k] + came[h - 1].astype(F32)).astype(hop_type)
-            now.append(hop(load, n, h))
-        came = now
-    total = lax.optimization_barrier(base)
+
+    total = base + delta
     for value in came:
         total = total + value.astype(F32)
     return total.astype(BF16).reshape(tok_dev, 2, head_cols)

time: 170 us -> 162 us (0.953)
  starting transfers between devices: 46.3 us -> 52.6 us
  other arithmetic: 13.6 us -> 8.06 us
  waiting for transfers between devices: 56.8 us -> 52.2 us
  matrix products: 6.12 us -> 3.87 us
  Pallas kernels: 27.3 us -> 25.1 us
    ppermute x9 -> x10, starting transfers between devices: 17.2 us -> 27.2 us  [the longest x2 10.7 us: shards(): lax.ppermute(sent_on[0], 'mp', rights)]
    ppermute x9 -> x10, waiting for transfers between devices: 22.3 us -> 15.8 us  [the longest x3 9.84 us: arrival(): lax.ppermute(tied(part_for(pairs), *waits), 'mp', pairs)]
    convert_element_type x3 -> x1, other arithmetic: 7.28 us -> 0.97 us  [shards(): sent_coeff = part_coeff.astype(hop_type)]
    ppermute x31, starting transfers between devices: 29.1 us -> 25.4 us  [swap(): return lax.ppermute(value, axis, [(i, i ^ mask) for i in range(size)])]
    pallas_call x3, Pallas kernels: 20 us -> 17.7 us  [step(): pl.pallas_call(functools.partial(kernel, masks, len(arrivals), len(earlie...]
    dot_general x1, matrix products: 4.52 us -> 2.32 us  [shards(): base = jnp.dot(tokens, own, preferred_element_type=F32)]
    concatenate x2, local copies, waits for them, and re-layouts: 0.26 us -> 2.24 us  [the longest x1 1.16 us: shards(): all_out = jnp.concatenate((outs, swap(outs, 'tenant', n_owner, 1)), axis=0)]
    ppermute x31, waiting for transfers between devices: 34.5 us -> 36.4 us  [swap(): return lax.ppermute(value, axis, [(i, i ^ mask) for i in range(size)])]
  transfers between devices with their start and end apart: 40 -> 41, of which waited for: 12 -> 16; matrix products, arithmetic and copies ran while one was open for 15% -> 12% of each run, Pallas kernels for 16% -> 12%
where the time goes in v3:
time: 162 us
  starting transfers between devices  52.6 us (32%)
  waiting for transfers between devices  52.2 us (32%)
  Pallas kernels  25.1 us (15%)
  local copies, waits for them, and re-layouts  15.7 us (10%)
  other arithmetic  8.06 us (5%)
  between operations  4.16 us (3%)
  matrix products  3.87 us (2%)
    ppermute x31, waiting for transfers between devices, swap(): return lax.ppermute(value, axis, [(i, i ^ mask) for i in range(size)])  36.4 us
    ppermute x31, starting transfers between devices, swap(): return lax.ppermute(value, axis, [(i, i ^ mask) for i in range(size)])  25.4 us
    pallas_call x3, Pallas kernels, step(): pl.pallas_call(functools.partial(kernel, masks, len(arrivals), len(earlie...  17.7 us
    ppermute x2, starting transfers between devices, shards(): lax.ppermute(sent_on[0], 'mp', rights)  10.7 us
    ppermute x3, waiting for transfers between devices, arrival(): lax.ppermute(tied(part_for(pairs), *waits), 'mp', pairs)  9.84 us
    ppermute x2, starting transfers between devices, shards(): lax.ppermute(part, 'mp', pairs)  8.12 us
    unnamed x68, local copies, waits for them, and re-layouts  6.17 us
    ppermute x2, waiting for transfers between devices, shards(): lax.ppermute(sent_on[0], 'mp', rights)  4.83 us
  transfers between devices with their start and end apart: 41, of which 16 were waited for; matrix products, arithmetic and copies ran while one was open for 12% of the time, Pallas kernels for 12%

profile of v3, /device:TPU:0, one launch (start us, length us, event | category | flops | bytes accessed | tf_op | source)
XLA Modules:
  0.0 161.7 jit_solution(7855468979653988060)
XLA Ops:
  0.0 2.9 %collective-permute-start.3 = (s32[2]{0:T(128)}, s32[2]{0:T(128)S(1)}, u32[]{:S(2)}, u32[]{:S(2)}) collective-permute-start(s32[2]{0:T(128)} %refs_0_), channel_id=1, source_target_pairs={{0,8},{4,12},{8,0},{12,4},{1,9},{5,13},{9,1},{13,5},{2,10},{6,14},... | collective-permute-start | bytes 32 | tf_op jit(solution)/shard_map/ppermute | solution.py:20
  3.1 2.2 %constant_dynamic-slice_fusion = (bf16[256,2,256]{2,1,0:T(2,128)(2,1)S(1)}, bf16[256,2,256]{2,1,0:T(2,128)(2,1)S(1)}, bf16[256,2,256]{2,1,0:T(2,128)(2,1)S(1)}, ...) fusion(bf16[8192,2,256]{2,1,0:T(2,128)(2,1)} %param.8, s32[]{:T(128)S(6)} %select_n.72, s32[]{:T(128)S(6)} %select_n.64, ...), kind=kLoop, calls=%fused_computation.16 | loop fusion | bytes 2621460 | tf_op jit(solution)/shard_map/dynamic_slice | solution.py:271
  5.3 6.1 %collective-permute-start = (bf16[256,512]{1,0:T(8,128)(2,1)S(1)}, bf16[256,512]{1,0:T(8,128)(2,1)S(1)}, u32[]{:S(2)}, u32[]{:S(2)}) collective-permute-start(bf16[256,512]{1,0:T(8,128)(2,1)S(1)} %bitcast.42), channel_id=1, source_target_pairs={{3,0},{0,3},{7,4},{4,7},{11,8},{8,11},{15,12},{12,15},{19,16},{16,... | collective-permute-start | bytes 786440 | tf_op jit(solution)/shard_map/ppermute | solution.py:296
  11.4 0.7 copy.13
  12.1 2.0 %collective-permute-start.1 = (bf16[256,512]{1,0:T(8,128)(2,1)}, bf16[256,512]{1,0:T(8,128)(2,1)}, u32[]{:S(2)}, u32[]{:S(2)}) collective-permute-start(bf16[256,512]{1,0:T(8,128)(2,1)} %bitcast.13), channel_id=1, source_target_pairs={{0,1},{3,2},{4,5},{7,6},{8,9},{11,10},{12,13},{15,14},{16,17},{19,... | collective-permute-start | bytes 786440 | tf_op jit(solution)/shard_map/ppermute | solution.py:296
  14.1 3.2 %constant_dynamic-slice_fusion.4 = bf16[2048,2,256]{2,1,0:T(2,128)(2,1)S(1)} fusion(bf16[8192,2,256]{2,1,0:T(2,128)(2,1)} %param.8, s32[]{:T(128)S(6)} %select_n.65), kind=kLoop, calls=%fused_computation.20 | loop fusion | bytes 4194308 | tf_op jit(solution)/shard_map/dynamic_slice | solution.py:304
  17.8 1.7 %copy-done = bf16[1024,2048]{1,0:T(8,128)(2,1)S(1)} copy-done((bf16[1024,2048]{1,0:T(8,128)(2,1)S(1)}, bf16[1024,2048]{1,0:T(8,128)(2,1)}, u32[]{:S(2)}) %copy-start) | copy-done | bytes 4194328
  19.6 2.3 %convolution_bitcast_fusion = f32[1024,512]{1,0:T(8,128)S(1)} fusion(bf16[1024,2048]{1,0:T(8,128)(2,1)S(1)} %copy-done, bf16[2048,512]{1,0:T(8,128)(2,1)S(1)} %bitcast.34), kind=kOutput, calls=%fused_computation.4 | convolution fusion | flops 2147483648 | bytes 8388608 | tf_op jit(solution)/shard_map/dot_general | solution.py:305
  22.0 1.1 fusion.3.refs_5_
  23.1 1.0 add.90.refs_0_
  24.2 2.4 %collective-permute-start.7 = (bf16[256,512]{1,0:T(8,128)(2,1)S(1)}, bf16[256,512]{1,0:T(8,128)(2,1)S(1)}, u32[]{:S(2)}, u32[]{:S(2)}) collective-permute-start(bf16[256,512]{1,0:T(8,128)(2,1)S(1)} %add.90.refs_0_), channel_id=1, source_target_pairs={{0,24},{4,28},{8,16},{12,20},{16,8},{20,12},{24,0},{28,4},{1,25},{... | collective-permute-start | bytes 786440 | tf_op jit(solution)/shard_map/ppermute | solution.py:20
  26.6 0.5 collective-permute-start.6
  27.1 0.6 collective-permute-start.5
  27.7 1.0 collective-permute-start.8
  28.7 2.7 %pack_named.1 = (bf16[2,64,2048]{2,1,0:T(8,128)(2,1)}, bf16[2,65,2,256]{3,2,1,0:T(2,128)(2,1)}, s32[2]{0:T(128)}) custom-call(s32[1]{0:T(128)} %bitcast.owner_ref, s32[24]{0:T(128)} %map_ref.1, s32[2]{0:T(128)} %refs_0_, s32[2]{0:T(128)} %copy-done.28, s32[2]{0:T(128)} %copy-done.27, s32[2]{0:T(128)} %copy-done.29, bf16[6,64,2048]{2,1,0:T(8,128)(2,1)} %refs_4_.1, ...), custom_call_target="tpu_custom_call" | custom-call | flops 20000000000 | bytes 1 | tf_op jit(solution)/shard_map/pack_named/pallas_call | solution.py:204
  31.4 9.8 %collective-permute-done.8.refs_0_ = bf16[256,512]{1,0:T(8,128)(2,1)S(1)} collective-permute-done((bf16[256,512]{1,0:T(8,128)(2,1)S(1)}, bf16[256,512]{1,0:T(8,128)(2,1)S(1)}, u32[]{:S(2)}, u32[]{:S(2)}) %collective-permute-start.8) | collective-permute-done | bytes 262176 | tf_op jit(solution)/shard_map/ppermute | solution.py:275
  42.4 0.6 pad_add_fusion.place_ref
  43.0 0.7 copy-done.24
  43.7 0.7 copy-done.25
  44.4 0.7 copy-done.26
  45.1 5.6 %walk_step.3.refs_10_ = bf16[1024,512]{1,0:T(8,128)(2,1)} custom-call(s32[2]{0:T(128)} %pad_add_fusion.place_ref, bf16[1024,2048]{1,0:T(8,128)(2,1)} %tok_ref.7, bf16[256,512]{1,0:T(8,128)(2,1)} %copy-done.9, bf16[256,512]{1,0:T(8,128)(2,1)} %collective-permute-done.5.refs_1_, bf16[256,512]{1,0:T(8,128)(2,1)} %collective-permute-done.6.refs_2_, ...), custom_call_target="tpu_custom_call" | custom-call | flops 20000000000 | bytes 1 | tf_op jit(solution)/shard_map/walk_step/pallas_call | solution.py:151
  50.7 2.5 %collective-permute-start.18 = (bf16[1024,512]{1,0:T(8,128)(2,1)}, bf16[1024,512]{1,0:T(8,128)(2,1)}, u32[]{:S(2)}, u32[]{:S(2)}) collective-permute-start(bf16[1024,512]{1,0:T(8,128)(2,1)} %walk_step.3.refs_10_), channel_id=1, source_target_pairs={{0,1},{3,2},{4,5},{7,6},{8,9},{11,10},{12,13},{15,14},{16,17},{19,... | collective-permute-start | bytes 3145736 | tf_op jit(solution)/shard_map/ppermute | solution.py:362
  53.2 2.2 %collective-permute-start.15 = (bf16[256,512]{1,0:T(8,128)(2,1)S(1)}, bf16[256,512]{1,0:T(8,128)(2,1)S(1)}, u32[]{:S(2)}, u32[]{:S(2)}) collective-permute-start(bf16[256,512]{1,0:T(8,128)(2,1)S(1)} %collective-permute-done.8.refs_0_), channel_id=1, source_target_pairs={{0,24},{4,28},{8,16},{12,20},{16,8},{20,12},{24,0},{28,4},{1,25},{... | collective-permute-start | bytes 786440 | tf_op jit(solution)/shard_map/ppermute | solution.py:20
  55.4 0.5 collective-permute-start.14
  55.9 0.8 collective-permute-start.13
  56.8 1.3 collective-permute-start.30
  58.1 5.3 %collective-permute-done.15.refs_3_ = bf16[256,512]{1,0:T(8,128)(2,1)S(1)} collective-permute-done((bf16[256,512]{1,0:T(8,128)(2,1)S(1)}, bf16[256,512]{1,0:T(8,128)(2,1)S(1)}, u32[]{:S(2)}, u32[]{:S(2)}) %collective-permute-start.15) | collective-permute-done | bytes 262176 | tf_op jit(solution)/shard_map/ppermute | solution.py:20
  63.4 0.7 collective-permute-start.31
  64.0 3.8 %collective-permute-done.14.refs_2_ = bf16[256,512]{1,0:T(8,128)(2,1)S(1)} collective-permute-done((bf16[256,512]{1,0:T(8,128)(2,1)S(1)}, bf16[256,512]{1,0:T(8,128)(2,1)S(1)}, u32[]{:S(2)}, u32[]{:S(2)}) %collective-permute-start.14) | collective-permute-done | bytes 262176 | tf_op jit(solution)/shard_map/ppermute | solution.py:20
  68.1 1.4 collective-permute-start.16
  70.3 0.8 collective-permute-done.20.refs_5_
  71.8 0.7 copy-done.19
  72.5 1.6 collective-permute-start.34
  74.2 1.1 collective-permute-done.18.refs_8_
  75.3 5.7 %walk_step.4 = bf16[1024,512]{1,0:T(8,128)(2,1)} custom-call(s32[2]{0:T(128)} %pad_add_fusion.place_ref, bf16[1024,2048]{1,0:T(8,128)(2,1)} %tok_ref.7, bf16[256,512]{1,0:T(8,128)(2,1)} %copy-done.6, bf16[256,512]{1,0:T(8,128)(2,1)} %copy-done.10, bf16[256,512]{1,0:T(8,128)(2,1)} %copy-done.8, bf16[256,512]{1,0:T(8,128)(2,1)} %copy-done.7, ...), custom_call_target="tpu_custom_call" | custom-call | flops 1 | bytes 1 | tf_op jit(solution)/shard_map/walk_step/pallas_call | solution.py:151
  81.0 1.7 %collective-permute-start.29 = (bf16[1024,512]{1,0:T(8,128)(2,1)}, bf16[1024,512]{1,0:T(8,128)(2,1)}, u32[]{:S(2)}, u32[]{:S(2)}) collective-permute-start(bf16[1024,512]{1,0:T(8,128)(2,1)} %walk_step.4), channel_id=1, source_target_pairs={{3,2},{2,1},{7,6},{6,5},{11,10},{10,9},{15,14},{14,13},{19,18},{18... | collective-permute-start | bytes 3145736 | tf_op jit(solution)/shard_map/ppermute | solution.py:364
  82.7 5.0 %collective-permute-start.28 = (bf16[1024,512]{1,0:T(8,128)(2,1)}, bf16[1024,512]{1,0:T(8,128)(2,1)}, u32[]{:S(2)}, u32[]{:S(2)}) collective-permute-start(bf16[1024,512]{1,0:T(8,128)(2,1)} %walk_step.4), channel_id=1, source_target_pairs={{0,1},{1,2},{4,5},{5,6},{8,9},{9,10},{12,13},{13,14},{16,17},{17,1... | collective-permute-start | bytes 3145736 | tf_op jit(solution)/shard_map/ppermute | solution.py:364
  87.7 1.1 constant_dynamic-update-slice_fusion.mine_ref
  88.9 1.7 %collective-permute-start.33 = (bf16[256,512]{1,0:T(8,128)(2,1)S(1)}, bf16[256,512]{1,0:T(8,128)(2,1)S(1)}, u32[]{:S(2)}, u32[]{:S(2)}) collective-permute-start(bf16[256,512]{1,0:T(8,128)(2,1)S(1)} %add.107.refs_0_), channel_id=1, source_target_pairs={{0,16},{4,20},{8,24},{12,28},{16,0},{20,4},{24,8},{28,12},{1,17},{... | collective-permute-start | bytes 786440 | tf_op jit(solution)/shard_map/ppermute | solution.py:20
  90.6 1.3 collective-permute-start.32
  91.9 5.7 %collective-permute-done.33.refs_2_ = bf16[256,512]{1,0:T(8,128)(2,1)S(1)} collective-permute-done((bf16[256,512]{1,0:T(8,128)(2,1)S(1)}, bf16[256,512]{1,0:T(8,128)(2,1)S(1)}, u32[]{:S(2)}, u32[]{:S(2)}) %collective-permute-start.33) | collective-permute-done | bytes 262176 | tf_op jit(solution)/shard_map/ppermute | solution.py:20
  97.6 1.3 collective-permute-done.32.refs_1_
  99.0 0.5 collective-permute-start.36
  99.5 1.0 collective-permute-done.35.refs_4_
  101.0 1.0 collective-permute-done.37.refs_6_
  102.1 1.4 collective-permute-start.26
  103.5 0.6 pad_add_fusion.1.place_ref
  104.1 4.8 %collective-permute-done.28.refs_8_ = bf16[1024,512]{1,0:T(8,128)(2,1)} collective-permute-done((bf16[1024,512]{1,0:T(8,128)(2,1)}, bf16[1024,512]{1,0:T(8,128)(2,1)}, u32[]{:S(2)}, u32[]{:S(2)}) %collective-permute-start.28) | collective-permute-done | bytes 1048608 | tf_op jit(solution)/shard_map/ppermute | solution.py:364
  108.9 6.4 %walk_step.5 = (bf16[1024,512]{1,0:T(8,128)(2,1)}, bf16[1024,512]{1,0:T(8,128)(2,1)}) custom-call(s32[3]{0:T(128)} %pad_add_fusion.1.place_ref, bf16[1024,2048]{1,0:T(8,128)(2,1)} %tok_ref.7, bf16[256,512]{1,0:T(8,128)(2,1)} %copy-done.3, bf16[256,512]{1,0:T(8,128)(2,1)} %copy-done.12, bf16[256,512]{1,0:T(8,128)(2,1)} %copy-done.11, ...), custom_call_target="tpu_custom_call" | custom-call | flops 1 | bytes 1 | tf_op jit(solution)/shard_map/walk_step/pallas_call | solution.py:151
  115.3 5.6 %collective-permute-start.39 = (bf16[1024,512]{1,0:T(8,128)(2,1)}, bf16[1024,512]{1,0:T(8,128)(2,1)}, u32[]{:S(2)}, u32[]{:S(2)}) collective-permute-start(bf16[1024,512]{1,0:T(8,128)(2,1)} %get-tuple-element.125), channel_id=1, source_target_pairs={{0,1},{1,2},{2,3},{4,5},{5,6},{6,7},{8,9},{9,10},{10,11},{12,13},{... | collective-permute-start | bytes 3145736 | tf_op jit(solution)/shard_map/ppermute | solution.py:364
  121.0 1.3 collective-permute-start.40
  122.3 1.3 pad_maximum_fusion
  123.5 4.7 %coefficients.1 = f32[2,64,512]{2,1,0:T(8,128)} custom-call(s32[2]{0:T(128)} %get-tuple-element.108.pick_ref, bf16[1024,2048]{1,0:T(8,128)(2,1)} %tok_ref.7, bf16[4,64,2048]{2,1,0:T(8,128)(2,1)} %copy-done.1, bf16[4,64,2048]{2,1,0:T(8,128)(2,1)} %collective-permute-done.17.other_ref), custom_call_target="tpu_custom_call" | custom-call | flops 1 | bytes 1 | tf_op jit(solution)/shard_map/coefficients/pallas_call | solution.py:232
  128.2 0.6 fusion.6
  131.2 1.0 convert_element_type.38
  132.2 2.7 %collective-permute-start.25 = (bf16[2,64,512]{2,1,0:T(8,128)(2,1)S(1)}, bf16[2,64,512]{2,1,0:T(8,128)(2,1)}, u32[]{:S(2)}, u32[]{:S(2)}) collective-permute-start(bf16[2,64,512]{2,1,0:T(8,128)(2,1)S(1)} %convert_element_type.38), channel_id=1, source_target_pairs={{0,1},{1,0},{2,3},{3,2},{4,5},{5,4},{6,7},{7,6},{8,9},{9,8},{10,11... | collective-permute-start | bytes 393224 | tf_op jit(solution)/shard_map/ppermute | solution.py:20
  134.9 1.8 %collective-permute-start.24 = (bf16[2,64,512]{2,1,0:T(8,128)(2,1)S(1)}, bf16[2,64,512]{2,1,0:T(8,128)(2,1)}, u32[]{:S(2)}, u32[]{:S(2)}) collective-permute-start(bf16[2,64,512]{2,1,0:T(8,128)(2,1)S(1)} %convert_element_type.38), channel_id=1, source_target_pairs={{0,2},{1,3},{2,0},{3,1},{4,6},{5,7},{6,4},{7,5},{8,10},{9,11},{10,... | collective-permute-start | bytes 393224 | tf_op jit(solution)/shard_map/ppermute | solution.py:20
  138.2 0.7 collective-permute-start.23
  138.8 1.2 constant_dynamic-update-slice_fusion.2
  140.4 11.4 %collective-permute-done.25 = bf16[2,64,512]{2,1,0:T(8,128)(2,1)} collective-permute-done((bf16[2,64,512]{2,1,0:T(8,128)(2,1)S(1)}, bf16[2,64,512]{2,1,0:T(8,128)(2,1)}, u32[]{:S(2)}, u32[]{:S(2)}) %collective-permute-start.25) | collective-permute-done | bytes 131104 | tf_op jit(solution)/shard_map/ppermute | solution.py:20
  151.8 4.9 %collective-permute-done.24 = bf16[2,64,512]{2,1,0:T(8,128)(2,1)} collective-permute-done((bf16[2,64,512]{2,1,0:T(8,128)(2,1)S(1)}, bf16[2,64,512]{2,1,0:T(8,128)(2,1)}, u32[]{:S(2)}, u32[]{:S(2)}) %collective-permute-start.24) | collective-permute-done | bytes 131104 | tf_op jit(solution)/shard_map/ppermute | solution.py:20
  156.7 1.6 fusion.4
  158.3 2.3 %fusion.2 = bf16[1024,512]{1,0:T(8,128)(2,1)S(1)} fusion(f32[1024,512]{1,0:T(8,128)S(1)} %convolution_bitcast_fusion, f32[2,512,512]{2,1,0:T(8,128)S(1)} %fusion.4, bf16[1024,512]{1,0:T(8,128)(2,1)} %collective-permute-done.40, bf16[1024,512]{1,0:T(8,128)(2,1)} %collective-permute-done.39), kind=kLoop, calls=%fused_computation.3 | loop fusion | flops 3145728 | bytes 7340032 | tf_op jit(solution)/shard_map/convert_element_type | solution.py:398
  160.6 1.1 reshape.46
  (112 shorter events, 4.8 us)
Async XLA Ops:
  0.0 24.1 %collective-permute-start.3 = (s32[2]{0:T(128)}, s32[2]{0:T(128)S(1)}, u32[]{:S(2)}, u32[]{:S(2)}) collective-permute-start(s32[2]{0:T(128)} %refs_0_), channel_id=1, source_target_pairs={{0,8},{4,12},{8,0},{12,4},{1,9},{5,13},{9,1},{13,5},{2,10},{6,14},... | collective-permute-start | bytes 32 | tf_op jit(solution)/shard_map/ppermute | solution.py:20
  2.9 21.2 %collective-permute-start.2 = (s32[2]{0:T(128)}, s32[2]{0:T(128)S(1)}, u32[]{:S(2)}, u32[]{:S(2)}) collective-permute-start(s32[2]{0:T(128)} %refs_0_), channel_id=1, source_target_pairs={{0,4},{4,0},{8,12},{12,8},{1,5},{5,1},{9,13},{13,9},{2,6},{6,2},{1... | collective-permute-start | bytes 32 | tf_op jit(solution)/shard_map/ppermute | solution.py:20
  2.9 21.2 %collective-permute-start.4 = (s32[2]{0:T(128)}, s32[2]{0:T(128)S(1)}, u32[]{:S(2)}, u32[]{:S(2)}) collective-permute-start(s32[2]{0:T(128)} %refs_0_), channel_id=1, source_target_pairs={{0,12},{4,8},{8,4},{12,0},{1,13},{5,9},{9,5},{13,1},{2,14},{6,10},... | collective-permute-start | bytes 32 | tf_op jit(solution)/shard_map/ppermute | solution.py:20
  5.3 17.8 %collective-permute-start = (bf16[256,512]{1,0:T(8,128)(2,1)S(1)}, bf16[256,512]{1,0:T(8,128)(2,1)S(1)}, u32[]{:S(2)}, u32[]{:S(2)}) collective-permute-start(bf16[256,512]{1,0:T(8,128)(2,1)S(1)} %bitcast.42), channel_id=1, source_target_pairs={{3,0},{0,3},{7,4},{4,7},{11,8},{8,11},{15,12},{12,15},{19,16},{16,... | collective-permute-start | bytes 786440 | tf_op jit(solution)/shard_map/ppermute | solution.py:296
  12.1 11.0 %collective-permute-start.1 = (bf16[256,512]{1,0:T(8,128)(2,1)}, bf16[256,512]{1,0:T(8,128)(2,1)}, u32[]{:S(2)}, u32[]{:S(2)}) collective-permute-start(bf16[256,512]{1,0:T(8,128)(2,1)} %bitcast.13), channel_id=1, source_target_pairs={{0,1},{3,2},{4,5},{7,6},{8,9},{11,10},{12,13},{15,14},{16,17},{19,... | collective-permute-start | bytes 786440 | tf_op jit(solution)/shard_map/ppermute | solution.py:296
  17.4 2.2 %copy-start = (bf16[1024,2048]{1,0:T(8,128)(2,1)S(1)}, bf16[1024,2048]{1,0:T(8,128)(2,1)}, u32[]{:S(2)}) copy-start(bf16[1024,2048]{1,0:T(8,128)(2,1)} %tok_ref.7) | copy-start | bytes 12582916
  19.6 2.3 %copy-start.22 = (bf16[6,64]{1,0:T(8,128)(2,1)S(1)}, bf16[6,64]{1,0:T(8,128)(2,1)}, u32[]{:S(2)}) copy-start(bf16[6,64]{1,0:T(8,128)(2,1)} %param.11) | copy-start | bytes 2308
  19.6 2.4 %copy-start.5 = (bf16[6,64,2,256]{3,2,1,0:T(2,128)(2,1)S(1)}, bf16[6,64,2,256]{3,2,1,0:T(2,128)(2,1)}, u32[]{:S(2)}) copy-start(bf16[6,64,2,256]{3,2,1,0:T(2,128)(2,1)} %param.10) | copy-start | bytes 1179652
  24.1 17.2 %copy-start.9 = (bf16[256,512]{1,0:T(8,128)(2,1)}, bf16[256,512]{1,0:T(8,128)(2,1)S(1)}, u32[]{:S(2)}) copy-start(bf16[256,512]{1,0:T(8,128)(2,1)S(1)} %add.90.refs_0_) | copy-start | bytes 786436
  24.1 4.6 %copy-start.27 = (s32[2]{0:T(128)}, s32[2]{0:T(128)S(1)}, u32[]{:S(2)}) copy-start(s32[2]{0:T(128)S(1)} %collective-permute-done.3.refs_2_) | copy-start | bytes 28
  24.1 4.6 %copy-start.28 = (s32[2]{0:T(128)}, s32[2]{0:T(128)S(1)}, u32[]{:S(2)}) copy-start(s32[2]{0:T(128)S(1)} %collective-permute-done.2.refs_1_) | copy-start | bytes 28
  24.2 4.5 %copy-start.29 = (s32[2]{0:T(128)}, s32[2]{0:T(128)S(1)}, u32[]{:S(2)}) copy-start(s32[2]{0:T(128)S(1)} %collective-permute-done.4.refs_3_) | copy-start | bytes 28
  24.2 17.1 %collective-permute-start.7 = (bf16[256,512]{1,0:T(8,128)(2,1)S(1)}, bf16[256,512]{1,0:T(8,128)(2,1)S(1)}, u32[]{:S(2)}, u32[]{:S(2)}) collective-permute-start(bf16[256,512]{1,0:T(8,128)(2,1)S(1)} %add.90.refs_0_), channel_id=1, source_target_pairs={{0,24},{4,28},{8,16},{12,20},{16,8},{20,12},{24,0},{28,4},{1,25},{... | collective-permute-start | bytes 786440 | tf_op jit(solution)/shard_map/ppermute | solution.py:20
  26.6 14.7 %collective-permute-start.6 = (bf16[256,512]{1,0:T(8,128)(2,1)S(1)}, bf16[256,512]{1,0:T(8,128)(2,1)}, u32[]{:S(2)}, u32[]{:S(2)}) collective-permute-start(bf16[256,512]{1,0:T(8,128)(2,1)S(1)} %add.90.refs_0_), channel_id=1, source_target_pairs={{0,16},{4,20},{8,24},{12,28},{16,0},{20,4},{24,8},{28,12},{1,17},{... | collective-permute-start | bytes 786440 | tf_op jit(solution)/shard_map/ppermute | solution.py:20
  27.1 14.2 %collective-permute-start.5 = (bf16[256,512]{1,0:T(8,128)(2,1)S(1)}, bf16[256,512]{1,0:T(8,128)(2,1)}, u32[]{:S(2)}, u32[]{:S(2)}) collective-permute-start(bf16[256,512]{1,0:T(8,128)(2,1)S(1)} %add.90.refs_0_), channel_id=1, source_target_pairs={{0,8},{4,12},{8,0},{12,4},{16,24},{20,28},{24,16},{28,20},{1,9},{5... | collective-permute-start | bytes 786440 | tf_op jit(solution)/shard_map/ppermute | solution.py:20
  27.7 13.5 %collective-permute-start.8 = (bf16[256,512]{1,0:T(8,128)(2,1)S(1)}, bf16[256,512]{1,0:T(8,128)(2,1)S(1)}, u32[]{:S(2)}, u32[]{:S(2)}) collective-permute-start(bf16[256,512]{1,0:T(8,128)(2,1)S(1)} %bitcast.40), channel_id=1, source_target_pairs={{2,0},{3,1},{0,2},{1,3},{6,4},{7,5},{4,6},{5,7},{10,8},{11,9},{8,1... | collective-permute-start | bytes 786440 | tf_op jit(solution)/shard_map/ppermute | solution.py:275
  41.3 26.8 %copy-start.6 = (bf16[256,512]{1,0:T(8,128)(2,1)}, bf16[256,512]{1,0:T(8,128)(2,1)S(1)}, u32[]{:S(2)}) copy-start(bf16[256,512]{1,0:T(8,128)(2,1)S(1)} %collective-permute-done.8.refs_0_) | copy-start | bytes 786436
  41.3 3.9 %copy-start.23 = (bf16[256,512]{1,0:T(8,128)(2,1)}, bf16[256,512]{1,0:T(8,128)(2,1)S(1)}, u32[]{:S(2)}) copy-start(bf16[256,512]{1,0:T(8,128)(2,1)S(1)} %collective-permute-done.7.refs_3_) | copy-start | bytes 786436
  41.3 1.7 %collective-permute-start.9 = (bf16[256,512]{1,0:T(8,128)(2,1)S(1)}, bf16[256,512]{1,0:T(8,128)(2,1)S(1)}, u32[]{:S(2)}, u32[]{:S(2)}) collective-permute-start(bf16[256,512]{1,0:T(8,128)(2,1)S(1)} %add.90.refs_0_), channel_id=1, source_target_pairs={{0,4},{4,0},{8,12},{12,8},{1,5},{5,1},{9,13},{13,9},{2,6},{6,2},{1... | collective-permute-start | bytes 786440 | tf_op jit(solution)/shard_map/ppermute | solution.py:20
  41.4 2.3 %collective-permute-start.10 = (bf16[256,512]{1,0:T(8,128)(2,1)}, bf16[256,512]{1,0:T(8,128)(2,1)S(1)}, u32[]{:S(2)}, u32[]{:S(2)}) collective-permute-start(bf16[256,512]{1,0:T(8,128)(2,1)} %collective-permute-done.5.refs_1_), channel_id=1, source_target_pairs={{0,4},{4,0},{8,12},{12,8},{1,5},{5,1},{9,13},{13,9},{2,6},{6,2},{1... | collective-permute-start | bytes 786440 | tf_op jit(solution)/shard_map/ppermute | solution.py:20
  41.9 2.5 %collective-permute-start.11 = (bf16[256,512]{1,0:T(8,128)(2,1)}, bf16[256,512]{1,0:T(8,128)(2,1)S(1)}, u32[]{:S(2)}, u32[]{:S(2)}) collective-permute-start(bf16[256,512]{1,0:T(8,128)(2,1)} %collective-permute-done.6.refs_2_), channel_id=1, source_target_pairs={{0,4},{4,0},{8,12},{12,8},{1,5},{5,1},{9,13},{13,9},{2,6},{6,2},{1... | collective-permute-start | bytes 786440 | tf_op jit(solution)/shard_map/ppermute | solution.py:20
  41.9 3.2 %collective-permute-start.12 = (bf16[256,512]{1,0:T(8,128)(2,1)S(1)}, bf16[256,512]{1,0:T(8,128)(2,1)}, u32[]{:S(2)}, u32[]{:S(2)}) collective-permute-start(bf16[256,512]{1,0:T(8,128)(2,1)S(1)} %collective-permute-done.7.refs_3_), channel_id=1, source_target_pairs={{0,4},{4,0},{8,12},{12,8},{1,5},{5,1},{9,13},{13,9},{2,6},{6,2},{1... | collective-permute-start | bytes 786440 | tf_op jit(solution)/shard_map/ppermute | solution.py:20
  43.0 25.1 %copy-start.4 = (bf16[2,64,2048]{2,1,0:T(8,128)(2,1)S(1)}, bf16[2,64,2048]{2,1,0:T(8,128)(2,1)}, u32[]{:S(2)}) copy-start(bf16[2,64,2048]{2,1,0:T(8,128)(2,1)} %get-tuple-element.90) | copy-start | bytes 1572868
  50.7 24.6 %collective-permute-start.18 = (bf16[1024,512]{1,0:T(8,128)(2,1)}, bf16[1024,512]{1,0:T(8,128)(2,1)}, u32[]{:S(2)}, u32[]{:S(2)}) collective-permute-start(bf16[1024,512]{1,0:T(8,128)(2,1)} %walk_step.3.refs_10_), channel_id=1, source_target_pairs={{0,1},{3,2},{4,5},{7,6},{8,9},{11,10},{12,13},{15,14},{16,17},{19,... | collective-permute-start | bytes 3145736 | tf_op jit(solution)/shard_map/ppermute | solution.py:362
  53.2 10.1 %collective-permute-start.15 = (bf16[256,512]{1,0:T(8,128)(2,1)S(1)}, bf16[256,512]{1,0:T(8,128)(2,1)S(1)}, u32[]{:S(2)}, u32[]{:S(2)}) collective-permute-start(bf16[256,512]{1,0:T(8,128)(2,1)S(1)} %collective-permute-done.8.refs_0_), channel_id=1, source_target_pairs={{0,24},{4,28},{8,16},{12,20},{16,8},{20,12},{24,0},{28,4},{1,25},{... | collective-permute-start | bytes 786440 | tf_op jit(solution)/shard_map/ppermute | solution.py:20
  55.4 12.4 %collective-permute-start.14 = (bf16[256,512]{1,0:T(8,128)(2,1)S(1)}, bf16[256,512]{1,0:T(8,128)(2,1)S(1)}, u32[]{:S(2)}, u32[]{:S(2)}) collective-permute-start(bf16[256,512]{1,0:T(8,128)(2,1)S(1)} %collective-permute-done.8.refs_0_), channel_id=1, source_target_pairs={{0,16},{4,20},{8,24},{12,28},{16,0},{20,4},{24,8},{28,12},{1,17},{... | collective-permute-start | bytes 786440 | tf_op jit(solution)/shard_map/ppermute | solution.py:20
  55.9 12.1 %collective-permute-start.13 = (bf16[256,512]{1,0:T(8,128)(2,1)S(1)}, bf16[256,512]{1,0:T(8,128)(2,1)S(1)}, u32[]{:S(2)}, u32[]{:S(2)}) collective-permute-start(bf16[256,512]{1,0:T(8,128)(2,1)S(1)} %collective-permute-done.8.refs_0_), channel_id=1, source_target_pairs={{0,8},{4,12},{8,0},{12,4},{16,24},{20,28},{24,16},{28,20},{1,9},{5... | collective-permute-start | bytes 786440 | tf_op jit(solution)/shard_map/ppermute | solution.py:20
  56.8 12.7 %collective-permute-start.30 = (bf16[256,512]{1,0:T(8,128)(2,1)S(1)}, bf16[256,512]{1,0:T(8,128)(2,1)S(1)}, u32[]{:S(2)}, u32[]{:S(2)}) collective-permute-start(bf16[256,512]{1,0:T(8,128)(2,1)S(1)} %bitcast.43), channel_id=1, source_target_pairs={{1,0},{2,3},{5,4},{6,7},{9,8},{10,11},{13,12},{14,15},{17,16},{18,... | collective-permute-start | bytes 786440 | tf_op jit(solution)/shard_map/ppermute | solution.py:275
  63.4 8.4 %copy-start.7 = (bf16[256,512]{1,0:T(8,128)(2,1)}, bf16[256,512]{1,0:T(8,128)(2,1)S(1)}, u32[]{:S(2)}) copy-start(bf16[256,512]{1,0:T(8,128)(2,1)S(1)} %collective-permute-done.15.refs_3_) | copy-start | bytes 786436
  63.4 6.3 %collective-permute-start.31 = (bf16[256,512]{1,0:T(8,128)(2,1)S(1)}, bf16[256,512]{1,0:T(8,128)(2,1)S(1)}, u32[]{:S(2)}, u32[]{:S(2)}) collective-permute-start(bf16[256,512]{1,0:T(8,128)(2,1)S(1)} %bitcast.41), channel_id=1, source_target_pairs={{2,1},{1,2},{6,5},{5,6},{10,9},{9,10},{14,13},{13,14},{18,17},{17,... | collective-permute-start | bytes 786440 | tf_op jit(solution)/shard_map/ppermute | solution.py:275
  67.8 6.3 %copy-start.8 = (bf16[256,512]{1,0:T(8,128)(2,1)}, bf16[256,512]{1,0:T(8,128)(2,1)S(1)}, u32[]{:S(2)}) copy-start(bf16[256,512]{1,0:T(8,128)(2,1)S(1)} %collective-permute-done.14.refs_2_) | copy-start | bytes 786436
  68.0 6.1 %copy-start.10 = (bf16[256,512]{1,0:T(8,128)(2,1)}, bf16[256,512]{1,0:T(8,128)(2,1)S(1)}, u32[]{:S(2)}) copy-start(bf16[256,512]{1,0:T(8,128)(2,1)S(1)} %collective-permute-done.13.refs_1_) | copy-start | bytes 786436
  68.0 2.0 %collective-permute-start.19 = (bf16[256,512]{1,0:T(8,128)(2,1)S(1)}, bf16[256,512]{1,0:T(8,128)(2,1)S(1)}, u32[]{:S(2)}, u32[]{:S(2)}) collective-permute-start(bf16[256,512]{1,0:T(8,128)(2,1)S(1)} %collective-permute-done.8.refs_0_), channel_id=1, source_target_pairs={{0,4},{4,0},{8,12},{12,8},{1,5},{5,1},{9,13},{13,9},{2,6},{6,2},{1... | collective-permute-start | bytes 786440 | tf_op jit(solution)/shard_map/ppermute | solution.py:20
  68.1 19.7 %collective-permute-start.16 = (bf16[2,64,2048]{2,1,0:T(8,128)(2,1)S(1)}, bf16[2,64,2048]{2,1,0:T(8,128)(2,1)}, u32[]{:S(2)}, u32[]{:S(2)}) collective-permute-start(bf16[2,64,2048]{2,1,0:T(8,128)(2,1)S(1)} %copy-done.4), channel_id=1, source_target_pairs={{0,8},{4,12},{8,0},{12,4},{1,9},{5,13},{9,1},{13,5},{2,10},{6,14},... | collective-permute-start | bytes 1572872 | tf_op jit(solution)/shard_map/ppermute | solution.py:20
  69.5 1.5 collective-permute-start.20
  69.7 1.7 %collective-permute-start.21 = (bf16[256,512]{1,0:T(8,128)(2,1)S(1)}, bf16[256,512]{1,0:T(8,128)(2,1)S(1)}, u32[]{:S(2)}, u32[]{:S(2)}) collective-permute-start(bf16[256,512]{1,0:T(8,128)(2,1)S(1)} %collective-permute-done.14.refs_2_), channel_id=1, source_target_pairs={{0,4},{4,0},{8,12},{12,8},{1,5},{5,1},{9,13},{13,9},{2,6},{6,2},{1... | collective-permute-start | bytes 786440 | tf_op jit(solution)/shard_map/ppermute | solution.py:20
  70.0 1.8 %collective-permute-start.22 = (bf16[256,512]{1,0:T(8,128)(2,1)S(1)}, bf16[256,512]{1,0:T(8,128)(2,1)S(1)}, u32[]{:S(2)}, u32[]{:S(2)}) collective-permute-start(bf16[256,512]{1,0:T(8,128)(2,1)S(1)} %collective-permute-done.15.refs_3_), channel_id=1, source_target_pairs={{0,4},{4,0},{8,12},{12,8},{1,5},{5,1},{9,13},{13,9},{2,6},{6,2},{1... | collective-permute-start | bytes 786440 | tf_op jit(solution)/shard_map/ppermute | solution.py:20
  70.2 28.7 %copy-start.3 = (bf16[256,512]{1,0:T(8,128)(2,1)}, bf16[256,512]{1,0:T(8,128)(2,1)S(1)}, u32[]{:S(2)}) copy-start(bf16[256,512]{1,0:T(8,128)(2,1)S(1)} %add.107.refs_0_) | copy-start | bytes 786436
  71.0 3.1 %copy-start.17 = (bf16[256,512]{1,0:T(8,128)(2,1)}, bf16[256,512]{1,0:T(8,128)(2,1)S(1)}, u32[]{:S(2)}) copy-start(bf16[256,512]{1,0:T(8,128)(2,1)S(1)} %collective-permute-done.20.refs_5_) | copy-start | bytes 786436
  71.4 2.8 %copy-start.18 = (bf16[256,512]{1,0:T(8,128)(2,1)}, bf16[256,512]{1,0:T(8,128)(2,1)S(1)}, u32[]{:S(2)}) copy-start(bf16[256,512]{1,0:T(8,128)(2,1)S(1)} %collective-permute-done.21.refs_6_) | copy-start | bytes 786436
  72.5 18.1 %collective-permute-start.34 = (bf16[256,512]{1,0:T(8,128)(2,1)S(1)}, bf16[256,512]{1,0:T(8,128)(2,1)}, u32[]{:S(2)}, u32[]{:S(2)}) collective-permute-start(bf16[256,512]{1,0:T(8,128)(2,1)S(1)} %add.107.refs_0_), channel_id=1, source_target_pairs={{0,24},{4,28},{8,16},{12,20},{16,8},{20,12},{24,0},{28,4},{1,25},{... | collective-permute-start | bytes 786440 | tf_op jit(solution)/shard_map/ppermute | solution.py:20
  74.2 27.9 %copy-start.20 = (bf16[2,65,2,256]{3,2,1,0:T(2,128)(2,1)S(1)}, bf16[2,65,2,256]{3,2,1,0:T(2,128)(2,1)}, u32[]{:S(2)}) copy-start(bf16[2,65,2,256]{3,2,1,0:T(2,128)(2,1)} %get-tuple-element.106) | copy-start | bytes 399364
  81.0 23.1 %collective-permute-start.29 = (bf16[1024,512]{1,0:T(8,128)(2,1)}, bf16[1024,512]{1,0:T(8,128)(2,1)}, u32[]{:S(2)}, u32[]{:S(2)}) collective-permute-start(bf16[1024,512]{1,0:T(8,128)(2,1)} %walk_step.4), channel_id=1, source_target_pairs={{3,2},{2,1},{7,6},{6,5},{11,10},{10,9},{15,14},{14,13},{19,18},{18... | collective-permute-start | bytes 3145736 | tf_op jit(solution)/shard_map/ppermute | solution.py:364
  82.7 26.2 %collective-permute-start.28 = (bf16[1024,512]{1,0:T(8,128)(2,1)}, bf16[1024,512]{1,0:T(8,128)(2,1)}, u32[]{:S(2)}, u32[]{:S(2)}) collective-permute-start(bf16[1024,512]{1,0:T(8,128)(2,1)} %walk_step.4), channel_id=1, source_target_pairs={{0,1},{1,2},{4,5},{5,6},{8,9},{9,10},{12,13},{13,14},{16,17},{17,1... | collective-permute-start | bytes 3145736 | tf_op jit(solution)/shard_map/ppermute | solution.py:364
  88.8 26.5 %copy-start.1 = (bf16[4,64,2048]{2,1,0:T(8,128)(2,1)}, bf16[4,64,2048]{2,1,0:T(8,128)(2,1)S(1)}, u32[]{:S(2)}) copy-start(bf16[4,64,2048]{2,1,0:T(8,128)(2,1)S(1)} %constant_dynamic-update-slice_fusion.mine_ref) | copy-start | bytes 3145732
  88.8 34.7 %collective-permute-start.17 = (bf16[4,64,2048]{2,1,0:T(8,128)(2,1)S(1)}, bf16[4,64,2048]{2,1,0:T(8,128)(2,1)}, u32[]{:S(2)}, u32[]{:S(2)}) collective-permute-start(bf16[4,64,2048]{2,1,0:T(8,128)(2,1)S(1)} %constant_dynamic-update-slice_fusion.mine_ref), channel_id=1, source_target_pairs={{0,4},{4,0},{8,12},{12,8},{1,5},{5,1},{9,13},{13,9},{2,6},{6,2},{1... | collective-permute-start | bytes 3145736 | tf_op jit(solution)/shard_map/ppermute | solution.py:20
  88.9 8.7 %collective-permute-start.33 = (bf16[256,512]{1,0:T(8,128)(2,1)S(1)}, bf16[256,512]{1,0:T(8,128)(2,1)S(1)}, u32[]{:S(2)}, u32[]{:S(2)}) collective-permute-start(bf16[256,512]{1,0:T(8,128)(2,1)S(1)} %add.107.refs_0_), channel_id=1, source_target_pairs={{0,16},{4,20},{8,24},{12,28},{16,0},{20,4},{24,8},{28,12},{1,17},{... | collective-permute-start | bytes 786440 | tf_op jit(solution)/shard_map/ppermute | solution.py:20
  90.6 8.4 %collective-permute-start.32 = (bf16[256,512]{1,0:T(8,128)(2,1)S(1)}, bf16[256,512]{1,0:T(8,128)(2,1)S(1)}, u32[]{:S(2)}, u32[]{:S(2)}) collective-permute-start(bf16[256,512]{1,0:T(8,128)(2,1)S(1)} %add.107.refs_0_), channel_id=1, source_target_pairs={{0,8},{4,12},{8,0},{12,4},{16,24},{20,28},{24,16},{28,20},{1,9},{5... | collective-permute-start | bytes 786440 | tf_op jit(solution)/shard_map/ppermute | solution.py:20
  97.6 2.9 %copy-start.11 = (bf16[256,512]{1,0:T(8,128)(2,1)}, bf16[256,512]{1,0:T(8,128)(2,1)S(1)}, u32[]{:S(2)}) copy-start(bf16[256,512]{1,0:T(8,128)(2,1)S(1)} %collective-permute-done.33.refs_2_) | copy-start | bytes 786436
  99.0 3.1 %copy-start.12 = (bf16[256,512]{1,0:T(8,128)(2,1)}, bf16[256,512]{1,0:T(8,128)(2,1)S(1)}, u32[]{:S(2)}) copy-start(bf16[256,512]{1,0:T(8,128)(2,1)S(1)} %collective-permute-done.32.refs_1_) | copy-start | bytes 786436
  99.0 1.5 collective-permute-start.35
  99.0 1.9 %collective-permute-start.36 = (bf16[256,512]{1,0:T(8,128)(2,1)S(1)}, bf16[256,512]{1,0:T(8,128)(2,1)S(1)}, u32[]{:S(2)}, u32[]{:S(2)}) collective-permute-start(bf16[256,512]{1,0:T(8,128)(2,1)S(1)} %collective-permute-done.32.refs_1_), channel_id=1, source_target_pairs={{0,4},{4,0},{8,12},{12,8},{1,5},{5,1},{9,13},{13,9},{2,6},{6,2},{1... | collective-permute-start | bytes 786440 | tf_op jit(solution)/shard_map/ppermute | solution.py:20
  100.5 1.5 collective-permute-start.37
  100.9 3.2 %collective-permute-start.38 = (bf16[256,512]{1,0:T(8,128)(2,1)}, bf16[256,512]{1,0:T(8,128)(2,1)}, u32[]{:S(2)}, u32[]{:S(2)}) collective-permute-start(bf16[256,512]{1,0:T(8,128)(2,1)} %collective-permute-done.34.refs_3_), channel_id=1, source_target_pairs={{0,4},{4,0},{8,12},{12,8},{1,5},{5,1},{9,13},{13,9},{2,6},{6,2},{1... | collective-permute-start | bytes 786440 | tf_op jit(solution)/shard_map/ppermute | solution.py:20
  102.1 6.9 %copy-start.16 = (bf16[256,512]{1,0:T(8,128)(2,1)}, bf16[256,512]{1,0:T(8,128)(2,1)S(1)}, u32[]{:S(2)}) copy-start(bf16[256,512]{1,0:T(8,128)(2,1)S(1)} %collective-permute-done.37.refs_6_) | copy-start | bytes 786436
  102.1 20.2 %collective-permute-start.26 = (bf16[2,65,2,256]{3,2,1,0:T(2,128)(2,1)S(1)}, bf16[2,65,2,256]{3,2,1,0:T(2,128)(2,1)}, u32[]{:S(2)}, u32[]{:S(2)}) collective-permute-start(bf16[2,65,2,256]{3,2,1,0:T(2,128)(2,1)S(1)} %copy-done.20), channel_id=1, source_target_pairs={{0,8},{4,12},{8,0},{12,4},{1,9},{5,13},{9,1},{13,5},{2,10},{6,14},... | collective-permute-start | bytes 399368 | tf_op jit(solution)/shard_map/ppermute | solution.py:20
  115.3 43.0 %collective-permute-start.39 = (bf16[1024,512]{1,0:T(8,128)(2,1)}, bf16[1024,512]{1,0:T(8,128)(2,1)}, u32[]{:S(2)}, u32[]{:S(2)}) collective-permute-start(bf16[1024,512]{1,0:T(8,128)(2,1)} %get-tuple-element.125), channel_id=1, source_target_pairs={{0,1},{1,2},{2,3},{4,5},{5,6},{6,7},{8,9},{9,10},{10,11},{12,13},{... | collective-permute-start | bytes 3145736 | tf_op jit(solution)/shard_map/ppermute | solution.py:364
  121.0 37.3 %collective-permute-start.40 = (bf16[1024,512]{1,0:T(8,128)(2,1)}, bf16[1024,512]{1,0:T(8,128)(2,1)}, u32[]{:S(2)}, u32[]{:S(2)}) collective-permute-start(bf16[1024,512]{1,0:T(8,128)(2,1)} %get-tuple-element.126), channel_id=1, source_target_pairs={{3,2},{2,1},{1,0},{7,6},{6,5},{5,4},{11,10},{10,9},{9,8},{15,14},{... | collective-permute-start | bytes 3145736 | tf_op jit(solution)/shard_map/ppermute | solution.py:364
  123.5 4.7 %copy-start.21 = (s32[2]{0:T(128)S(1)}, s32[2]{0:T(128)}, u32[]{:S(2)}) copy-start(s32[2]{0:T(128)} %get-tuple-element.108.pick_ref) | copy-start | bytes 28
  128.2 28.5 %copy-start.2 = (f32[2,64,512]{2,1,0:T(8,128)S(1)}, f32[2,64,512]{2,1,0:T(8,128)}, u32[]{:S(2)}) copy-start(f32[2,64,512]{2,1,0:T(8,128)} %coefficients.1) | copy-start | bytes 786436
  128.2 9.9 %collective-permute-start.27 = (bf16[4,65,2,256]{3,2,1,0:T(2,128)(2,1)S(1)}, bf16[4,65,2,256]{3,2,1,0:T(2,128)(2,1)}, u32[]{:S(2)}, u32[]{:S(2)}) collective-permute-start(bf16[4,65,2,256]{3,2,1,0:T(2,128)(2,1)S(1)} %pad_maximum_fusion), channel_id=1, source_target_pairs={{0,4},{4,0},{8,12},{12,8},{1,5},{5,1},{9,13},{13,9},{2,6},{6,2},{1... | collective-permute-start | bytes 798728 | tf_op jit(solution)/shard_map/ppermute | solution.py:20
  132.2 19.6 %collective-permute-start.25 = (bf16[2,64,512]{2,1,0:T(8,128)(2,1)S(1)}, bf16[2,64,512]{2,1,0:T(8,128)(2,1)}, u32[]{:S(2)}, u32[]{:S(2)}) collective-permute-start(bf16[2,64,512]{2,1,0:T(8,128)(2,1)S(1)} %convert_element_type.38), channel_id=1, source_target_pairs={{0,1},{1,0},{2,3},{3,2},{4,5},{5,4},{6,7},{7,6},{8,9},{9,8},{10,11... | collective-permute-start | bytes 393224 | tf_op jit(solution)/shard_map/ppermute | solution.py:20
  134.9 21.8 %collective-permute-start.24 = (bf16[2,64,512]{2,1,0:T(8,128)(2,1)S(1)}, bf16[2,64,512]{2,1,0:T(8,128)(2,1)}, u32[]{:S(2)}, u32[]{:S(2)}) collective-permute-start(bf16[2,64,512]{2,1,0:T(8,128)(2,1)S(1)} %convert_element_type.38), channel_id=1, source_target_pairs={{0,2},{1,3},{2,0},{3,1},{4,6},{5,7},{6,4},{7,5},{8,10},{9,11},{10,... | collective-permute-start | bytes 393224 | tf_op jit(solution)/shard_map/ppermute | solution.py:20
  138.2 18.6 %collective-permute-start.23 = (bf16[2,64,512]{2,1,0:T(8,128)(2,1)S(1)}, bf16[2,64,512]{2,1,0:T(8,128)(2,1)S(1)}, u32[]{:S(2)}, u32[]{:S(2)}) collective-permute-start(bf16[2,64,512]{2,1,0:T(8,128)(2,1)S(1)} %convert_element_type.38), channel_id=1, source_target_pairs={{0,3},{1,2},{2,1},{3,0},{4,7},{5,6},{6,5},{7,4},{8,11},{9,10},{10,... | collective-permute-start | bytes 393224 | tf_op jit(solution)/shard_map/ppermute | solution.py:20
  (7 other events, 7.3 us)

commit v4 on v3

--- a/solution.py
+++ b/solution.py
@@ -11,7 +11,7 @@
 F32 = jnp.float32
 BF16 = jnp.bfloat16
 I32 = jnp.int32
-VMEM_LIMIT = 60 * 1024 * 1024
+VMEM_LIMIT = 20 * 1024 * 1024
 SMALL = pl.CostEstimate(flops=1, bytes_accessed=1, transcendentals=0)
 LARGE = pl.CostEstimate(flops=20_000_000_000, bytes_accessed=1, transcendentals=0)
 
@@ -127,7 +127,7 @@
         out_refs[0][...] = total[...].astype(out_refs[0].dtype)
 
 
-def step(place, tokens, pieces, arrivals, earlier, outs, out_type, cost):
+def step(place, tokens, pieces, arrivals, earlier, outs, out_type, cost, room=VMEM_LIMIT):
     tok_dev, depth = tokens.shape
     masks, pieces = tuple(pieces), tuple(pieces.values())
     rows, cols = pieces[0].shape
@@ -154,7 +154,7 @@
         in_specs=[pl.BlockSpec(memory_space=pltpu.SMEM)] + [where] * (1 + count) + [far] * extra,
         out_specs=[vmem] * outs,
         scratch_shapes=scratch,
-        compiler_params=pltpu.CompilerParams(vmem_limit_bytes=VMEM_LIMIT),
+        compiler_params=pltpu.CompilerParams(vmem_limit_bytes=room),
         cost_estimate=cost,
         name="walk_step",
     )(place, tokens, *pieces, *arrivals, *earlier)
@@ -217,6 +217,37 @@
     )(owner, owner_map, *asked, delta_in, out_rows)
 
 
+def choose_kernel(pick_ref, mine_ref, other_ref, out_ref, sems):
+    half = mine_ref.shape[0]
+    for r in range(out_ref.shape[0]):
+        at = pick_ref[r]
+
+        @pl.when(at < half)
+        def _(r=r, at=at):
+            copy = pltpu.make_async_copy(mine_ref.at[at], out_ref.at[r], sems.at[r])
+            copy.start()
+            copy.wait()
+
+        @pl.when(at >= half)
+        def _(r=r, at=at):
+            copy = pltpu.make_async_copy(other_ref.at[at - half], out_ref.at[r], sems.at[r])
+            copy.start()
+            copy.wait()
+
+
+def choose(pick, mine, other):
+    far = pl.BlockSpec(memory_space=pl.ANY)
+    return pl.pallas_call(
+        choose_kernel,
+        out_shape=jax.ShapeDtypeStruct(pick.shape + mine.shape[1:], mine.dtype),
+        in_specs=[pl.BlockSpec(memory_space=pltpu.SMEM), far, far],
+        out_specs=pl.BlockSpec(memory_space=pltpu.VMEM),
+        scratch_shapes=[pltpu.SemaphoreType.DMA(pick.shape)],
+        cost_estimate=SMALL,
+        name="choose_factors",
+    )(pick, mine, other)
+
+
 def coeff_kernel(pick_ref, tok_ref, mine_ref, other_ref, coeff_ref, *, half):
     here = pick_ref[pl.program_id(0)] < half
     factor = jnp.where(here, mine_ref[...].astype(F32), other_ref[...].astype(F32)).astype(BF16)
@@ -345,7 +376,7 @@
         if fused:
             sent_on = step(
                 tied(spot, *moved), tokens, pieces, moved, earlier, len(uses), hop_type,
-                SMALL if new else LARGE,
+                SMALL if new else LARGE, VMEM_LIMIT if t < n - 1 else 3 * VMEM_LIMIT,
             )
             low[new] = sent_on[0]
         else:
@@ -363,26 +394,18 @@
         else:
             moved = [lax.ppermute(sent_on[0], "mp", rights), lax.ppermute(sent_on[-1], "mp", lefts)]
     came = moved
-    factors, outs = gathered(packed_in), gathered(packed_out)
+    factors = gathered(packed_in)
     part_coeff = coefficients(
         pick, tokens, factors, swap(factors, "tenant", n_owner, 1), resp_len
     )
     part_coeff = tied(part_coeff, low[min(1, n - 2)])
-    if n <= 4:
-        sent_coeff = part_coeff.astype(hop_type)
-        coeff = part_coeff
-        for k in range(n - 1, 0, -1):
-            coeff = coeff + swap(sent_coeff, "mp", n, k).astype(F32)
-    else:
-        coeff, mask = part_coeff, 1
-        while mask < n:
-            coeff = coeff + swap(coeff, "mp", n, mask)
-            mask *= 2
-    outs, later_pick = lax.optimization_barrier((outs, pick, part_coeff))[:2]
-    all_out = jnp.concatenate((outs, swap(outs, "tenant", n_owner, 1)), axis=0)
-    chosen = jnp.stack(
-        [lax.dynamic_index_in_dim(all_out, later_pick[r], 0, keepdims=False) for r in range(resp_dev)]
-    )
+    coeff, mask = part_coeff, 1
+    while mask < n:
+        kind = hop_type
+        coeff = coeff + swap(coeff.astype(kind), "mp", n, mask).astype(F32)
+        mask *= 2
+    outs = gathered(tied(packed_out, part_coeff))
+    chosen = choose(pick, outs, swap(outs, "tenant", n_owner, 1))
     scale = chosen[:, rank, 0, :rank].astype(F32)
     lowrank = (coeff * scale[:, :, None]).astype(BF16)
     delta = jnp.einsum(

time: 162 us -> 154 us (0.951)
  waiting for transfers between devices: 52.2 us -> 59.4 us
  other arithmetic: 8.06 us -> 4.19 us
  between operations: 4.16 us -> 0.43 us
  Pallas kernels: 25.1 us -> 21.5 us
  starting transfers between devices: 52.6 us -> 49.8 us
    ppermute x31 -> x30, waiting for transfers between devices: 36.4 us -> 39.9 us  [swap(): return lax.ppermute(value, axis, [(i, i ^ mask) for i in range(size)])]
    pallas_call x0 -> x1, Pallas kernels: none -> 3.09 us  [choose(): pl.pallas_call(choose_kernel, out_shape=jax.ShapeDtypeStruct(pick.shape +...]
    pallas_call x3, Pallas kernels: 17.7 us -> 14.8 us  [step(): pl.pallas_call(functools.partial(kernel, masks, len(arrivals), len(earlie...]
    pallas_call x1, Pallas kernels: 4.65 us -> 2.09 us  [coefficients(): pl.pallas_call(functools.partial(coeff_kernel, half=half), out_shape=jax....]
    ppermute x31 -> x30, starting transfers between devices: 25.4 us -> 23.6 us  [swap(): return lax.ppermute(value, axis, [(i, i ^ mask) for i in range(size)])]
    ppermute x1, waiting for transfers between devices: 1.1 us -> 2.8 us  [shards(): moved = [lax.ppermute(sent_on[0], 'mp', rights + lefts)]]
    unnamed x68 -> x40, local copies, waits for them, and re-layouts: 6.17 us -> 6.53 us
  transfers between devices with their start and end apart: 41 -> 40, of which waited for: 16 -> 21; matrix products, arithmetic and copies ran while one was open for 12% -> 9% of each run, Pallas kernels for 12% -> 11%
where the time goes in v4:
time: 154 us
  waiting for transfers between devices  59.4 us (39%)
  starting transfers between devices  49.8 us (32%)
  Pallas kernels  21.5 us (14%)
  local copies, waits for them, and re-layouts  14.3 us (9%)
  matrix products  4.26 us (3%)
  other arithmetic  4.19 us (3%)
    ppermute x30, waiting for transfers between devices, swap(): return lax.ppermute(value, axis, [(i, i ^ mask) for i in range(size)])  39.9 us
    ppermute x30, starting transfers between devices, swap(): return lax.ppermute(value, axis, [(i, i ^ mask) for i in range(size)])  23.6 us
    pallas_call x3, Pallas kernels, step(): pl.pallas_call(functools.partial(kernel, masks, len(arrivals), len(earlie...  14.8 us
    ppermute x2, starting transfers between devices, shards(): lax.ppermute(sent_on[0], 'mp', rights)  10.6 us
    ppermute x3, waiting for transfers between devices, arrival(): lax.ppermute(tied(part_for(pairs), *waits), 'mp', pairs)  10.3 us
    ppermute x2, starting transfers between devices, shards(): lax.ppermute(part, 'mp', pairs)  7.43 us
    unnamed x40, local copies, waits for them, and re-layouts  6.53 us
    ppermute x2, waiting for transfers between devices, shards(): lax.ppermute(sent_on[0], 'mp', rights)  5.99 us
  transfers between devices with their start and end apart: 40, of which 21 were waited for; matrix products, arithmetic and copies ran while one was open for 9% of the time, Pallas kernels for 11%

profile of v4, /device:TPU:0, one launch (start us, length us, event | category | flops | bytes accessed | tf_op | source)
XLA Modules:
  0.0 153.9 jit_solution(8125050210722478594)
XLA Ops:
  0.0 2.9 %collective-permute-start.3 = (s32[2]{0:T(128)}, s32[2]{0:T(128)S(1)}, u32[]{:S(2)}, u32[]{:S(2)}) collective-permute-start(s32[2]{0:T(128)} %refs_0_), channel_id=1, source_target_pairs={{0,8},{4,12},{8,0},{12,4},{1,9},{5,13},{9,1},{13,5},{2,10},{6,14},... | collective-permute-start | bytes 32 | tf_op jit(solution)/shard_map/ppermute | solution.py:20
  3.1 2.2 %constant_dynamic-slice_fusion = (bf16[256,2,256]{2,1,0:T(2,128)(2,1)S(1)}, bf16[256,2,256]{2,1,0:T(2,128)(2,1)S(1)}, bf16[256,2,256]{2,1,0:T(2,128)(2,1)S(1)}, ...) fusion(bf16[8192,2,256]{2,1,0:T(2,128)(2,1)} %param.8, s32[]{:T(128)S(6)} %select_n.63, s32[]{:T(128)S(6)} %select_n.57, ...), kind=kLoop, calls=%fused_computation.16 | loop fusion | bytes 2621460 | tf_op jit(solution)/shard_map/dynamic_slice | solution.py:302
  5.3 6.1 %collective-permute-start = (bf16[256,512]{1,0:T(8,128)(2,1)S(1)}, bf16[256,512]{1,0:T(8,128)(2,1)S(1)}, u32[]{:S(2)}, u32[]{:S(2)}) collective-permute-start(bf16[256,512]{1,0:T(8,128)(2,1)S(1)} %bitcast.40), channel_id=1, source_target_pairs={{3,0},{0,3},{7,4},{4,7},{11,8},{8,11},{15,12},{12,15},{19,16},{16,... | collective-permute-start | bytes 786440 | tf_op jit(solution)/shard_map/ppermute | solution.py:327
  11.4 1.3 collective-permute-start.1
  12.8 3.2 %constant_dynamic-slice_fusion.2 = bf16[2048,2,256]{2,1,0:T(2,128)(2,1)S(1)} fusion(bf16[8192,2,256]{2,1,0:T(2,128)(2,1)} %param.8, s32[]{:T(128)S(6)} %select_n.58), kind=kLoop, calls=%fused_computation.18 | loop fusion | bytes 4194308 | tf_op jit(solution)/shard_map/dynamic_slice | solution.py:335
  16.0 0.5 copy.15
  16.6 1.6 %copy-done = bf16[1024,2048]{1,0:T(8,128)(2,1)S(1)} copy-done((bf16[1024,2048]{1,0:T(8,128)(2,1)S(1)}, bf16[1024,2048]{1,0:T(8,128)(2,1)}, u32[]{:S(2)}) %copy-start) | copy-done | bytes 4194328
  18.2 3.7 %convolution_bitcast_fusion = f32[1024,512]{1,0:T(8,128)} fusion(bf16[1024,2048]{1,0:T(8,128)(2,1)S(1)} %copy-done, bf16[2048,512]{1,0:T(8,128)(2,1)S(1)} %bitcast.32), kind=kOutput, calls=%fused_computation.4 | convolution fusion | flops 2147483648 | bytes 8388608 | tf_op jit(solution)/shard_map/dot_general | solution.py:336
  22.7 2.5 %collective-permute-start.7 = (bf16[256,512]{1,0:T(8,128)(2,1)S(1)}, bf16[256,512]{1,0:T(8,128)(2,1)S(1)}, u32[]{:S(2)}, u32[]{:S(2)}) collective-permute-start(bf16[256,512]{1,0:T(8,128)(2,1)S(1)} %add.80.refs_0_), channel_id=1, source_target_pairs={{0,24},{4,28},{8,16},{12,20},{16,8},{20,12},{24,0},{28,4},{1,25},{... | collective-permute-start | bytes 786440 | tf_op jit(solution)/shard_map/ppermute | solution.py:20
  25.3 0.5 collective-permute-start.6
  25.8 0.5 collective-permute-start.5
  26.3 1.3 collective-permute-start.8
  27.6 1.5 pack_named.1
  29.2 10.3 %collective-permute-done.8.refs_0_ = bf16[256,512]{1,0:T(8,128)(2,1)S(1)} collective-permute-done((bf16[256,512]{1,0:T(8,128)(2,1)S(1)}, bf16[256,512]{1,0:T(8,128)(2,1)S(1)}, u32[]{:S(2)}, u32[]{:S(2)}) %collective-permute-start.8) | collective-permute-done | bytes 262176 | tf_op jit(solution)/shard_map/ppermute | solution.py:306
  39.6 0.5 collective-permute-start.10
  40.2 0.4 collective-permute-start.12
  40.7 0.4 collective-permute-done.9.refs_4_
  41.1 0.4 collective-permute-done.10.refs_5_
  41.5 0.4 collective-permute-done.11.refs_6_
  41.9 0.4 collective-permute-done.12.refs_7_
  42.2 4.1 %walk_step.3.refs_10_ = bf16[1024,512]{1,0:T(8,128)(2,1)S(1)} custom-call(s32[2]{0:T(128)S(1)} %pad_add_fusion.place_ref, bf16[1024,2048]{1,0:T(8,128)(2,1)S(1)} %copy-done, bf16[256,512]{1,0:T(8,128)(2,1)S(1)} %add.80.refs_0_, bf16[256,512]{1,0:T(8,128)(2,1)S(1)} %collective-permute-done.5.refs_1_, bf16[256,512]{1,0:T(8,128)(2,1)S(1)} %collective-permute-done.6.refs_2_, ...), custom_call_target="tpu_custom_call" | custom-call | flops 20000000000 | bytes 1 | tf_op jit(solution)/shard_map/walk_step/pallas_call | solution.py:151
  46.3 1.9 %collective-permute-start.18 = (bf16[1024,512]{1,0:T(8,128)(2,1)S(1)}, bf16[1024,512]{1,0:T(8,128)(2,1)S(1)}, u32[]{:S(2)}, u32[]{:S(2)}) collective-permute-start(bf16[1024,512]{1,0:T(8,128)(2,1)S(1)} %walk_step.3.refs_10_), channel_id=1, source_target_pairs={{0,1},{3,2},{4,5},{7,6},{8,9},{11,10},{12,13},{15,14},{16,17},{19,... | collective-permute-start | bytes 3145736 | tf_op jit(solution)/shard_map/ppermute | solution.py:393
  48.3 1.9 %collective-permute-start.15 = (bf16[256,512]{1,0:T(8,128)(2,1)S(1)}, bf16[256,512]{1,0:T(8,128)(2,1)S(1)}, u32[]{:S(2)}, u32[]{:S(2)}) collective-permute-start(bf16[256,512]{1,0:T(8,128)(2,1)S(1)} %collective-permute-done.8.refs_0_), channel_id=1, source_target_pairs={{0,24},{4,28},{8,16},{12,20},{16,8},{20,12},{24,0},{28,4},{1,25},{... | collective-permute-start | bytes 786440 | tf_op jit(solution)/shard_map/ppermute | solution.py:20
  50.2 0.8 collective-permute-start.14
  51.0 0.8 collective-permute-start.13
  51.9 1.3 collective-permute-start.29
  53.2 5.3 %collective-permute-done.15.refs_3_ = bf16[256,512]{1,0:T(8,128)(2,1)S(1)} collective-permute-done((bf16[256,512]{1,0:T(8,128)(2,1)S(1)}, bf16[256,512]{1,0:T(8,128)(2,1)S(1)}, u32[]{:S(2)}, u32[]{:S(2)}) %collective-permute-start.15) | collective-permute-done | bytes 262176 | tf_op jit(solution)/shard_map/ppermute | solution.py:20
  58.5 0.7 collective-permute-start.30
  59.2 3.8 %collective-permute-done.14.refs_2_ = bf16[256,512]{1,0:T(8,128)(2,1)S(1)} collective-permute-done((bf16[256,512]{1,0:T(8,128)(2,1)S(1)}, bf16[256,512]{1,0:T(8,128)(2,1)S(1)}, u32[]{:S(2)}, u32[]{:S(2)}) %collective-permute-start.14) | collective-permute-done | bytes 262176 | tf_op jit(solution)/shard_map/ppermute | solution.py:20
  63.0 1.3 collective-permute-start.16
  65.1 0.7 collective-permute-done.20.refs_5_
  66.2 0.4 collective-permute-done.22.refs_7_
  66.5 1.6 %collective-permute-start.33 = (bf16[256,512]{1,0:T(8,128)(2,1)S(1)}, bf16[256,512]{1,0:T(8,128)(2,1)}, u32[]{:S(2)}, u32[]{:S(2)}) collective-permute-start(bf16[256,512]{1,0:T(8,128)(2,1)S(1)} %add.94.refs_0_), channel_id=1, source_target_pairs={{0,24},{4,28},{8,16},{12,20},{16,8},{20,12},{24,0},{28,4},{1,25},{... | collective-permute-start | bytes 786440 | tf_op jit(solution)/shard_map/ppermute | solution.py:20
  68.1 2.8 %collective-permute-done.18.refs_8_ = bf16[1024,512]{1,0:T(8,128)(2,1)S(1)} collective-permute-done((bf16[1024,512]{1,0:T(8,128)(2,1)S(1)}, bf16[1024,512]{1,0:T(8,128)(2,1)S(1)}, u32[]{:S(2)}, u32[]{:S(2)}) %collective-permute-start.18) | collective-permute-done | bytes 1048608 | tf_op jit(solution)/shard_map/ppermute | solution.py:393
  70.9 4.3 %walk_step.4 = bf16[1024,512]{1,0:T(8,128)(2,1)S(1)} custom-call(s32[2]{0:T(128)S(1)} %pad_add_fusion.place_ref, bf16[1024,2048]{1,0:T(8,128)(2,1)S(1)} %copy-done, bf16[256,512]{1,0:T(8,128)(2,1)S(1)} %collective-permute-done.8.refs_0_, bf16[256,512]{1,0:T(8,128)(2,1)S(1)} %collective-permute-done.13.refs_1_, ...), custom_call_target="tpu_custom_call" | custom-call | flops 1 | bytes 1 | tf_op jit(solution)/shard_map/walk_step/pallas_call | solution.py:151
  75.3 1.7 %collective-permute-start.28 = (bf16[1024,512]{1,0:T(8,128)(2,1)S(1)}, bf16[1024,512]{1,0:T(8,128)(2,1)}, u32[]{:S(2)}, u32[]{:S(2)}) collective-permute-start(bf16[1024,512]{1,0:T(8,128)(2,1)S(1)} %walk_step.4), channel_id=1, source_target_pairs={{3,2},{2,1},{7,6},{6,5},{11,10},{10,9},{15,14},{14,13},{19,18},{18... | collective-permute-start | bytes 3145736 | tf_op jit(solution)/shard_map/ppermute | solution.py:395
  76.9 5.0 %collective-permute-start.27 = (bf16[1024,512]{1,0:T(8,128)(2,1)S(1)}, bf16[1024,512]{1,0:T(8,128)(2,1)}, u32[]{:S(2)}, u32[]{:S(2)}) collective-permute-start(bf16[1024,512]{1,0:T(8,128)(2,1)S(1)} %walk_step.4), channel_id=1, source_target_pairs={{0,1},{1,2},{4,5},{5,6},{8,9},{9,10},{12,13},{13,14},{16,17},{17,1... | collective-permute-start | bytes 3145736 | tf_op jit(solution)/shard_map/ppermute | solution.py:395
  82.1 1.5 collective-permute-start.32
  83.9 1.0 collective-permute-start.31
  84.9 6.0 %collective-permute-done.32.refs_2_ = bf16[256,512]{1,0:T(8,128)(2,1)} collective-permute-done((bf16[256,512]{1,0:T(8,128)(2,1)S(1)}, bf16[256,512]{1,0:T(8,128)(2,1)}, u32[]{:S(2)}, u32[]{:S(2)}) %collective-permute-start.32) | collective-permute-done | bytes 262176 | tf_op jit(solution)/shard_map/ppermute | solution.py:20
  90.9 1.0 collective-permute-done.31.refs_1_
  92.0 0.5 collective-permute-start.35
  92.5 1.0 collective-permute-done.34.refs_4_
  94.2 0.7 copy-done.14
  95.1 0.7 pad_add_fusion.1.place_ref
  95.8 1.1 collective-permute-done.37.refs_7_
  96.9 6.0 %collective-permute-done.27.refs_8_ = bf16[1024,512]{1,0:T(8,128)(2,1)} collective-permute-done((bf16[1024,512]{1,0:T(8,128)(2,1)S(1)}, bf16[1024,512]{1,0:T(8,128)(2,1)}, u32[]{:S(2)}, u32[]{:S(2)}) %collective-permute-start.27) | collective-permute-done | bytes 1048608 | tf_op jit(solution)/shard_map/ppermute | solution.py:395
  102.8 6.4 %walk_step.5 = (bf16[1024,512]{1,0:T(8,128)(2,1)}, bf16[1024,512]{1,0:T(8,128)(2,1)}) custom-call(s32[3]{0:T(128)} %pad_add_fusion.1.place_ref, bf16[1024,2048]{1,0:T(8,128)(2,1)} %tok_ref.7, bf16[256,512]{1,0:T(8,128)(2,1)} %copy-done.8, bf16[256,512]{1,0:T(8,128)(2,1)} %copy-done.12, bf16[256,512]{1,0:T(8,128)(2,1)} %collective-permute-done.32.refs_2_, ...), custom_call_target="tpu_custom_call" | custom-call | flops 1 | bytes 1 | tf_op jit(solution)/shard_map/walk_step/pallas_call | solution.py:151
  109.3 5.6 %collective-permute-start.38 = (bf16[1024,512]{1,0:T(8,128)(2,1)}, bf16[1024,512]{1,0:T(8,128)(2,1)}, u32[]{:S(2)}, u32[]{:S(2)}) collective-permute-start(bf16[1024,512]{1,0:T(8,128)(2,1)} %get-tuple-element.123), channel_id=1, source_target_pairs={{0,1},{1,2},{2,3},{4,5},{5,6},{6,7},{8,9},{9,10},{10,11},{12,13},{... | collective-permute-start | bytes 3145736 | tf_op jit(solution)/shard_map/ppermute | solution.py:395
  114.8 1.3 collective-permute-start.39
  116.1 2.2 %copy-done.1 = bf16[1024,2048]{1,0:T(8,128)(2,1)S(1)} copy-done((bf16[1024,2048]{1,0:T(8,128)(2,1)S(1)}, bf16[1024,2048]{1,0:T(8,128)(2,1)}, u32[]{:S(2)}) %copy-start.1) | copy-done | bytes 4194328
  118.3 2.1 %coefficients.1 = f32[2,64,512]{2,1,0:T(8,128)S(1)} custom-call(s32[2]{0:T(128)S(1)} %get-tuple-element.73.pick_ref, bf16[1024,2048]{1,0:T(8,128)(2,1)S(1)} %copy-done.1, bf16[4,64,2048]{2,1,0:T(8,128)(2,1)S(1)} %constant_dynamic-update-slice_fusion.mine_ref, bf16[4,64,2048]{2,1,0:T(8,128)(2,1)S(1)} %collective-permute-done.17.other_ref), custom_call_target="tpu_custom_call" | custom-call | flops 1 | bytes 1 | tf_op jit(solution)/shard_map/coefficients/pallas_call | solution.py:263
  120.4 1.3 collective-permute-start.25
  121.7 2.7 %collective-permute-start.23 = (bf16[2,64,512]{2,1,0:T(8,128)(2,1)S(1)}, bf16[2,64,512]{2,1,0:T(8,128)(2,1)S(1)}, u32[]{:S(2)}, u32[]{:S(2)}) collective-permute-start(bf16[2,64,512]{2,1,0:T(8,128)(2,1)S(1)} %convert_element_type.38), channel_id=1, source_target_pairs={{0,1},{1,0},{2,3},{3,2},{4,5},{5,4},{6,7},{7,6},{8,9},{9,8},{10,11... | collective-permute-start | bytes 393224 | tf_op jit(solution)/shard_map/ppermute | solution.py:20
  124.6 0.9 collective-permute-done.25
  125.7 17.2 %collective-permute-done.23 = bf16[2,64,512]{2,1,0:T(8,128)(2,1)S(1)} collective-permute-done((bf16[2,64,512]{2,1,0:T(8,128)(2,1)S(1)}, bf16[2,64,512]{2,1,0:T(8,128)(2,1)S(1)}, u32[]{:S(2)}, u32[]{:S(2)}) %collective-permute-start.23) | collective-permute-done | bytes 131104 | tf_op jit(solution)/shard_map/ppermute | solution.py:20
  143.0 1.3 collective-permute-start.24
  144.3 0.7 copy-done.11
  145.0 3.1 %choose_factors.1 = bf16[2,65,2,256]{3,2,1,0:T(2,128)(2,1)} custom-call(s32[2]{0:T(128)} %copy-done.3, bf16[4,65,2,256]{3,2,1,0:T(2,128)(2,1)} %copy-done.9, bf16[4,65,2,256]{3,2,1,0:T(2,128)(2,1)} %copy-done.11), custom_call_target="tpu_custom_call" | custom-call | flops 1 | bytes 1 | tf_op jit(solution)/shard_map/choose_factors/pallas_call | solution.py:240
  148.1 1.0 slice.9
  149.2 0.7 slice_convert_fusion
  149.9 0.6 fusion.5
  150.5 2.3 %fusion.2 = bf16[1024,512]{1,0:T(8,128)(2,1)S(1)} fusion(f32[1024,512]{1,0:T(8,128)S(1)} %copy-done.7, f32[2,512,512]{2,1,0:T(8,128)S(1)} %fusion.5, bf16[1024,512]{1,0:T(8,128)(2,1)} %collective-permute-done.39, bf16[1024,512]{1,0:T(8,128)(2,1)} %collective-permute-done.38), kind=kLoop, calls=%fused_computation.3 | loop fusion | flops 3145728 | bytes 7340032 | tf_op jit(solution)/shard_map/convert_element_type | solution.py:421
  152.8 1.1 reshape.46
  (81 shorter events, 4.3 us)
Async XLA Ops:
  0.0 22.7 %collective-permute-start.3 = (s32[2]{0:T(128)}, s32[2]{0:T(128)S(1)}, u32[]{:S(2)}, u32[]{:S(2)}) collective-permute-start(s32[2]{0:T(128)} %refs_0_), channel_id=1, source_target_pairs={{0,8},{4,12},{8,0},{12,4},{1,9},{5,13},{9,1},{13,5},{2,10},{6,14},... | collective-permute-start | bytes 32 | tf_op jit(solution)/shard_map/ppermute | solution.py:20
  2.9 19.8 %collective-permute-start.2 = (s32[2]{0:T(128)}, s32[2]{0:T(128)S(1)}, u32[]{:S(2)}, u32[]{:S(2)}) collective-permute-start(s32[2]{0:T(128)} %refs_0_), channel_id=1, source_target_pairs={{0,4},{4,0},{8,12},{12,8},{1,5},{5,1},{9,13},{13,9},{2,6},{6,2},{1... | collective-permute-start | bytes 32 | tf_op jit(solution)/shard_map/ppermute | solution.py:20
  2.9 19.8 %collective-permute-start.4 = (s32[2]{0:T(128)}, s32[2]{0:T(128)S(1)}, u32[]{:S(2)}, u32[]{:S(2)}) collective-permute-start(s32[2]{0:T(128)} %refs_0_), channel_id=1, source_target_pairs={{0,12},{4,8},{8,4},{12,0},{1,13},{5,9},{9,5},{13,1},{2,14},{6,10},... | collective-permute-start | bytes 32 | tf_op jit(solution)/shard_map/ppermute | solution.py:20
  5.3 17.0 %collective-permute-start = (bf16[256,512]{1,0:T(8,128)(2,1)S(1)}, bf16[256,512]{1,0:T(8,128)(2,1)S(1)}, u32[]{:S(2)}, u32[]{:S(2)}) collective-permute-start(bf16[256,512]{1,0:T(8,128)(2,1)S(1)} %bitcast.40), channel_id=1, source_target_pairs={{3,0},{0,3},{7,4},{4,7},{11,8},{8,11},{15,12},{12,15},{19,16},{16,... | collective-permute-start | bytes 786440 | tf_op jit(solution)/shard_map/ppermute | solution.py:327
  11.4 11.2 %collective-permute-start.1 = (bf16[256,512]{1,0:T(8,128)(2,1)S(1)}, bf16[256,512]{1,0:T(8,128)(2,1)S(1)}, u32[]{:S(2)}, u32[]{:S(2)}) collective-permute-start(bf16[256,512]{1,0:T(8,128)(2,1)S(1)} %bitcast.41), channel_id=1, source_target_pairs={{0,1},{3,2},{4,5},{7,6},{8,9},{11,10},{12,13},{15,14},{16,17},{19,... | collective-permute-start | bytes 786440 | tf_op jit(solution)/shard_map/ppermute | solution.py:327
  16.0 2.2 %copy-start = (bf16[1024,2048]{1,0:T(8,128)(2,1)S(1)}, bf16[1024,2048]{1,0:T(8,128)(2,1)}, u32[]{:S(2)}) copy-start(bf16[1024,2048]{1,0:T(8,128)(2,1)} %tok_ref.7) | copy-start | bytes 12582916
  18.2 3.7 %copy-start.15 = (bf16[6,64]{1,0:T(8,128)(2,1)S(1)}, bf16[6,64]{1,0:T(8,128)(2,1)}, u32[]{:S(2)}) copy-start(bf16[6,64]{1,0:T(8,128)(2,1)} %param.11) | copy-start | bytes 2308
  18.2 3.7 %copy-start.10 = (bf16[6,64,2,256]{3,2,1,0:T(2,128)(2,1)S(1)}, bf16[6,64,2,256]{3,2,1,0:T(2,128)(2,1)}, u32[]{:S(2)}) copy-start(bf16[6,64,2,256]{3,2,1,0:T(2,128)(2,1)} %param.10) | copy-start | bytes 1179652
  21.9 5.7 %copy-start.4 = (bf16[6,64,2048]{2,1,0:T(8,128)(2,1)S(1)}, bf16[6,64,2048]{2,1,0:T(8,128)(2,1)}, u32[]{:S(2)}) copy-start(bf16[6,64,2048]{2,1,0:T(8,128)(2,1)} %refs_4_.1) | copy-start | bytes 4718596
  21.9 5.7 %copy-start.5 = (s32[24]{0:T(128)S(1)}, s32[24]{0:T(128)}, u32[]{:S(2)}) copy-start(s32[24]{0:T(128)} %map_ref.1) | copy-start | bytes 292
  21.9 5.7 %copy-start.6 = (s32[2]{0:T(128)S(1)}, s32[2]{0:T(128)}, u32[]{:S(2)}) copy-start(s32[2]{0:T(128)} %refs_0_) | copy-start | bytes 28
  22.7 16.8 %collective-permute-start.7 = (bf16[256,512]{1,0:T(8,128)(2,1)S(1)}, bf16[256,512]{1,0:T(8,128)(2,1)S(1)}, u32[]{:S(2)}, u32[]{:S(2)}) collective-permute-start(bf16[256,512]{1,0:T(8,128)(2,1)S(1)} %add.80.refs_0_), channel_id=1, source_target_pairs={{0,24},{4,28},{8,16},{12,20},{16,8},{20,12},{24,0},{28,4},{1,25},{... | collective-permute-start | bytes 786440 | tf_op jit(solution)/shard_map/ppermute | solution.py:20
  25.3 14.3 %collective-permute-start.6 = (bf16[256,512]{1,0:T(8,128)(2,1)S(1)}, bf16[256,512]{1,0:T(8,128)(2,1)S(1)}, u32[]{:S(2)}, u32[]{:S(2)}) collective-permute-start(bf16[256,512]{1,0:T(8,128)(2,1)S(1)} %add.80.refs_0_), channel_id=1, source_target_pairs={{0,16},{4,20},{8,24},{12,28},{16,0},{20,4},{24,8},{28,12},{1,17},{... | collective-permute-start | bytes 786440 | tf_op jit(solution)/shard_map/ppermute | solution.py:20
  25.8 13.7 %collective-permute-start.5 = (bf16[256,512]{1,0:T(8,128)(2,1)S(1)}, bf16[256,512]{1,0:T(8,128)(2,1)S(1)}, u32[]{:S(2)}, u32[]{:S(2)}) collective-permute-start(bf16[256,512]{1,0:T(8,128)(2,1)S(1)} %add.80.refs_0_), channel_id=1, source_target_pairs={{0,8},{4,12},{8,0},{12,4},{16,24},{20,28},{24,16},{28,20},{1,9},{5... | collective-permute-start | bytes 786440 | tf_op jit(solution)/shard_map/ppermute | solution.py:20
  26.3 13.2 %collective-permute-start.8 = (bf16[256,512]{1,0:T(8,128)(2,1)S(1)}, bf16[256,512]{1,0:T(8,128)(2,1)S(1)}, u32[]{:S(2)}, u32[]{:S(2)}) collective-permute-start(bf16[256,512]{1,0:T(8,128)(2,1)S(1)} %bitcast.38), channel_id=1, source_target_pairs={{2,0},{3,1},{0,2},{1,3},{6,4},{7,5},{4,6},{5,7},{10,8},{11,9},{8,1... | collective-permute-start | bytes 786440 | tf_op jit(solution)/shard_map/ppermute | solution.py:306
  29.2 87.0 %copy-start.3 = (s32[2]{0:T(128)}, s32[2]{0:T(128)S(1)}, u32[]{:S(2)}) copy-start(s32[2]{0:T(128)S(1)} %get-tuple-element.73.pick_ref) | copy-start | bytes 28
  39.5 1.6 %collective-permute-start.9 = (bf16[256,512]{1,0:T(8,128)(2,1)S(1)}, bf16[256,512]{1,0:T(8,128)(2,1)S(1)}, u32[]{:S(2)}, u32[]{:S(2)}) collective-permute-start(bf16[256,512]{1,0:T(8,128)(2,1)S(1)} %add.80.refs_0_), channel_id=1, source_target_pairs={{0,4},{4,0},{8,12},{12,8},{1,5},{5,1},{9,13},{13,9},{2,6},{6,2},{1... | collective-permute-start | bytes 786440 | tf_op jit(solution)/shard_map/ppermute | solution.py:20
  39.6 1.9 %collective-permute-start.10 = (bf16[256,512]{1,0:T(8,128)(2,1)S(1)}, bf16[256,512]{1,0:T(8,128)(2,1)S(1)}, u32[]{:S(2)}, u32[]{:S(2)}) collective-permute-start(bf16[256,512]{1,0:T(8,128)(2,1)S(1)} %collective-permute-done.5.refs_1_), channel_id=1, source_target_pairs={{0,4},{4,0},{8,12},{12,8},{1,5},{5,1},{9,13},{13,9},{2,6},{6,2},{1... | collective-permute-start | bytes 786440 | tf_op jit(solution)/shard_map/ppermute | solution.py:20
  40.1 1.8 %collective-permute-start.11 = (bf16[256,512]{1,0:T(8,128)(2,1)S(1)}, bf16[256,512]{1,0:T(8,128)(2,1)S(1)}, u32[]{:S(2)}, u32[]{:S(2)}) collective-permute-start(bf16[256,512]{1,0:T(8,128)(2,1)S(1)} %collective-permute-done.6.refs_2_), channel_id=1, source_target_pairs={{0,4},{4,0},{8,12},{12,8},{1,5},{5,1},{9,13},{13,9},{2,6},{6,2},{1... | collective-permute-start | bytes 786440 | tf_op jit(solution)/shard_map/ppermute | solution.py:20
  40.2 2.1 %collective-permute-start.12 = (bf16[256,512]{1,0:T(8,128)(2,1)S(1)}, bf16[256,512]{1,0:T(8,128)(2,1)S(1)}, u32[]{:S(2)}, u32[]{:S(2)}) collective-permute-start(bf16[256,512]{1,0:T(8,128)(2,1)S(1)} %collective-permute-done.7.refs_3_), channel_id=1, source_target_pairs={{0,4},{4,0},{8,12},{12,8},{1,5},{5,1},{9,13},{13,9},{2,6},{6,2},{1... | collective-permute-start | bytes 786440 | tf_op jit(solution)/shard_map/ppermute | solution.py:20
  46.3 28.9 %copy-start.2 = (bf16[1024,512]{1,0:T(8,128)(2,1)}, bf16[1024,512]{1,0:T(8,128)(2,1)S(1)}, u32[]{:S(2)}) copy-start(bf16[1024,512]{1,0:T(8,128)(2,1)S(1)} %walk_step.3.refs_10_) | copy-start | bytes 3145732
  46.3 24.6 %collective-permute-start.18 = (bf16[1024,512]{1,0:T(8,128)(2,1)S(1)}, bf16[1024,512]{1,0:T(8,128)(2,1)S(1)}, u32[]{:S(2)}, u32[]{:S(2)}) collective-permute-start(bf16[1024,512]{1,0:T(8,128)(2,1)S(1)} %walk_step.3.refs_10_), channel_id=1, source_target_pairs={{0,1},{3,2},{4,5},{7,6},{8,9},{11,10},{12,13},{15,14},{16,17},{19,... | collective-permute-start | bytes 3145736 | tf_op jit(solution)/shard_map/ppermute | solution.py:393
  48.3 10.2 %collective-permute-start.15 = (bf16[256,512]{1,0:T(8,128)(2,1)S(1)}, bf16[256,512]{1,0:T(8,128)(2,1)S(1)}, u32[]{:S(2)}, u32[]{:S(2)}) collective-permute-start(bf16[256,512]{1,0:T(8,128)(2,1)S(1)} %collective-permute-done.8.refs_0_), channel_id=1, source_target_pairs={{0,24},{4,28},{8,16},{12,20},{16,8},{20,12},{24,0},{28,4},{1,25},{... | collective-permute-start | bytes 786440 | tf_op jit(solution)/shard_map/ppermute | solution.py:20
  50.2 12.7 %collective-permute-start.14 = (bf16[256,512]{1,0:T(8,128)(2,1)S(1)}, bf16[256,512]{1,0:T(8,128)(2,1)S(1)}, u32[]{:S(2)}, u32[]{:S(2)}) collective-permute-start(bf16[256,512]{1,0:T(8,128)(2,1)S(1)} %collective-permute-done.8.refs_0_), channel_id=1, source_target_pairs={{0,16},{4,20},{8,24},{12,28},{16,0},{20,4},{24,8},{28,12},{1,17},{... | collective-permute-start | bytes 786440 | tf_op jit(solution)/shard_map/ppermute | solution.py:20
  51.0 11.9 %collective-permute-start.13 = (bf16[256,512]{1,0:T(8,128)(2,1)S(1)}, bf16[256,512]{1,0:T(8,128)(2,1)S(1)}, u32[]{:S(2)}, u32[]{:S(2)}) collective-permute-start(bf16[256,512]{1,0:T(8,128)(2,1)S(1)} %collective-permute-done.8.refs_0_), channel_id=1, source_target_pairs={{0,8},{4,12},{8,0},{12,4},{16,24},{20,28},{24,16},{28,20},{1,9},{5... | collective-permute-start | bytes 786440 | tf_op jit(solution)/shard_map/ppermute | solution.py:20
  51.9 12.3 %collective-permute-start.29 = (bf16[256,512]{1,0:T(8,128)(2,1)S(1)}, bf16[256,512]{1,0:T(8,128)(2,1)S(1)}, u32[]{:S(2)}, u32[]{:S(2)}) collective-permute-start(bf16[256,512]{1,0:T(8,128)(2,1)S(1)} %bitcast.42), channel_id=1, source_target_pairs={{1,0},{2,3},{5,4},{6,7},{9,8},{10,11},{13,12},{14,15},{17,16},{18,... | collective-permute-start | bytes 786440 | tf_op jit(solution)/shard_map/ppermute | solution.py:306
  58.5 6.0 %collective-permute-start.30 = (bf16[256,512]{1,0:T(8,128)(2,1)S(1)}, bf16[256,512]{1,0:T(8,128)(2,1)S(1)}, u32[]{:S(2)}, u32[]{:S(2)}) collective-permute-start(bf16[256,512]{1,0:T(8,128)(2,1)S(1)} %bitcast.39), channel_id=1, source_target_pairs={{2,1},{1,2},{6,5},{5,6},{10,9},{9,10},{14,13},{13,14},{18,17},{17,... | collective-permute-start | bytes 786440 | tf_op jit(solution)/shard_map/ppermute | solution.py:306
  62.9 1.8 %collective-permute-start.19 = (bf16[256,512]{1,0:T(8,128)(2,1)S(1)}, bf16[256,512]{1,0:T(8,128)(2,1)S(1)}, u32[]{:S(2)}, u32[]{:S(2)}) collective-permute-start(bf16[256,512]{1,0:T(8,128)(2,1)S(1)} %collective-permute-done.8.refs_0_), channel_id=1, source_target_pairs={{0,4},{4,0},{8,12},{12,8},{1,5},{5,1},{9,13},{13,9},{2,6},{6,2},{1... | collective-permute-start | bytes 786440 | tf_op jit(solution)/shard_map/ppermute | solution.py:20
  63.0 19.0 %collective-permute-start.16 = (bf16[2,64,2048]{2,1,0:T(8,128)(2,1)S(1)}, bf16[2,64,2048]{2,1,0:T(8,128)(2,1)S(1)}, u32[]{:S(2)}, u32[]{:S(2)}) collective-permute-start(bf16[2,64,2048]{2,1,0:T(8,128)(2,1)S(1)} %get-tuple-element.89), channel_id=1, source_target_pairs={{0,8},{4,12},{8,0},{12,4},{1,9},{5,13},{9,1},{13,5},{2,10},{6,14},... | collective-permute-start | bytes 1572872 | tf_op jit(solution)/shard_map/ppermute | solution.py:20
  64.2 1.5 collective-permute-start.20
  64.5 1.7 %collective-permute-start.21 = (bf16[256,512]{1,0:T(8,128)(2,1)S(1)}, bf16[256,512]{1,0:T(8,128)(2,1)S(1)}, u32[]{:S(2)}, u32[]{:S(2)}) collective-permute-start(bf16[256,512]{1,0:T(8,128)(2,1)S(1)} %collective-permute-done.14.refs_2_), channel_id=1, source_target_pairs={{0,4},{4,0},{8,12},{12,8},{1,5},{5,1},{9,13},{13,9},{2,6},{6,2},{1... | collective-permute-start | bytes 786440 | tf_op jit(solution)/shard_map/ppermute | solution.py:20
  64.8 1.8 %collective-permute-start.22 = (bf16[256,512]{1,0:T(8,128)(2,1)S(1)}, bf16[256,512]{1,0:T(8,128)(2,1)S(1)}, u32[]{:S(2)}, u32[]{:S(2)}) collective-permute-start(bf16[256,512]{1,0:T(8,128)(2,1)S(1)} %collective-permute-done.15.refs_3_), channel_id=1, source_target_pairs={{0,4},{4,0},{8,12},{12,8},{1,5},{5,1},{9,13},{13,9},{2,6},{6,2},{1... | collective-permute-start | bytes 786440 | tf_op jit(solution)/shard_map/ppermute | solution.py:20
  65.1 26.9 %copy-start.8 = (bf16[256,512]{1,0:T(8,128)(2,1)}, bf16[256,512]{1,0:T(8,128)(2,1)S(1)}, u32[]{:S(2)}) copy-start(bf16[256,512]{1,0:T(8,128)(2,1)S(1)} %add.94.refs_0_) | copy-start | bytes 786436
  66.5 17.3 %collective-permute-start.33 = (bf16[256,512]{1,0:T(8,128)(2,1)S(1)}, bf16[256,512]{1,0:T(8,128)(2,1)}, u32[]{:S(2)}, u32[]{:S(2)}) collective-permute-start(bf16[256,512]{1,0:T(8,128)(2,1)S(1)} %add.94.refs_0_), channel_id=1, source_target_pairs={{0,24},{4,28},{8,16},{12,20},{16,8},{20,12},{24,0},{28,4},{1,25},{... | collective-permute-start | bytes 786440 | tf_op jit(solution)/shard_map/ppermute | solution.py:20
  75.3 21.6 %collective-permute-start.28 = (bf16[1024,512]{1,0:T(8,128)(2,1)S(1)}, bf16[1024,512]{1,0:T(8,128)(2,1)}, u32[]{:S(2)}, u32[]{:S(2)}) collective-permute-start(bf16[1024,512]{1,0:T(8,128)(2,1)S(1)} %walk_step.4), channel_id=1, source_target_pairs={{3,2},{2,1},{7,6},{6,5},{11,10},{10,9},{15,14},{14,13},{19,18},{18... | collective-permute-start | bytes 3145736 | tf_op jit(solution)/shard_map/ppermute | solution.py:395
  76.9 25.9 %collective-permute-start.27 = (bf16[1024,512]{1,0:T(8,128)(2,1)S(1)}, bf16[1024,512]{1,0:T(8,128)(2,1)}, u32[]{:S(2)}, u32[]{:S(2)}) collective-permute-start(bf16[1024,512]{1,0:T(8,128)(2,1)S(1)} %walk_step.4), channel_id=1, source_target_pairs={{0,1},{1,2},{4,5},{5,6},{8,9},{9,10},{12,13},{13,14},{16,17},{17,1... | collective-permute-start | bytes 3145736 | tf_op jit(solution)/shard_map/ppermute | solution.py:395
  82.0 34.1 %collective-permute-start.17 = (bf16[4,64,2048]{2,1,0:T(8,128)(2,1)S(1)}, bf16[4,64,2048]{2,1,0:T(8,128)(2,1)S(1)}, u32[]{:S(2)}, u32[]{:S(2)}) collective-permute-start(bf16[4,64,2048]{2,1,0:T(8,128)(2,1)S(1)} %constant_dynamic-update-slice_fusion.mine_ref), channel_id=1, source_target_pairs={{0,4},{4,0},{8,12},{12,8},{1,5},{5,1},{9,13},{13,9},{2,6},{6,2},{1... | collective-permute-start | bytes 3145736 | tf_op jit(solution)/shard_map/ppermute | solution.py:20
  82.1 8.8 %collective-permute-start.32 = (bf16[256,512]{1,0:T(8,128)(2,1)S(1)}, bf16[256,512]{1,0:T(8,128)(2,1)}, u32[]{:S(2)}, u32[]{:S(2)}) collective-permute-start(bf16[256,512]{1,0:T(8,128)(2,1)S(1)} %add.94.refs_0_), channel_id=1, source_target_pairs={{0,16},{4,20},{8,24},{12,28},{16,0},{20,4},{24,8},{28,12},{1,17},{... | collective-permute-start | bytes 786440 | tf_op jit(solution)/shard_map/ppermute | solution.py:20
  83.9 8.1 %collective-permute-start.31 = (bf16[256,512]{1,0:T(8,128)(2,1)S(1)}, bf16[256,512]{1,0:T(8,128)(2,1)S(1)}, u32[]{:S(2)}, u32[]{:S(2)}) collective-permute-start(bf16[256,512]{1,0:T(8,128)(2,1)S(1)} %add.94.refs_0_), channel_id=1, source_target_pairs={{0,8},{4,12},{8,0},{12,4},{16,24},{20,28},{24,16},{28,20},{1,9},{5... | collective-permute-start | bytes 786440 | tf_op jit(solution)/shard_map/ppermute | solution.py:20
  91.9 1.5 %copy-start.12 = (bf16[256,512]{1,0:T(8,128)(2,1)}, bf16[256,512]{1,0:T(8,128)(2,1)S(1)}, u32[]{:S(2)}) copy-start(bf16[256,512]{1,0:T(8,128)(2,1)S(1)} %collective-permute-done.31.refs_1_) | copy-start | bytes 786436
  91.9 1.5 collective-permute-start.34
  92.0 1.9 %collective-permute-start.35 = (bf16[256,512]{1,0:T(8,128)(2,1)S(1)}, bf16[256,512]{1,0:T(8,128)(2,1)S(1)}, u32[]{:S(2)}, u32[]{:S(2)}) collective-permute-start(bf16[256,512]{1,0:T(8,128)(2,1)S(1)} %collective-permute-done.31.refs_1_), channel_id=1, source_target_pairs={{0,4},{4,0},{8,12},{12,8},{1,5},{5,1},{9,13},{13,9},{2,6},{6,2},{1... | collective-permute-start | bytes 786440 | tf_op jit(solution)/shard_map/ppermute | solution.py:20
  93.5 0.7 copy-start.13
  93.5 2.3 %collective-permute-start.36 = (bf16[256,512]{1,0:T(8,128)(2,1)}, bf16[256,512]{1,0:T(8,128)(2,1)}, u32[]{:S(2)}, u32[]{:S(2)}) collective-permute-start(bf16[256,512]{1,0:T(8,128)(2,1)} %collective-permute-done.32.refs_2_), channel_id=1, source_target_pairs={{0,4},{4,0},{8,12},{12,8},{1,5},{5,1},{9,13},{13,9},{2,6},{6,2},{1... | collective-permute-start | bytes 786440 | tf_op jit(solution)/shard_map/ppermute | solution.py:20
  94.2 0.8 copy-start.14
  95.0 1.9 %collective-permute-start.37 = (bf16[256,512]{1,0:T(8,128)(2,1)}, bf16[256,512]{1,0:T(8,128)(2,1)}, u32[]{:S(2)}, u32[]{:S(2)}) collective-permute-start(bf16[256,512]{1,0:T(8,128)(2,1)} %collective-permute-done.33.refs_3_), channel_id=1, source_target_pairs={{0,4},{4,0},{8,12},{12,8},{1,5},{5,1},{9,13},{13,9},{2,6},{6,2},{1... | collective-permute-start | bytes 786440 | tf_op jit(solution)/shard_map/ppermute | solution.py:20
  109.3 41.2 %collective-permute-start.38 = (bf16[1024,512]{1,0:T(8,128)(2,1)}, bf16[1024,512]{1,0:T(8,128)(2,1)}, u32[]{:S(2)}, u32[]{:S(2)}) collective-permute-start(bf16[1024,512]{1,0:T(8,128)(2,1)} %get-tuple-element.123), channel_id=1, source_target_pairs={{0,1},{1,2},{2,3},{4,5},{5,6},{6,7},{8,9},{9,10},{10,11},{12,13},{... | collective-permute-start | bytes 3145736 | tf_op jit(solution)/shard_map/ppermute | solution.py:395
  114.8 35.7 %collective-permute-start.39 = (bf16[1024,512]{1,0:T(8,128)(2,1)}, bf16[1024,512]{1,0:T(8,128)(2,1)}, u32[]{:S(2)}, u32[]{:S(2)}) collective-permute-start(bf16[1024,512]{1,0:T(8,128)(2,1)} %get-tuple-element.124), channel_id=1, source_target_pairs={{3,2},{2,1},{1,0},{7,6},{6,5},{5,4},{11,10},{10,9},{9,8},{15,14},{... | collective-permute-start | bytes 3145736 | tf_op jit(solution)/shard_map/ppermute | solution.py:395
  116.1 2.2 %copy-start.1 = (bf16[1024,2048]{1,0:T(8,128)(2,1)S(1)}, bf16[1024,2048]{1,0:T(8,128)(2,1)}, u32[]{:S(2)}) copy-start(bf16[1024,2048]{1,0:T(8,128)(2,1)} %tok_ref.7) | copy-start | bytes 12582916
  120.4 5.1 %collective-permute-start.25 = (bf16[2,65,2,256]{3,2,1,0:T(2,128)(2,1)S(1)}, bf16[2,65,2,256]{3,2,1,0:T(2,128)(2,1)S(1)}, u32[]{:S(2)}, u32[]{:S(2)}) collective-permute-start(bf16[2,65,2,256]{3,2,1,0:T(2,128)(2,1)S(1)} %get-tuple-element.106), channel_id=1, source_target_pairs={{0,8},{4,12},{8,0},{12,4},{1,9},{5,13},{9,1},{13,5},{2,10},{6,14},... | collective-permute-start | bytes 399368 | tf_op jit(solution)/shard_map/ppermute | solution.py:20
  121.7 21.2 %collective-permute-start.23 = (bf16[2,64,512]{2,1,0:T(8,128)(2,1)S(1)}, bf16[2,64,512]{2,1,0:T(8,128)(2,1)S(1)}, u32[]{:S(2)}, u32[]{:S(2)}) collective-permute-start(bf16[2,64,512]{2,1,0:T(8,128)(2,1)S(1)} %convert_element_type.38), channel_id=1, source_target_pairs={{0,1},{1,0},{2,3},{3,2},{4,5},{5,4},{6,7},{7,6},{8,9},{9,8},{10,11... | collective-permute-start | bytes 393224 | tf_op jit(solution)/shard_map/ppermute | solution.py:20
  125.6 18.7 %copy-start.9 = (bf16[4,65,2,256]{3,2,1,0:T(2,128)(2,1)}, bf16[4,65,2,256]{3,2,1,0:T(2,128)(2,1)S(1)}, u32[]{:S(2)}) copy-start(bf16[4,65,2,256]{3,2,1,0:T(2,128)(2,1)S(1)} %constant_dynamic-update-slice_fusion.2.mine_ref) | copy-start | bytes 798724
  125.6 18.7 %collective-permute-start.26 = (bf16[4,65,2,256]{3,2,1,0:T(2,128)(2,1)S(1)}, bf16[4,65,2,256]{3,2,1,0:T(2,128)(2,1)S(1)}, u32[]{:S(2)}, u32[]{:S(2)}) collective-permute-start(bf16[4,65,2,256]{3,2,1,0:T(2,128)(2,1)S(1)} %constant_dynamic-update-slice_fusion.2.mine_ref), channel_id=1, source_target_pairs={{0,4},{4,0},{8,12},{12,8},{1,5},{5,1},{9,13},{13,9},{2,6},{6,2},{1... | collective-permute-start | bytes 798728 | tf_op jit(solution)/shard_map/ppermute | solution.py:20
  142.9 7.6 %copy-start.7 = (f32[1024,512]{1,0:T(8,128)S(1)}, f32[1024,512]{1,0:T(8,128)}, u32[]{:S(2)}) copy-start(f32[1024,512]{1,0:T(8,128)} %convolution_bitcast_fusion) | copy-start | bytes 6291460
  143.0 6.9 %collective-permute-start.24 = (bf16[2,64,512]{2,1,0:T(8,128)(2,1)S(1)}, bf16[2,64,512]{2,1,0:T(8,128)(2,1)S(1)}, u32[]{:S(2)}, u32[]{:S(2)}) collective-permute-start(bf16[2,64,512]{2,1,0:T(8,128)(2,1)S(1)} %fusion.4), channel_id=1, source_target_pairs={{0,2},{1,3},{2,0},{3,1},{4,6},{5,7},{6,4},{7,5},{8,10},{9,11},{10,... | collective-permute-start | bytes 393224 | tf_op jit(solution)/shard_map/ppermute | solution.py:20
  144.3 0.7 copy-start.11
